TPU v7x, 512 devices: a whole 4x8x8 slice. The times are simulated.
512 devices in a mesh: tm: 16 (over y, core), space: 32 (over z, x).
Axes of the slice: x: 4, y: 8, z: 8, core: 2. Of those that a mesh axis runs over, the one named last changes fastest.
Arguments:
- iterate: float32 [64, 256, 2048], P('tm', 'space'), may hold values from -8 to 8
- initial: float32 [256, 2048], P('space'), may hold values from -6 to 6
- diffusion: float32 [256, 2048], P('space'), may hold values from 0.05 to 0.5
- courant_x: float32 [256, 2048], P('space'), may hold values from -1 to 1
- courant_y: float32 [256, 2048], P('space'), may hold values from -4 to 4
Outputs:
- new_iterate: float32 [64, 256, 2048], P('tm', 'space')
All inputs are finite; a program needn't handle non-finite values.
Results may differ from a plain program's by a relative error of at most 0.0003.
Values sent between devices are 32-bit elements; how exact they have to be, the bound alone decides.
No kernel may reach another device: no remote copies, remote signals or barrier semaphores. Data moves between devices by JAX's collectives and lax.ppermute only.
A program may use at most 64 MiB of HBM per device.

v0:
```python
import math

import jax
import jax.numpy as jnp
from jax import lax
from jax.sharding import PartitionSpec as P

SWEEPS = 8


alpha_ratio = 0.01


def shifted(value, axis, steps):
    count = lax.axis_size(axis)
    leading, last = (max(0, -steps), min(count, count - steps))
    return lax.ppermute(value, axis, [(source, source + steps) for source in range(leading, last)])


def with_halo(x, sides, width):
    for axis, dim in sides:
        peers, length = (lax.axis_size(axis), x.shape[dim])
        up = [(i, (i + 1) % peers) for i in range(peers - 1)]
        down = [(j, i) for i, j in up]
        last = lax.slice_in_dim(x, length - width, length, axis=dim)
        leading = lax.slice_in_dim(x, 0, width, axis=dim)
        before = lax.ppermute(last, axis, up)
        after = lax.ppermute(leading, axis, down)
        x = jnp.concatenate([before, x, after], axis=dim)
    return x


def exact_dot(left, right):
    return jnp.dot(left, right, precision=lax.Precision.HIGHEST, preferred_element_type=jnp.float32)


def stencil_weights(diffusion, courant_x, courant_y):
    west_weight = diffusion + jnp.maximum(courant_x, 0.0)
    east_weight = diffusion + jnp.maximum(-courant_x, 0.0)
    north_weight = diffusion + jnp.maximum(courant_y, 0.0)
    south_weight = diffusion + jnp.maximum(-courant_y, 0.0)
    return (west_weight, east_weight, north_weight, south_weight)


def neighbours(padded, stencil):
    summed = stencil[0] * padded[..., 1:-1, :-2] + stencil[1] * padded[..., 1:-1, 2:]
    return summed + stencil[2] * padded[..., :-2, 1:-1] + stencil[3] * padded[..., 2:, 1:-1]


def time_tables(length):
    indices = jnp.arange(length, dtype=jnp.int32)
    product_index = indices[:, None] * indices[None, :] % length
    angles = 2.0 * math.pi / length * product_index.astype(jnp.float32)
    scaling = jnp.power(alpha_ratio, indices.astype(jnp.float32) / length)
    fwd_real = jnp.cos(angles) * scaling[None, :]
    fwd_imag = -jnp.sin(angles) * scaling[None, :]
    inv_real = jnp.cos(angles) / (length * scaling[:, None])
    inv_imag = -jnp.sin(angles) / (length * scaling[:, None])
    return (fwd_real, fwd_imag, inv_real, inv_imag)


def frequency_shifts(freq_index, length):
    angles = 2.0 * math.pi / length * freq_index.astype(jnp.float32)
    beta_value = alpha_ratio ** (1.0 / length)
    return (1.0 - beta_value * jnp.cos(angles), beta_value * jnp.sin(angles))


def relaxation(f_real, f_imag, shift_real, shift_imag, stencil, centre, extend):
    diag_real = shift_real + centre
    inverse_norm = 1.0 / (diag_real * diag_real + shift_imag * shift_imag)
    sol_real = (f_real * diag_real + f_imag * shift_imag) * inverse_norm
    sol_imag = (f_imag * diag_real - f_real * shift_imag) * inverse_norm
    for sweep_index in range(SWEEPS - 1):
        padded = extend(jnp.stack([sol_real, sol_imag]))
        q_real = f_real + neighbours(padded[0], stencil)
        q_imag = f_imag + neighbours(padded[1], stencil)
        sol_real = (q_real * diag_real + q_imag * shift_imag) * inverse_norm
        sol_imag = (q_imag * diag_real - q_real * shift_imag) * inverse_norm
    return (sol_real, sol_imag)


def local(iterate, initial, diffusion, courant_x, courant_y):
    steps_dev, row_count, col_count = iterate.shape
    time_devices = lax.axis_size("tm")
    length = steps_dev * time_devices
    stencil = stencil_weights(diffusion, courant_x, courant_y)
    centre = stencil[0] + stencil[1] + stencil[2] + stencil[3]
    last_step = shifted(iterate[steps_dev - 1], "tm", 1)
    first_step = jnp.where(lax.axis_index("tm") == 0, initial, last_step)
    earlier = jnp.concatenate([first_step[None], iterate[: steps_dev - 1]], 0)
    rimmed = with_halo(iterate, (("space", 1),), 1)
    rimmed = jnp.pad(rimmed, ((0, 0), (0, 0), (1, 1)))
    residual = earlier - iterate + neighbours(rimmed, stencil) - centre * iterate
    fwd_real, fwd_imag, inv_real, inv_imag = time_tables(length)
    portion = lax.all_to_all(residual, "tm", split_axis=2, concat_axis=0, tiled=True)
    flattened = portion.reshape(length, -1)
    hat_real = exact_dot(fwd_real, flattened).reshape(portion.shape)
    hat_imag = exact_dot(fwd_imag, flattened).reshape(portion.shape)
    freq_real, freq_imag = (
        lax.all_to_all(hat_real, "tm", split_axis=0, concat_axis=2, tiled=True),
        lax.all_to_all(hat_imag, "tm", split_axis=0, concat_axis=2, tiled=True),
    )
    freq_index = lax.axis_index("tm") * steps_dev + jnp.arange(steps_dev, dtype=jnp.int32)
    lam_real, lam_imag = frequency_shifts(freq_index, length)

    def extend(stacked):
        padded = with_halo(stacked, (("space", 2),), 1)
        return jnp.pad(padded, ((0, 0), (0, 0), (0, 0), (1, 1)))

    sol_real, sol_imag = relaxation(
        freq_real,
        freq_imag,
        lam_real[:, None, None],
        lam_imag[:, None, None],
        stencil,
        centre,
        extend,
    )
    portion = (
        lax.all_to_all(sol_real, "tm", split_axis=2, concat_axis=0, tiled=True),
        lax.all_to_all(sol_imag, "tm", split_axis=2, concat_axis=0, tiled=True),
    )
    dims_out = portion[0].shape
    summed = exact_dot(inv_real, portion[0].reshape(length, -1)) + exact_dot(
        inv_imag, portion[1].reshape(length, -1)
    )
    columns = summed.reshape(dims_out)
    correction = lax.all_to_all(columns, "tm", split_axis=0, concat_axis=2, tiled=True)
    return iterate + correction


def solution(mesh):
    return jax.shard_map(
        local,
        mesh=mesh,
        in_specs=(
            P("tm", "space", None),
            P("space", None),
            P("space", None),
            P("space", None),
            P("space", None),
        ),
        out_specs=P("tm", "space", None),
        check_vma=False,
    )
```

profile of v0, /device:TPU:199, one launch (start us, length us, event | category | flops | bytes accessed | tf_op | source)
XLA Modules:
  0.0 260.4 jit_solution(701580666706623518)
XLA Ops:
  0.0 1.1 fusion.177
  1.2 5.1 %collective-permute-start.1 = (f32[4,1,2048]{2,0,1:T(4,128)S(1)}, f32[4,1,2048]{2,0,1:T(4,128)S(1)}, u32[]{:S(2)}, u32[]{:S(2)}) collective-permute-start(f32[4,1,2048]{2,0,1:T(4,128)S(1)} %copy.279), channel_id=1, source_target_pairs={{0,1},{1,2},{2,3},{3,4},{4,5},{5,6},{6,7},{7,8},{8,9},{9,10},{10,1... | collective-permute-start | bytes 98312 | tf_op jit(solution)/shard_map/ppermute | solution.py:27
  6.4 2.1 collective-permute-start.2
  8.4 0.8 slice_bitcast_fusion.14
  9.3 4.0 %collective-permute-start = (f32[8,2048]{1,0:T(8,128)S(1)}, f32[8,2048]{1,0:T(8,128)S(1)}, u32[]{:S(2)}, u32[]{:S(2)}) collective-permute-start(f32[8,2048]{1,0:T(8,128)S(1)} %slice_bitcast_fusion.14), channel_id=1, source_target_pairs={{0,32},{32,64},{64,96},{96,128},{128,160},{160,192},{192,224},{224... | collective-permute-start | bytes 196616 | tf_op jit(solution)/shard_map/ppermute | solution.py:17
  13.3 0.9 add_add_fusion
  15.2 3.1 %copy.238 = f32[4,8,2048]{1,0,2:T(4,128)} copy(f32[4,8,2048]{2,1,0:T(8,128)S(1)} %fusion.119) | data formatting | bytes 524288 | tf_op jit(solution)/shard_map/sub | solution.py:93
  18.2 7.2 %reshape.125 = f32[16,1,4096]{2,1,0:T(1,128)} reshape(f32[2048,4,8]{2,1,0:T(4,128)} %bitcast.176) | data formatting | bytes 524288
  25.4 9.2 %all-to-all-start = ((f32[16,1,4096]{2,1,0:T(1,128)}), f32[16,1,4096]{2,1,0:T(1,128)S(1)}, u32[]{:S(2)}, u32[]{:S(2)}) async-start(f32[16,1,4096]{2,1,0:T(1,128)} %reshape.125), calls=%async_computation | async-start | bytes 524288 | tf_op jit(solution)/shard_map/all_to_all | solution.py:95
  34.6 11.7 %all-to-all-done = f32[16,1,4096]{2,1,0:T(1,128)S(1)} async-done(((f32[16,1,4096]{2,1,0:T(1,128)}), f32[16,1,4096]{2,1,0:T(1,128)S(1)}, u32[]{:S(2)}, u32[]{:S(2)}) %all-to-all-start) | async-done | bytes 262176 | tf_op jit(solution)/shard_map/all_to_all | solution.py:95
  46.9 1.2 reduce
  48.1 6.3 %reshape.126 = f32[2048,4,8]{2,1,0:T(4,128)} reshape(f32[16,4096]{1,0:T(8,128)S(1)} %reduce) | data formatting | bytes 524288
  54.5 3.4 %copy.239 = f32[4,8,16,128]{3,1,0,2:T(8,128)S(1)} copy(f32[4,8,16,128]{1,0,3,2:T(4,128)} %bitcast.177) | data formatting | bytes 524288 | tf_op jit(solution)/shard_map/all_to_all | solution.py:95
  57.9 0.6 fusion.58
  58.4 0.9 copy.241
  59.3 3.4 %all-to-all-start.1 = ((f32[64,8,128]{2,1,0:T(8,128)}), f32[64,8,128]{2,1,0:T(8,128)S(1)}, u32[]{:S(2)}, u32[]{:S(2)}) async-start(f32[64,8,128]{2,1,0:T(8,128)} %copy.241), calls=%async_computation.1 | async-start | bytes 524288 | tf_op jit(solution)/shard_map/all_to_all | solution.py:100
  63.3 0.9 copy.244
  64.1 9.7 %all-to-all-done.1 = f32[64,8,128]{2,1,0:T(8,128)S(1)} async-done(((f32[64,8,128]{2,1,0:T(8,128)}), f32[64,8,128]{2,1,0:T(8,128)S(1)}, u32[]{:S(2)}, u32[]{:S(2)}) %all-to-all-start.1) | async-done | bytes 262176 | tf_op jit(solution)/shard_map/all_to_all | solution.py:100
  73.9 3.4 %all-to-all-start.2 = ((f32[64,8,128]{2,1,0:T(8,128)}), f32[64,8,128]{2,1,0:T(8,128)S(1)}, u32[]{:S(2)}, u32[]{:S(2)}) async-start(f32[64,8,128]{2,1,0:T(8,128)} %copy.244), calls=%async_computation.2 | async-start | bytes 524288 | tf_op jit(solution)/shard_map/all_to_all | solution.py:101
  77.4 11.6 %all-to-all-done.2 = f32[64,8,128]{2,1,0:T(8,128)S(1)} async-done(((f32[64,8,128]{2,1,0:T(8,128)}), f32[64,8,128]{2,1,0:T(8,128)S(1)}, u32[]{:S(2)}, u32[]{:S(2)}) %all-to-all-start.2) | async-done | bytes 262176 | tf_op jit(solution)/shard_map/all_to_all | solution.py:101
  89.4 6.9 %collective-permute-start.3 = (f32[2,4,1,2048]{3,1,2,0:T(4,128)S(1)}, f32[2,4,1,2048]{3,1,2,0:T(4,128)S(1)}, u32[]{:S(2)}, u32[]{:S(2)}) collective-permute-start(f32[2,4,1,2048]{3,1,2,0:T(4,128)S(1)} %copy.281), channel_id=1, source_target_pairs={{0,1},{1,2},{2,3},{3,4},{4,5},{5,6},{6,7},{7,8},{8,9},{9,10},{10,1... | collective-permute-start | bytes 196616 | tf_op jit(solution)/shard_map/ppermute | solution.py:27
  96.4 1.9 collective-permute-start.4
  98.4 7.0 %collective-permute-done.4 = f32[2,4,1,2048]{3,1,2,0:T(4,128)S(1)} collective-permute-done((f32[2,4,1,2048]{3,1,2,0:T(4,128)S(1)}, f32[2,4,1,2048]{3,1,2,0:T(4,128)S(1)}, u32[]{:S(2)}, u32[]{:S(2)}) %collective-permute-start.4) | collective-permute-done | bytes 65568 | tf_op jit(solution)/shard_map/ppermute | solution.py:28
  105.5 0.7 select_maximum_fusion.18
  107.1 1.9 collective-permute-start.5
  109.1 3.5 %collective-permute-start.6 = (f32[2,4,1,2048]{3,1,2,0:T(4,128)S(1)}, f32[2,4,1,2048]{3,1,2,0:T(4,128)S(1)}, u32[]{:S(2)}, u32[]{:S(2)}) collective-permute-start(f32[2,4,1,2048]{3,1,2,0:T(4,128)S(1)} %copy.251), channel_id=1, source_target_pairs={{1,0},{2,1},{3,2},{4,3},{5,4},{6,5},{7,6},{8,7},{9,8},{10,9},{11,1... | collective-permute-start | bytes 196616 | tf_op jit(solution)/shard_map/ppermute | solution.py:28
  112.7 4.7 %collective-permute-done.6 = f32[2,4,1,2048]{3,1,2,0:T(4,128)S(1)} collective-permute-done((f32[2,4,1,2048]{3,1,2,0:T(4,128)S(1)}, f32[2,4,1,2048]{3,1,2,0:T(4,128)S(1)}, u32[]{:S(2)}, u32[]{:S(2)}) %collective-permute-start.6) | collective-permute-done | bytes 65568 | tf_op jit(solution)/shard_map/ppermute | solution.py:28
  117.5 0.7 select_maximum_fusion.15
  119.2 1.9 collective-permute-start.7
  121.1 3.4 %collective-permute-start.8 = (f32[2,4,1,2048]{3,1,2,0:T(4,128)S(1)}, f32[2,4,1,2048]{3,1,2,0:T(4,128)S(1)}, u32[]{:S(2)}, u32[]{:S(2)}) collective-permute-start(f32[2,4,1,2048]{3,1,2,0:T(4,128)S(1)} %copy.255), channel_id=1, source_target_pairs={{1,0},{2,1},{3,2},{4,3},{5,4},{6,5},{7,6},{8,7},{9,8},{10,9},{11,1... | collective-permute-start | bytes 196616 | tf_op jit(solution)/shard_map/ppermute | solution.py:28
  124.6 4.9 %collective-permute-done.8 = f32[2,4,1,2048]{3,1,2,0:T(4,128)S(1)} collective-permute-done((f32[2,4,1,2048]{3,1,2,0:T(4,128)S(1)}, f32[2,4,1,2048]{3,1,2,0:T(4,128)S(1)}, u32[]{:S(2)}, u32[]{:S(2)}) %collective-permute-start.8) | collective-permute-done | bytes 65568 | tf_op jit(solution)/shard_map/ppermute | solution.py:28
  129.5 0.7 select_maximum_fusion.12
  131.2 1.9 collective-permute-start.9
  133.2 3.4 %collective-permute-start.10 = (f32[2,4,1,2048]{3,1,2,0:T(4,128)S(1)}, f32[2,4,1,2048]{3,1,2,0:T(4,128)S(1)}, u32[]{:S(2)}, u32[]{:S(2)}) collective-permute-start(f32[2,4,1,2048]{3,1,2,0:T(4,128)S(1)} %copy.259), channel_id=1, source_target_pairs={{1,0},{2,1},{3,2},{4,3},{5,4},{6,5},{7,6},{8,7},{9,8},{10,9},{11,1... | collective-permute-start | bytes 196616 | tf_op jit(solution)/shard_map/ppermute | solution.py:28
  136.6 4.9 %collective-permute-done.10 = f32[2,4,1,2048]{3,1,2,0:T(4,128)S(1)} collective-permute-done((f32[2,4,1,2048]{3,1,2,0:T(4,128)S(1)}, f32[2,4,1,2048]{3,1,2,0:T(4,128)S(1)}, u32[]{:S(2)}, u32[]{:S(2)}) %collective-permute-start.10) | collective-permute-done | bytes 65568 | tf_op jit(solution)/shard_map/ppermute | solution.py:28
  141.6 0.7 select_maximum_fusion.9
  143.2 1.9 collective-permute-start.11
  145.2 3.4 %collective-permute-start.12 = (f32[2,4,1,2048]{3,1,2,0:T(4,128)S(1)}, f32[2,4,1,2048]{3,1,2,0:T(4,128)S(1)}, u32[]{:S(2)}, u32[]{:S(2)}) collective-permute-start(f32[2,4,1,2048]{3,1,2,0:T(4,128)S(1)} %copy.263), channel_id=1, source_target_pairs={{1,0},{2,1},{3,2},{4,3},{5,4},{6,5},{7,6},{8,7},{9,8},{10,9},{11,1... | collective-permute-start | bytes 196616 | tf_op jit(solution)/shard_map/ppermute | solution.py:28
  148.6 4.9 %collective-permute-done.12 = f32[2,4,1,2048]{3,1,2,0:T(4,128)S(1)} collective-permute-done((f32[2,4,1,2048]{3,1,2,0:T(4,128)S(1)}, f32[2,4,1,2048]{3,1,2,0:T(4,128)S(1)}, u32[]{:S(2)}, u32[]{:S(2)}) %collective-permute-start.12) | collective-permute-done | bytes 65568 | tf_op jit(solution)/shard_map/ppermute | solution.py:28
  153.6 0.7 select_maximum_fusion.6
  155.2 1.9 collective-permute-start.13
  157.2 3.4 %collective-permute-start.14 = (f32[2,4,1,2048]{3,1,2,0:T(4,128)S(1)}, f32[2,4,1,2048]{3,1,2,0:T(4,128)S(1)}, u32[]{:S(2)}, u32[]{:S(2)}) collective-permute-start(f32[2,4,1,2048]{3,1,2,0:T(4,128)S(1)} %copy.267), channel_id=1, source_target_pairs={{1,0},{2,1},{3,2},{4,3},{5,4},{6,5},{7,6},{8,7},{9,8},{10,9},{11,1... | collective-permute-start | bytes 196616 | tf_op jit(solution)/shard_map/ppermute | solution.py:28
  160.7 4.9 %collective-permute-done.14 = f32[2,4,1,2048]{3,1,2,0:T(4,128)S(1)} collective-permute-done((f32[2,4,1,2048]{3,1,2,0:T(4,128)S(1)}, f32[2,4,1,2048]{3,1,2,0:T(4,128)S(1)}, u32[]{:S(2)}, u32[]{:S(2)}) %collective-permute-start.14) | collective-permute-done | bytes 65568 | tf_op jit(solution)/shard_map/ppermute | solution.py:28
  165.6 0.7 select_maximum_fusion.3
  167.3 1.9 collective-permute-start.15
  169.2 3.6 %collective-permute-start.16 = (f32[2,4,1,2048]{3,1,2,0:T(4,128)S(1)}, f32[2,4,1,2048]{3,1,2,0:T(4,128)S(1)}, u32[]{:S(2)}, u32[]{:S(2)}) collective-permute-start(f32[2,4,1,2048]{3,1,2,0:T(4,128)S(1)} %copy.271), channel_id=1, source_target_pairs={{1,0},{2,1},{3,2},{4,3},{5,4},{6,5},{7,6},{8,7},{9,8},{10,9},{11,1... | collective-permute-start | bytes 196616 | tf_op jit(solution)/shard_map/ppermute | solution.py:28
  172.9 4.7 %collective-permute-done.16 = f32[2,4,1,2048]{3,1,2,0:T(4,128)S(1)} collective-permute-done((f32[2,4,1,2048]{3,1,2,0:T(4,128)S(1)}, f32[2,4,1,2048]{3,1,2,0:T(4,128)S(1)}, u32[]{:S(2)}, u32[]{:S(2)}) %collective-permute-start.16) | collective-permute-done | bytes 65568 | tf_op jit(solution)/shard_map/ppermute | solution.py:28
  177.6 0.7 select_maximum_fusion
  179.2 3.1 %copy.274 = f32[4,8,2048]{1,0,2:T(4,128)} copy(f32[4,8,2048]{2,1,0:T(8,128)S(1)} %fusion.48) | data formatting | bytes 524288 | tf_op jit(solution)/shard_map/mul | solution.py:77
  182.2 7.2 %reshape.127 = f32[16,1,4096]{2,1,0:T(1,128)} reshape(f32[2048,4,8]{2,1,0:T(4,128)} %bitcast.178) | data formatting | bytes 524288
  189.4 10.9 %all-to-all-start.3 = ((f32[16,1,4096]{2,1,0:T(1,128)}), f32[16,1,4096]{2,1,0:T(1,128)S(1)}, u32[]{:S(2)}, u32[]{:S(2)}) async-start(f32[16,1,4096]{2,1,0:T(1,128)} %reshape.127), calls=%async_computation.3 | async-start | bytes 524288 | tf_op jit(solution)/shard_map/all_to_all | solution.py:120
  200.3 3.1 %copy.276 = f32[4,8,2048]{1,0,2:T(4,128)} copy(f32[4,8,2048]{2,1,0:T(8,128)S(1)} %get-tuple-element.5) | data formatting | bytes 524288 | tf_op jit(solution)/shard_map/mul | solution.py:78
  203.4 7.2 %reshape.129 = f32[16,1,4096]{2,1,0:T(1,128)} reshape(f32[2048,4,8]{2,1,0:T(4,128)} %bitcast.179) | data formatting | bytes 524288
  210.5 1.6 all-to-all-done.3
  212.2 5.6 %all-to-all-start.4 = ((f32[16,1,4096]{2,1,0:T(1,128)}), f32[16,1,4096]{2,1,0:T(1,128)S(1)}, u32[]{:S(2)}, u32[]{:S(2)}) async-start(f32[16,1,4096]{2,1,0:T(1,128)} %reshape.129), calls=%async_computation.4 | async-start | bytes 524288 | tf_op jit(solution)/shard_map/all_to_all | solution.py:121
  217.8 1.3 reduce.1
  219.1 6.3 %reshape.128 = f32[2048,4,8]{2,1,0:T(4,128)} reshape(f32[16,4096]{1,0:T(8,128)S(1)} %reduce.1) | data formatting | bytes 524288
  225.4 3.4 %copy.275 = f32[4,8,16,128]{3,1,0,2:T(8,128)S(1)} copy(f32[4,8,16,128]{1,0,3,2:T(4,128)} %bitcast.180) | data formatting | bytes 524288 | tf_op jit(solution)/shard_map/all_to_all | solution.py:120
  228.8 0.7 all-to-all-done.4
  229.5 1.2 reduce.2
  230.8 6.3 %reshape.130 = f32[2048,4,8]{2,1,0:T(4,128)} reshape(f32[16,4096]{1,0:T(8,128)S(1)} %reduce.2) | data formatting | bytes 524288
  237.1 3.4 %copy.277 = f32[4,8,16,128]{3,1,0,2:T(8,128)S(1)} copy(f32[4,8,16,128]{1,0,3,2:T(4,128)} %bitcast.181) | data formatting | bytes 524288 | tf_op jit(solution)/shard_map/all_to_all | solution.py:121
  241.6 18.1 %all_to_all.105 = f32[64,8,128]{2,1,0:T(8,128)S(1)} all-to-all(f32[64,8,128]{2,1,0:T(8,128)S(1)} %bitcast.187), channel_id=1, replica_groups=mesh['tm'=16,'space'=32] {'tm'}, dimensions={0} | all-to-all | bytes 524288 | tf_op jit(solution)/shard_map/all_to_all | solution.py:128
  259.7 0.7 bitcast_add_fusion
  (89 shorter events, 10.8 us)
Async XLA Ops:
  0.0 14.5 %copy-start = (f32[4,8,2048]{2,1,0:T(8,128)S(1)}, f32[4,8,2048]{2,1,0:T(8,128)}, u32[]{:S(2)}) copy-start(f32[4,8,2048]{2,1,0:T(8,128)} %param.5) | copy-start | bytes 786436
  1.1 13.7 %copy-start.1 = (f32[8,2048]{1,0:T(8,128)S(1)}, f32[8,2048]{1,0:T(8,128)}, u32[]{:S(2)}) copy-start(f32[8,2048]{1,0:T(8,128)} %param.6) | copy-start | bytes 196612
  1.2 13.1 %collective-permute-start.1 = (f32[4,1,2048]{2,0,1:T(4,128)S(1)}, f32[4,1,2048]{2,0,1:T(4,128)S(1)}, u32[]{:S(2)}, u32[]{:S(2)}) collective-permute-start(f32[4,1,2048]{2,0,1:T(4,128)S(1)} %copy.279), channel_id=1, source_target_pairs={{0,1},{1,2},{2,3},{3,4},{4,5},{5,6},{6,7},{7,8},{8,9},{9,10},{10,1... | collective-permute-start | bytes 98312 | tf_op jit(solution)/shard_map/ppermute | solution.py:27
  6.3 8.6 %slice-start = ((f32[4,8,2048]{2,1,0:T(8,128)}), f32[3,8,2048]{2,1,0:T(8,128)S(1)}, s32[]{:S(2)}) async-start(f32[4,8,2048]{2,1,0:T(8,128)} %param.5), calls=%async_computation.6 | async-start | bytes 393216 | tf_op jit(solution)/shard_map/slice | solution.py:90
  6.4 8.1 %collective-permute-start.2 = (f32[4,1,2048]{2,0,1:T(4,128)S(1)}, f32[4,1,2048]{2,0,1:T(4,128)S(1)}, u32[]{:S(2)}, u32[]{:S(2)}) collective-permute-start(f32[4,1,2048]{2,0,1:T(4,128)S(1)} %copy.280), channel_id=1, source_target_pairs={{1,0},{2,1},{3,2},{4,3},{5,4},{6,5},{7,6},{8,7},{9,8},{10,9},{11,1... | collective-permute-start | bytes 98312 | tf_op jit(solution)/shard_map/ppermute | solution.py:28
  9.3 5.6 %collective-permute-start = (f32[8,2048]{1,0:T(8,128)S(1)}, f32[8,2048]{1,0:T(8,128)S(1)}, u32[]{:S(2)}, u32[]{:S(2)}) collective-permute-start(f32[8,2048]{1,0:T(8,128)S(1)} %slice_bitcast_fusion.14), channel_id=1, source_target_pairs={{0,32},{32,64},{64,96},{96,128},{128,160},{160,192},{192,224},{224... | collective-permute-start | bytes 196616 | tf_op jit(solution)/shard_map/ppermute | solution.py:17
  25.4 20.9 %all-to-all-start = ((f32[16,1,4096]{2,1,0:T(1,128)}), f32[16,1,4096]{2,1,0:T(1,128)S(1)}, u32[]{:S(2)}, u32[]{:S(2)}) async-start(f32[16,1,4096]{2,1,0:T(1,128)} %reshape.125), calls=%async_computation | async-start | bytes 524288 | tf_op jit(solution)/shard_map/all_to_all | solution.py:95
  59.3 14.6 %all-to-all-start.1 = ((f32[64,8,128]{2,1,0:T(8,128)}), f32[64,8,128]{2,1,0:T(8,128)S(1)}, u32[]{:S(2)}, u32[]{:S(2)}) async-start(f32[64,8,128]{2,1,0:T(8,128)} %copy.241), calls=%async_computation.1 | async-start | bytes 524288 | tf_op jit(solution)/shard_map/all_to_all | solution.py:100
  73.9 15.1 %all-to-all-start.2 = ((f32[64,8,128]{2,1,0:T(8,128)}), f32[64,8,128]{2,1,0:T(8,128)S(1)}, u32[]{:S(2)}, u32[]{:S(2)}) async-start(f32[64,8,128]{2,1,0:T(8,128)} %copy.244), calls=%async_computation.2 | async-start | bytes 524288 | tf_op jit(solution)/shard_map/all_to_all | solution.py:101
  89.4 8.9 %collective-permute-start.3 = (f32[2,4,1,2048]{3,1,2,0:T(4,128)S(1)}, f32[2,4,1,2048]{3,1,2,0:T(4,128)S(1)}, u32[]{:S(2)}, u32[]{:S(2)}) collective-permute-start(f32[2,4,1,2048]{3,1,2,0:T(4,128)S(1)} %copy.281), channel_id=1, source_target_pairs={{0,1},{1,2},{2,3},{3,4},{4,5},{5,6},{6,7},{7,8},{8,9},{9,10},{10,1... | collective-permute-start | bytes 196616 | tf_op jit(solution)/shard_map/ppermute | solution.py:27
  96.4 9.0 %collective-permute-start.4 = (f32[2,4,1,2048]{3,1,2,0:T(4,128)S(1)}, f32[2,4,1,2048]{3,1,2,0:T(4,128)S(1)}, u32[]{:S(2)}, u32[]{:S(2)}) collective-permute-start(f32[2,4,1,2048]{3,1,2,0:T(4,128)S(1)} %copy.282), channel_id=1, source_target_pairs={{1,0},{2,1},{3,2},{4,3},{5,4},{6,5},{7,6},{8,7},{9,8},{10,9},{11,1... | collective-permute-start | bytes 196616 | tf_op jit(solution)/shard_map/ppermute | solution.py:28
  107.1 5.5 %collective-permute-start.5 = (f32[2,4,1,2048]{3,1,2,0:T(4,128)S(1)}, f32[2,4,1,2048]{3,1,2,0:T(4,128)S(1)}, u32[]{:S(2)}, u32[]{:S(2)}) collective-permute-start(f32[2,4,1,2048]{3,1,2,0:T(4,128)S(1)} %copy.250), channel_id=1, source_target_pairs={{0,1},{1,2},{2,3},{3,4},{4,5},{5,6},{6,7},{7,8},{8,9},{9,10},{10,1... | collective-permute-start | bytes 196616 | tf_op jit(solution)/shard_map/ppermute | solution.py:27
  109.1 8.3 %collective-permute-start.6 = (f32[2,4,1,2048]{3,1,2,0:T(4,128)S(1)}, f32[2,4,1,2048]{3,1,2,0:T(4,128)S(1)}, u32[]{:S(2)}, u32[]{:S(2)}) collective-permute-start(f32[2,4,1,2048]{3,1,2,0:T(4,128)S(1)} %copy.251), channel_id=1, source_target_pairs={{1,0},{2,1},{3,2},{4,3},{5,4},{6,5},{7,6},{8,7},{9,8},{10,9},{11,1... | collective-permute-start | bytes 196616 | tf_op jit(solution)/shard_map/ppermute | solution.py:28
  119.2 5.3 %collective-permute-start.7 = (f32[2,4,1,2048]{3,1,2,0:T(4,128)S(1)}, f32[2,4,1,2048]{3,1,2,0:T(4,128)S(1)}, u32[]{:S(2)}, u32[]{:S(2)}) collective-permute-start(f32[2,4,1,2048]{3,1,2,0:T(4,128)S(1)} %copy.254), channel_id=1, source_target_pairs={{0,1},{1,2},{2,3},{3,4},{4,5},{5,6},{6,7},{7,8},{8,9},{9,10},{10,1... | collective-permute-start | bytes 196616 | tf_op jit(solution)/shard_map/ppermute | solution.py:27
  121.1 8.3 %collective-permute-start.8 = (f32[2,4,1,2048]{3,1,2,0:T(4,128)S(1)}, f32[2,4,1,2048]{3,1,2,0:T(4,128)S(1)}, u32[]{:S(2)}, u32[]{:S(2)}) collective-permute-start(f32[2,4,1,2048]{3,1,2,0:T(4,128)S(1)} %copy.255), channel_id=1, source_target_pairs={{1,0},{2,1},{3,2},{4,3},{5,4},{6,5},{7,6},{8,7},{9,8},{10,9},{11,1... | collective-permute-start | bytes 196616 | tf_op jit(solution)/shard_map/ppermute | solution.py:28
  131.2 5.3 %collective-permute-start.9 = (f32[2,4,1,2048]{3,1,2,0:T(4,128)S(1)}, f32[2,4,1,2048]{3,1,2,0:T(4,128)S(1)}, u32[]{:S(2)}, u32[]{:S(2)}) collective-permute-start(f32[2,4,1,2048]{3,1,2,0:T(4,128)S(1)} %copy.258), channel_id=1, source_target_pairs={{0,1},{1,2},{2,3},{3,4},{4,5},{5,6},{6,7},{7,8},{8,9},{9,10},{10,1... | collective-permute-start | bytes 196616 | tf_op jit(solution)/shard_map/ppermute | solution.py:27
  133.2 8.3 %collective-permute-start.10 = (f32[2,4,1,2048]{3,1,2,0:T(4,128)S(1)}, f32[2,4,1,2048]{3,1,2,0:T(4,128)S(1)}, u32[]{:S(2)}, u32[]{:S(2)}) collective-permute-start(f32[2,4,1,2048]{3,1,2,0:T(4,128)S(1)} %copy.259), channel_id=1, source_target_pairs={{1,0},{2,1},{3,2},{4,3},{5,4},{6,5},{7,6},{8,7},{9,8},{10,9},{11,1... | collective-permute-start | bytes 196616 | tf_op jit(solution)/shard_map/ppermute | solution.py:28
  143.2 5.3 %collective-permute-start.11 = (f32[2,4,1,2048]{3,1,2,0:T(4,128)S(1)}, f32[2,4,1,2048]{3,1,2,0:T(4,128)S(1)}, u32[]{:S(2)}, u32[]{:S(2)}) collective-permute-start(f32[2,4,1,2048]{3,1,2,0:T(4,128)S(1)} %copy.262), channel_id=1, source_target_pairs={{0,1},{1,2},{2,3},{3,4},{4,5},{5,6},{6,7},{7,8},{8,9},{9,10},{10,1... | collective-permute-start | bytes 196616 | tf_op jit(solution)/shard_map/ppermute | solution.py:27
  145.2 8.3 %collective-permute-start.12 = (f32[2,4,1,2048]{3,1,2,0:T(4,128)S(1)}, f32[2,4,1,2048]{3,1,2,0:T(4,128)S(1)}, u32[]{:S(2)}, u32[]{:S(2)}) collective-permute-start(f32[2,4,1,2048]{3,1,2,0:T(4,128)S(1)} %copy.263), channel_id=1, source_target_pairs={{1,0},{2,1},{3,2},{4,3},{5,4},{6,5},{7,6},{8,7},{9,8},{10,9},{11,1... | collective-permute-start | bytes 196616 | tf_op jit(solution)/shard_map/ppermute | solution.py:28
  155.2 5.3 %collective-permute-start.13 = (f32[2,4,1,2048]{3,1,2,0:T(4,128)S(1)}, f32[2,4,1,2048]{3,1,2,0:T(4,128)S(1)}, u32[]{:S(2)}, u32[]{:S(2)}) collective-permute-start(f32[2,4,1,2048]{3,1,2,0:T(4,128)S(1)} %copy.266), channel_id=1, source_target_pairs={{0,1},{1,2},{2,3},{3,4},{4,5},{5,6},{6,7},{7,8},{8,9},{9,10},{10,1... | collective-permute-start | bytes 196616 | tf_op jit(solution)/shard_map/ppermute | solution.py:27
  157.2 8.3 %collective-permute-start.14 = (f32[2,4,1,2048]{3,1,2,0:T(4,128)S(1)}, f32[2,4,1,2048]{3,1,2,0:T(4,128)S(1)}, u32[]{:S(2)}, u32[]{:S(2)}) collective-permute-start(f32[2,4,1,2048]{3,1,2,0:T(4,128)S(1)} %copy.267), channel_id=1, source_target_pairs={{1,0},{2,1},{3,2},{4,3},{5,4},{6,5},{7,6},{8,7},{9,8},{10,9},{11,1... | collective-permute-start | bytes 196616 | tf_op jit(solution)/shard_map/ppermute | solution.py:28
  167.3 5.6 %collective-permute-start.15 = (f32[2,4,1,2048]{3,1,2,0:T(4,128)S(1)}, f32[2,4,1,2048]{3,1,2,0:T(4,128)S(1)}, u32[]{:S(2)}, u32[]{:S(2)}) collective-permute-start(f32[2,4,1,2048]{3,1,2,0:T(4,128)S(1)} %copy.270), channel_id=1, source_target_pairs={{0,1},{1,2},{2,3},{3,4},{4,5},{5,6},{6,7},{7,8},{8,9},{9,10},{10,1... | collective-permute-start | bytes 196616 | tf_op jit(solution)/shard_map/ppermute | solution.py:27
  169.2 8.3 %collective-permute-start.16 = (f32[2,4,1,2048]{3,1,2,0:T(4,128)S(1)}, f32[2,4,1,2048]{3,1,2,0:T(4,128)S(1)}, u32[]{:S(2)}, u32[]{:S(2)}) collective-permute-start(f32[2,4,1,2048]{3,1,2,0:T(4,128)S(1)} %copy.271), channel_id=1, source_target_pairs={{1,0},{2,1},{3,2},{4,3},{5,4},{6,5},{7,6},{8,7},{9,8},{10,9},{11,1... | collective-permute-start | bytes 196616 | tf_op jit(solution)/shard_map/ppermute | solution.py:28
  189.4 22.8 %all-to-all-start.3 = ((f32[16,1,4096]{2,1,0:T(1,128)}), f32[16,1,4096]{2,1,0:T(1,128)S(1)}, u32[]{:S(2)}, u32[]{:S(2)}) async-start(f32[16,1,4096]{2,1,0:T(1,128)} %reshape.127), calls=%async_computation.3 | async-start | bytes 524288 | tf_op jit(solution)/shard_map/all_to_all | solution.py:120
  212.2 17.3 %all-to-all-start.4 = ((f32[16,1,4096]{2,1,0:T(1,128)}), f32[16,1,4096]{2,1,0:T(1,128)S(1)}, u32[]{:S(2)}, u32[]{:S(2)}) async-start(f32[16,1,4096]{2,1,0:T(1,128)} %reshape.129), calls=%async_computation.4 | async-start | bytes 524288 | tf_op jit(solution)/shard_map/all_to_all | solution.py:121
where the time goes:
time: 262 us; the launch traced here: 260 us
  starting transfers between devices  84.8 us (32%)
  waiting for transfers between devices  71.4 us (27%)
  local copies, waits for them, and re-layouts  66.2 us (25%)
  blocking collectives  18.1 us (7%)
  other arithmetic  17 us (6%)
    unnamed x15, local copies, waits for them, and re-layouts  40.6 us
    ppermute x8, waiting for transfers between devices, with_halo(): after = lax.ppermute(leading, axis, down)  36 us
    ppermute x8, starting transfers between devices, with_halo(): after = lax.ppermute(leading, axis, down)  24.5 us
    ppermute x8, starting transfers between devices, with_halo(): before = lax.ppermute(last, axis, up)  23.6 us
    all_to_all x1, blocking collectives, local(): lax.all_to_all(columns, 'tm', split_axis=0, concat_axis=2, tiled=True)  18.1 us
    all_to_all x1, waiting for transfers between devices, local(): lax.all_to_all(residual, 'tm', split_axis=2, concat_axis=0, tiled=True)  11.7 us
    all_to_all x1, waiting for transfers between devices, local(): lax.all_to_all(hat_imag, 'tm', split_axis=0, concat_axis=2, tiled=True)  11.6 us
    all_to_all x1, starting transfers between devices, local(): lax.all_to_all(sol_real, 'tm', split_axis=2, concat_axis=0, tiled=True)  10.9 us
  transfers between devices with their start and end apart: 22, of which 13 were waited for; matrix products, arithmetic and copies ran while one was open for 10% of the time, Pallas kernels for 0%

commit v1 on v0

v1 whole, which is shorter than its diff:
```python
import math

import jax
import jax.numpy as jnp
import numpy as np
from jax import lax
from jax.experimental import pallas as pl
from jax.experimental.pallas import tpu as pltpu
from jax.sharding import PartitionSpec as P

SWEEPS = 8
ALPHA = 0.01
STEPS = 64
HALF = STEPS // 2
DEVS = 16
LOCAL = STEPS // DEVS
ROWS = 8
LANES = 128
BLOCK = ROWS * LOCAL + ROWS
SPAN = 3 * ROWS
WIDE = 2 * LANES
F32 = jnp.float32


def tables():
    n = np.arange(STEPS)
    g = ALPHA ** (n / STEPS)
    k = np.arange(HALF)
    ang = 2.0 * np.pi * (np.outer(k, n) % STEPS) / STEPS
    fwd = np.concatenate([np.cos(ang) * g, -np.sin(ang) * g], 0)
    fwd[HALF] = (-1.0) ** n * g
    inv = np.concatenate([2.0 * np.cos(ang), -2.0 * np.sin(ang)], 0).T
    inv[:, 0] = 1.0
    inv[:, HALF] = (-1.0) ** n
    inv = inv / (STEPS * g[:, None])
    beta = ALPHA ** (1.0 / STEPS)
    shift_re = 1.0 - beta * np.cos(2.0 * np.pi * k / STEPS)
    shift_im = beta * np.sin(2.0 * np.pi * k / STEPS)
    shift_alt = shift_re.copy()
    shift_alt[0] = 1.0 + beta
    shifts = np.zeros((HALF, 3 * LANES), np.float32)
    shifts[:, :LANES] = shift_re[:, None]
    shifts[:, LANES : 2 * LANES] = shift_im[:, None]
    shifts[:, 2 * LANES :] = shift_alt[:, None]
    return fwd.astype(np.float32), inv.astype(np.float32), shifts


def lane_ids(rows):
    return lax.broadcasted_iota(jnp.int32, (rows, LANES), 1)


def rim(left, right):
    lane = lane_ids(ROWS)
    both = jnp.where(lane < 8, right, jnp.where(lane >= LANES - 8, left, 0.0))
    moved = pltpu.roll(both, 8, 1, stride=16, stride_axis=0)
    return jnp.sum(moved, axis=0, keepdims=True)


def pack_kernel(t_ref, it_ref, ini_ref, dif_ref, cx_ref, cy_ref, send_ref, coef_ref):
    zero = jnp.zeros((ROWS, LANES), F32)
    for d in range(DEVS):
        rims = []
        for n in range(LOCAL):
            cols = lambda e: it_ref[n, :, e * LANES : (e + 1) * LANES]
            send_ref[d, n * ROWS : (n + 1) * ROWS, :] = cols(d)
            rims.append(rim(cols(d - 1) if d else zero, cols(d + 1) if d + 1 < DEVS else zero))
        rims.append(jnp.zeros((ROWS - LOCAL, LANES), F32))
        send_ref[d, LOCAL * ROWS :, :] = jnp.concatenate(rims, 0)
    t = t_ref[0]
    rims = []
    for a, ref in enumerate((ini_ref, dif_ref, cx_ref, cy_ref)):
        cols = lambda e: ref[:, pl.ds(pl.multiple_of(e * LANES, LANES), LANES)]
        coef_ref[a * ROWS : (a + 1) * ROWS, :] = cols(t)
        left = jnp.where(t > 0, cols(jnp.maximum(t - 1, 0)), 0.0)
        right = jnp.where(t < DEVS - 1, cols(jnp.minimum(t + 1, DEVS - 1)), 0.0)
        rims.append(rim(left, right))
    rims.append(jnp.zeros((ROWS - LOCAL, LANES), F32))
    coef_ref[LOCAL * ROWS :, :] = jnp.concatenate(rims, 0)


def mul(matrix, value):
    return jnp.dot(matrix, value, precision=lax.Precision.HIGHEST, preferred_element_type=F32)


def solve_kernel(
    fwd_ref, inv_ref, shift_ref, up_ref, own_ref, dn_ref, cup_ref, cown_ref, cdn_ref,
    out_ref, x_ref, rim_ref, side_ref, wt_ref, a_ref, alt_ref, b_ref, f_ref, w_ref, v_ref,
):
    lane = lane_ids(1)
    inside = (lane < 8) | (lane >= LANES - 8)
    for blk, (ref, cref) in enumerate(((up_ref, cup_ref), (own_ref, cown_ref), (dn_ref, cdn_ref))):
        for d in range(DEVS):
            rim_ref[d * LOCAL : (d + 1) * LOCAL, :] = ref[d * BLOCK + LOCAL * ROWS : d * BLOCK + LOCAL * ROWS + LOCAL, :]
        rims = rim_ref[...]
        for r in range(ROWS):
            j = blk * ROWS + r
            for d in range(DEVS):
                x_ref[j, 8 + d * LOCAL : 8 + (d + 1) * LOCAL, :LANES] = ref[pl.ds(d * BLOCK + r, LOCAL, stride=ROWS), :]
            turned = pltpu.roll(rims, (2 * LANES - 16 * r - 8) % LANES, 1)
            x_ref[j, 8:, LANES:] = jnp.where(inside, turned, 0.0)
            turned = pltpu.roll(cref[LOCAL * ROWS :, :], (2 * LANES - 16 * r - 8) % LANES, 1)
            turned = jnp.where(inside, turned, 0.0)
            x_ref[j, 7:8, :LANES] = cref[r : r + 1, :]
            x_ref[j, 7:8, LANES:] = turned[0:1]
            for a in (1, 2, 3):
                side_ref[a, r : r + 1, :] = turned[a : a + 1]
        wide = []
        for a in (1, 2, 3):
            wide.append(jnp.concatenate([cref[a * ROWS : (a + 1) * ROWS, :], side_ref[a]], 1))
        dif, cx, cy = wide
        west = dif + jnp.maximum(cx, 0.0)
        east = dif + jnp.maximum(-cx, 0.0)
        north = dif + jnp.maximum(cy, 0.0)
        south = dif + jnp.maximum(-cy, 0.0)
        rows = slice(blk * ROWS, (blk + 1) * ROWS)
        for a, value in enumerate((west, east, north, south, west + east + north + south)):
            wt_ref[a, rows, :] = value

    def weights(j):
        return [wt_ref[a, pl.ds(j, 1), :] for a in range(5)]

    def near(wts, here, above, below):
        summed = wts[0] * pltpu.roll(here, 1, 1) + wts[1] * pltpu.roll(here, WIDE - 1, 1)
        return summed + wts[2] * above + wts[3] * below

    def first(j, carry):
        wts = weights(j)
        here = x_ref[j, 8:, :]
        r = x_ref[j, 7 : 7 + STEPS, :] - here + near(wts, here, x_ref[j - 1, 8:, :], x_ref[j + 1, 8:, :]) - wts[4] * here
        hat = mul(fwd_ref[...], r)
        for g in range(HALF // 8):
            part = slice(8 * g, 8 * g + 8)
            h_re, h_im = hat[8 * g : 8 * g + 8], hat[HALF + 8 * g : HALF + 8 * g + 8]
            rep = lambda c: jnp.concatenate([shift_ref[part, c * LANES : (c + 1) * LANES]] * 2, 1)
            s_im = rep(1)
            d_re = rep(0) + wts[4]
            norm = 1.0 / (d_re * d_re + s_im * s_im)
            a_re = d_re * norm
            a_im = a_re
            b = s_im * norm
            if g == 0:
                d_im = rep(2) + wts[4]
                a_im = d_im * (1.0 / (d_im * d_im + s_im * s_im))
                alt_ref[j] = a_im
            a_ref[j, part, :] = a_re
            b_ref[j, part, :] = b
            w_re = h_re * a_re + h_im * b
            w_im = h_im * a_im - h_re * b
            f_ref[j, part, :] = w_re
            f_ref[j, HALF + 8 * g : HALF + 8 * g + 8, :] = w_im
        return carry

    lax.fori_loop(1, SPAN - 1, first, 0)

    def sweep(src, dst, j):
        wts = weights(j)
        for g in range(HALF // 8):
            p_re = slice(8 * g, 8 * g + 8)
            p_im = slice(HALF + 8 * g, HALF + 8 * g + 8)
            n_re = near(wts, src[j, p_re, :], src[j - 1, p_re, :], src[j + 1, p_re, :])
            n_im = near(wts, src[j, p_im, :], src[j - 1, p_im, :], src[j + 1, p_im, :])
            a_re, b = a_ref[j, p_re, :], b_ref[j, p_re, :]
            a_im = alt_ref[j] if g == 0 else a_re
            dst[j, p_re, :] = f_ref[j, p_re, :] + (n_re * a_re + n_im * b)
            dst[j, p_im, :] = f_ref[j, p_im, :] + (n_im * a_im - n_re * b)

    src = f_ref
    for m in range(2, SWEEPS + 1):
        dst = w_ref if m % 2 == 0 else v_ref

        def body(j, carry, src=src, dst=dst):
            sweep(src, dst, j)
            return carry

        lax.fori_loop(m, SPAN - m, body, 0)
        src = dst

    for r in range(0, ROWS, 2):
        j = ROWS + r
        pair = jnp.concatenate([src[j, :, :LANES], src[j + 1, :, :LANES]], 1)
        corr = mul(inv_ref[...], pair)
        out_ref[pl.ds(r, STEPS, stride=ROWS), :] = x_ref[j, 8:, :LANES] + corr[:, :LANES]
        out_ref[pl.ds(r + 1, STEPS, stride=ROWS), :] = x_ref[j + 1, 8:, :LANES] + corr[:, LANES:]


def place_kernel(in_ref, out_ref):
    for d in range(DEVS):
        for n in range(LOCAL):
            out_ref[n, :, d * LANES : (d + 1) * LANES] = in_ref[d, n * ROWS : (n + 1) * ROWS, :]


def vmem(count):
    return [pl.BlockSpec(memory_space=pltpu.VMEM)] * count


def pack(t, iterate, initial, diffusion, courant_x, courant_y):
    return pl.pallas_call(
        pack_kernel,
        name="pack",
        out_shape=(
            jax.ShapeDtypeStruct((DEVS, BLOCK, LANES), F32),
            jax.ShapeDtypeStruct((BLOCK, LANES), F32),
        ),
        in_specs=[pl.BlockSpec(memory_space=pltpu.SMEM)] + vmem(5),
        out_specs=tuple(vmem(2)),
    )(t, iterate, initial, diffusion, courant_x, courant_y)


def solve(up, own, down, coef_up, coef, coef_down):
    fwd, inv, shifts = tables()
    big = pltpu.VMEM((SPAN, STEPS, WIDE), F32)
    half = pltpu.VMEM((SPAN, HALF, WIDE), F32)
    return pl.pallas_call(
        solve_kernel,
        name="solve",
        out_shape=jax.ShapeDtypeStruct((STEPS * ROWS, LANES), F32),
        in_specs=vmem(9),
        out_specs=vmem(1)[0],
        scratch_shapes=[
            pltpu.VMEM((SPAN, STEPS + 8, WIDE), F32),
            pltpu.VMEM((STEPS, LANES), F32),
            pltpu.VMEM((LOCAL, ROWS, LANES), F32),
            pltpu.VMEM((5, SPAN, WIDE), F32),
            half,
            pltpu.VMEM((SPAN, 8, WIDE), F32),
            half,
            big,
            big,
            big,
        ],
        compiler_params=pltpu.CompilerParams(vmem_limit_bytes=32 * 1024 * 1024),
    )(jnp.asarray(fwd), jnp.asarray(inv), jnp.asarray(shifts), up, own, down, coef_up, coef, coef_down)


def place(received):
    return pl.pallas_call(
        place_kernel,
        name="place",
        out_shape=jax.ShapeDtypeStruct((LOCAL, ROWS, DEVS * LANES), F32),
        in_specs=vmem(1),
        out_specs=vmem(1)[0],
    )(received)


def local(iterate, initial, diffusion, courant_x, courant_y):
    t = lax.axis_index("tm").astype(jnp.int32).reshape(1)
    send, coef = pack(t, iterate, initial, diffusion, courant_x, courant_y)
    count = lax.axis_size("space")
    down = [(i, i + 1) for i in range(count - 1)]
    up = [(i + 1, i) for i in range(count - 1)]
    coef_up = lax.ppermute(coef, "space", down)
    coef_down = lax.ppermute(coef, "space", up)
    own = lax.all_to_all(send, "tm", split_axis=0, concat_axis=0, tiled=True)
    own = own.reshape(DEVS * BLOCK, LANES)
    above = lax.ppermute(own, "space", down)
    below = lax.ppermute(own, "space", up)
    new = solve(above, own, below, coef_up, coef, coef_down)
    back = lax.all_to_all(new.reshape(DEVS, LOCAL * ROWS, LANES), "tm", split_axis=0, concat_axis=0, tiled=True)
    return place(back)


def solution(mesh):
    return jax.shard_map(
        local,
        mesh=mesh,
        in_specs=(
            P("tm", "space", None),
            P("space", None),
            P("space", None),
            P("space", None),
            P("space", None),
        ),
        out_specs=P("tm", "space", None),
        check_vma=False,
    )
```

time: 262 us -> 79.7 us (0.30)
  the two profiles are of different devices: /device:TPU:199 before, /device:TPU:257 now
where the time goes in v1:
time: 79.7 us; the launch traced here: 79.3 us
  blocking collectives  37.5 us (47%)
  Pallas kernels  21.7 us (27%)
  starting transfers between devices  14 us (18%)
  waiting for transfers between devices  5.92 us (7%)
    all_to_all x1, blocking collectives, local(): own = lax.all_to_all(send, 'tm', split_axis=0, concat_axis=0, tiled=True)  21 us
    pallas_call x1, Pallas kernels, solve(): pl.pallas_call(solve_kernel, name='solve', out_shape=jax.ShapeDtypeStruct...  18.1 us
    all_to_all x1, blocking collectives, local(): lax.all_to_all(new.reshape(DEVS, LOCAL * ROWS, LANES), 'tm', split_axis=0...  16.5 us
    ppermute x1, starting transfers between devices, local(): coef_down = lax.ppermute(coef, 'space', up)  6.68 us
    ppermute x1, waiting for transfers between devices, local(): coef_up = lax.ppermute(coef, 'space', down)  5.91 us
    ppermute x1, starting transfers between devices, local(): below = lax.ppermute(own, 'space', up)  3.47 us
    ppermute x1, starting transfers between devices, local(): above = lax.ppermute(own, 'space', down)  1.92 us
    ppermute x1, starting transfers between devices, local(): coef_up = lax.ppermute(coef, 'space', down)  1.92 us
  transfers between devices with their start and end apart: 4, of which 1 were waited for; matrix products, arithmetic and copies ran while one was open for 0% of the time, Pallas kernels for 0%

profile of v1, /device:TPU:257, one launch (start us, length us, event | category | flops | bytes accessed | tf_op | source)
XLA Modules:
  0.0 79.3 jit_solution(1345051753387347606)
XLA Ops:
  0.0 1.9 %pack.1 = (f32[16,40,128]{2,1,0:T(8,128)}, f32[40,128]{1,0:T(8,128)}) custom-call(s32[1]{0:T(128)} %bitcast.t_ref, f32[4,8,2048]{2,1,0:T(8,128)} %it_ref.1, f32[8,2048]{1,0:T(8,128)} %ini_ref.1, f32[8,2048]{1,0:T(8,128)} %dif_ref.1, f32[8,2048]{1,0:T(8,128)} %cx_ref.1, f32[8,2048]{1,0:T(8,128)} %cy_ref.1), custom_call_target="tpu_custom_call" | custom-call | tf_op jit(solution)/shard_map/pack/pallas_call | solution.py:197
  1.9 0.0 copy-start.3
  1.9 0.0 copy-start
  1.9 0.0 copy-start.1
  1.9 0.0 copy-start.2
  1.9 21.0 %all_to_all.10 = f32[16,40,128]{2,1,0:T(8,128)S(1)} all-to-all(f32[16,40,128]{2,1,0:T(8,128)} %get-tuple-element.7), channel_id=1, replica_groups=mesh['tm'=16,'space'=32] {'tm'}, dimensions={0} | all-to-all | bytes 655360 | tf_op jit(solution)/shard_map/all_to_all | solution.py:253
  22.9 3.5 %collective-permute-start.1 = (f32[640,128]{1,0:T(8,128)S(1)}, f32[640,128]{1,0:T(8,128)S(1)}, u32[]{:S(2)}, u32[]{:S(2)}) collective-permute-start(f32[640,128]{1,0:T(8,128)S(1)} %bitcast.3), channel_id=1, source_target_pairs={{1,0},{2,1},{3,2},{4,3},{5,4},{6,5},{7,6},{8,7},{9,8},{10,9},{11,1... | collective-permute-start | bytes 983048 | tf_op jit(solution)/shard_map/ppermute | solution.py:256
  26.4 1.9 %collective-permute-start = (f32[640,128]{1,0:T(8,128)S(1)}, f32[640,128]{1,0:T(8,128)S(1)}, u32[]{:S(2)}, u32[]{:S(2)}) collective-permute-start(f32[640,128]{1,0:T(8,128)S(1)} %bitcast.4), channel_id=1, source_target_pairs={{0,1},{1,2},{2,3},{3,4},{4,5},{5,6},{6,7},{7,8},{8,9},{9,10},{10,1... | collective-permute-start | bytes 983048 | tf_op jit(solution)/shard_map/ppermute | solution.py:255
  28.3 0.0 copy-done.3
  28.3 6.7 %collective-permute-start.3 = (f32[40,128]{1,0:T(8,128)S(1)}, f32[40,128]{1,0:T(8,128)S(1)}, u32[]{:S(2)}, u32[]{:S(2)}) collective-permute-start(f32[40,128]{1,0:T(8,128)S(1)} %copy-done.3), channel_id=1, source_target_pairs={{1,0},{2,1},{3,2},{4,3},{5,4},{6,5},{7,6},{8,7},{9,8},{10,9},{11,1... | collective-permute-start | bytes 61448 | tf_op jit(solution)/shard_map/ppermute | solution.py:252
  35.0 1.9 %collective-permute-start.2 = (f32[40,128]{1,0:T(8,128)S(1)}, f32[40,128]{1,0:T(8,128)S(1)}, u32[]{:S(2)}, u32[]{:S(2)}) collective-permute-start(f32[40,128]{1,0:T(8,128)S(1)} %copy-done.3), channel_id=1, source_target_pairs={{0,1},{1,2},{2,3},{3,4},{4,5},{5,6},{6,7},{7,8},{8,9},{9,10},{10,1... | collective-permute-start | bytes 61448 | tf_op jit(solution)/shard_map/ppermute | solution.py:251
  37.0 0.0 collective-permute-done.3.cdn_ref
  37.0 5.9 %collective-permute-done.2.cup_ref = f32[40,128]{1,0:T(8,128)S(1)} collective-permute-done((f32[40,128]{1,0:T(8,128)S(1)}, f32[40,128]{1,0:T(8,128)S(1)}, u32[]{:S(2)}, u32[]{:S(2)}) %collective-permute-start.2) | collective-permute-done | bytes 20512 | tf_op jit(solution)/shard_map/ppermute | solution.py:251
  42.9 0.0 collective-permute-done.1.dn_ref
  42.9 0.0 collective-permute-done.up_ref
  42.9 0.0 copy-done
  42.9 0.0 copy-done.1
  42.9 0.0 copy-done.2
  42.9 18.1 %solve.1 = f32[512,128]{1,0:T(8,128)S(1)} custom-call(f32[64,64]{1,0:T(8,128)S(1)} %copy-done.2, f32[64,64]{1,0:T(8,128)S(1)} %copy-done.1, f32[32,384]{1,0:T(8,128)S(1)} %copy-done, f32[640,128]{1,0:T(8,128)S(1)} %collective-permute-done.up_ref, f32[640,128]{1,0:T(8,128)S(1)} %bitcast.5, f32[640,128]{1,0:T(8,128)S(1)} %collective-permute-done.1.dn_ref, ...), custom_call_target="tpu_custom_call" | custom-call | tf_op jit(solution)/shard_map/solve/pallas_call | solution.py:213
  61.1 16.5 %all_to_all.11.in_ref = f32[16,32,128]{2,1,0:T(8,128)} all-to-all(f32[16,32,128]{2,1,0:T(8,128)S(1)} %bitcast.6), channel_id=1, replica_groups=mesh['tm'=16,'space'=32] {'tm'}, dimensions={0} | all-to-all | bytes 524288 | tf_op jit(solution)/shard_map/all_to_all | solution.py:258
  77.6 1.7 %place.1 = f32[4,8,2048]{2,1,0:T(8,128)} custom-call(f32[16,32,128]{2,1,0:T(8,128)} %all_to_all.11.in_ref), custom_call_target="tpu_custom_call" | custom-call | tf_op jit(solution)/shard_map/place/pallas_call | solution.py:236
Async XLA Ops:
  1.9 26.4 %copy-start.3 = (f32[40,128]{1,0:T(8,128)S(1)}, f32[40,128]{1,0:T(8,128)}, u32[]{:S(2)}) copy-start(f32[40,128]{1,0:T(8,128)} %get-tuple-element.8.cown_ref) | copy-start | bytes 61444
  1.9 41.0 %copy-start = (f32[32,384]{1,0:T(8,128)S(1)}, f32[32,384]{1,0:T(8,128)}, u32[]{:S(2)}) copy-start(f32[32,384]{1,0:T(8,128)} %constant.14.clone.shift_ref) | copy-start | bytes 147460
  1.9 41.0 %copy-start.1 = (f32[64,64]{1,0:T(8,128)S(1)}, f32[64,64]{1,0:T(8,128)}, u32[]{:S(2)}) copy-start(f32[64,64]{1,0:T(8,128)} %constant.13.clone.inv_ref) | copy-start | bytes 49156
  1.9 41.0 %copy-start.2 = (f32[64,64]{1,0:T(8,128)S(1)}, f32[64,64]{1,0:T(8,128)}, u32[]{:S(2)}) copy-start(f32[64,64]{1,0:T(8,128)} %constant.12.clone.fwd_ref) | copy-start | bytes 49156
  22.9 20.0 %collective-permute-start.1 = (f32[640,128]{1,0:T(8,128)S(1)}, f32[640,128]{1,0:T(8,128)S(1)}, u32[]{:S(2)}, u32[]{:S(2)}) collective-permute-start(f32[640,128]{1,0:T(8,128)S(1)} %bitcast.3), channel_id=1, source_target_pairs={{1,0},{2,1},{3,2},{4,3},{5,4},{6,5},{7,6},{8,7},{9,8},{10,9},{11,1... | collective-permute-start | bytes 983048 | tf_op jit(solution)/shard_map/ppermute | solution.py:256
  26.4 16.5 %collective-permute-start = (f32[640,128]{1,0:T(8,128)S(1)}, f32[640,128]{1,0:T(8,128)S(1)}, u32[]{:S(2)}, u32[]{:S(2)}) collective-permute-start(f32[640,128]{1,0:T(8,128)S(1)} %bitcast.4), channel_id=1, source_target_pairs={{0,1},{1,2},{2,3},{3,4},{4,5},{5,6},{6,7},{7,8},{8,9},{9,10},{10,1... | collective-permute-start | bytes 983048 | tf_op jit(solution)/shard_map/ppermute | solution.py:255
  28.3 8.6 %collective-permute-start.3 = (f32[40,128]{1,0:T(8,128)S(1)}, f32[40,128]{1,0:T(8,128)S(1)}, u32[]{:S(2)}, u32[]{:S(2)}) collective-permute-start(f32[40,128]{1,0:T(8,128)S(1)} %copy-done.3), channel_id=1, source_target_pairs={{1,0},{2,1},{3,2},{4,3},{5,4},{6,5},{7,6},{8,7},{9,8},{10,9},{11,1... | collective-permute-start | bytes 61448 | tf_op jit(solution)/shard_map/ppermute | solution.py:252
  35.0 7.8 %collective-permute-start.2 = (f32[40,128]{1,0:T(8,128)S(1)}, f32[40,128]{1,0:T(8,128)S(1)}, u32[]{:S(2)}, u32[]{:S(2)}) collective-permute-start(f32[40,128]{1,0:T(8,128)S(1)} %copy-done.3), channel_id=1, source_target_pairs={{0,1},{1,2},{2,3},{3,4},{4,5},{5,6},{6,7},{7,8},{8,9},{9,10},{10,1... | collective-permute-start | bytes 61448 | tf_op jit(solution)/shard_map/ppermute | solution.py:251

commit v2 on v1

--- a/solution.py
+++ b/solution.py
@@ -56,26 +56,26 @@
     return jnp.sum(moved, axis=0, keepdims=True)
 
 
-def pack_kernel(t_ref, it_ref, ini_ref, dif_ref, cx_ref, cy_ref, send_ref, coef_ref):
+def pack_kernel(t_ref, it_ref, ini_ref, dif_ref, cx_ref, cy_ref, send_ref):
+    t = t_ref[0]
+    which, share = t % 4, t // 4
+    coef = jnp.where(which < 2, jnp.where(which == 0, ini_ref[...], dif_ref[...]), jnp.where(which == 2, cx_ref[...], cy_ref[...]))
+    turned = pltpu.roll(coef, (ROWS - 2 * share) % ROWS, 0)
     zero = jnp.zeros((ROWS, LANES), F32)
+
+    def sides(cols, d):
+        return rim(cols(d - 1) if d else zero, cols(d + 1) if d + 1 < DEVS else zero)
+
     for d in range(DEVS):
         rims = []
         for n in range(LOCAL):
             cols = lambda e: it_ref[n, :, e * LANES : (e + 1) * LANES]
             send_ref[d, n * ROWS : (n + 1) * ROWS, :] = cols(d)
-            rims.append(rim(cols(d - 1) if d else zero, cols(d + 1) if d + 1 < DEVS else zero))
-        rims.append(jnp.zeros((ROWS - LOCAL, LANES), F32))
+            rims.append(sides(cols, d))
+        rims.append(turned[:2, d * LANES : (d + 1) * LANES])
+        rims.append(sides(lambda e: coef[:, e * LANES : (e + 1) * LANES], d))
+        rims.append(jnp.zeros((1, LANES), F32))
         send_ref[d, LOCAL * ROWS :, :] = jnp.concatenate(rims, 0)
-    t = t_ref[0]
-    rims = []
-    for a, ref in enumerate((ini_ref, dif_ref, cx_ref, cy_ref)):
-        cols = lambda e: ref[:, pl.ds(pl.multiple_of(e * LANES, LANES), LANES)]
-        coef_ref[a * ROWS : (a + 1) * ROWS, :] = cols(t)
-        left = jnp.where(t > 0, cols(jnp.maximum(t - 1, 0)), 0.0)
-        right = jnp.where(t < DEVS - 1, cols(jnp.minimum(t + 1, DEVS - 1)), 0.0)
-        rims.append(rim(left, right))
-    rims.append(jnp.zeros((ROWS - LOCAL, LANES), F32))
-    coef_ref[LOCAL * ROWS :, :] = jnp.concatenate(rims, 0)
 
 
 def mul(matrix, value):
@@ -83,31 +83,30 @@
 
 
 def solve_kernel(
-    fwd_ref, inv_ref, shift_ref, up_ref, own_ref, dn_ref, cup_ref, cown_ref, cdn_ref,
-    out_ref, x_ref, rim_ref, side_ref, wt_ref, a_ref, alt_ref, b_ref, f_ref, w_ref, v_ref,
+    fwd_ref, inv_ref, shift_ref, up_ref, own_ref, dn_ref,
+    out_ref, x_ref, rim_ref, coef_ref, wt_ref, a_ref, alt_ref, b_ref, f_ref, w_ref, v_ref,
 ):
     lane = lane_ids(1)
     inside = (lane < 8) | (lane >= LANES - 8)
-    for blk, (ref, cref) in enumerate(((up_ref, cup_ref), (own_ref, cown_ref), (dn_ref, cdn_ref))):
+    for blk, ref in enumerate((up_ref, own_ref, dn_ref)):
         for d in range(DEVS):
-            rim_ref[d * LOCAL : (d + 1) * LOCAL, :] = ref[d * BLOCK + LOCAL * ROWS : d * BLOCK + LOCAL * ROWS + LOCAL, :]
+            base = d * BLOCK + LOCAL * ROWS
+            rim_ref[d * LOCAL : (d + 1) * LOCAL, :] = ref[base : base + LOCAL, :]
+            share = 2 * (d // 4)
+            coef_ref[d % 4, share : share + 2, :LANES] = ref[base + LOCAL : base + LOCAL + 2, :]
+            if d < 4:
+                rim_ref[STEPS + d : STEPS + d + 1, :] = ref[base + LOCAL + 2 : base + LOCAL + 3, :]
         rims = rim_ref[...]
         for r in range(ROWS):
             j = blk * ROWS + r
             for d in range(DEVS):
                 x_ref[j, 8 + d * LOCAL : 8 + (d + 1) * LOCAL, :LANES] = ref[pl.ds(d * BLOCK + r, LOCAL, stride=ROWS), :]
-            turned = pltpu.roll(rims, (2 * LANES - 16 * r - 8) % LANES, 1)
-            x_ref[j, 8:, LANES:] = jnp.where(inside, turned, 0.0)
-            turned = pltpu.roll(cref[LOCAL * ROWS :, :], (2 * LANES - 16 * r - 8) % LANES, 1)
-            turned = jnp.where(inside, turned, 0.0)
-            x_ref[j, 7:8, :LANES] = cref[r : r + 1, :]
-            x_ref[j, 7:8, LANES:] = turned[0:1]
-            for a in (1, 2, 3):
-                side_ref[a, r : r + 1, :] = turned[a : a + 1]
-        wide = []
-        for a in (1, 2, 3):
-            wide.append(jnp.concatenate([cref[a * ROWS : (a + 1) * ROWS, :], side_ref[a]], 1))
-        dif, cx, cy = wide
+            turned = jnp.where(inside, pltpu.roll(rims, (2 * LANES - 16 * r - 8) % LANES, 1), 0.0)
+            x_ref[j, 8:, LANES:] = turned[:STEPS]
+            for a in range(4):
+                coef_ref[a, r : r + 1, LANES:] = turned[STEPS + a : STEPS + a + 1]
+            x_ref[j, 7:8, :] = coef_ref[0, r : r + 1, :]
+        dif, cx, cy = coef_ref[1], coef_ref[2], coef_ref[3]
         west = dif + jnp.maximum(cx, 0.0)
         east = dif + jnp.maximum(-cx, 0.0)
         north = dif + jnp.maximum(cy, 0.0)
@@ -117,13 +116,13 @@
             wt_ref[a, rows, :] = value
 
     def weights(j):
-        return [wt_ref[a, pl.ds(j, 1), :] for a in range(5)]
+        return [wt_ref[a, j : j + 1, :] for a in range(5)]
 
     def near(wts, here, above, below):
         summed = wts[0] * pltpu.roll(here, 1, 1) + wts[1] * pltpu.roll(here, WIDE - 1, 1)
         return summed + wts[2] * above + wts[3] * below
 
-    def first(j, carry):
+    def first(j):
         wts = weights(j)
         here = x_ref[j, 8:, :]
         r = x_ref[j, 7 : 7 + STEPS, :] - here + near(wts, here, x_ref[j - 1, 8:, :], x_ref[j + 1, 8:, :]) - wts[4] * here
@@ -148,9 +147,9 @@
             w_im = h_im * a_im - h_re * b
             f_ref[j, part, :] = w_re
             f_ref[j, HALF + 8 * g : HALF + 8 * g + 8, :] = w_im
-        return carry
-
-    lax.fori_loop(1, SPAN - 1, first, 0)
+
+    for j in range(1, SPAN - 1):
+        first(j)
 
     def sweep(src, dst, j):
         wts = weights(j)
@@ -167,12 +166,8 @@
     src = f_ref
     for m in range(2, SWEEPS + 1):
         dst = w_ref if m % 2 == 0 else v_ref
-
-        def body(j, carry, src=src, dst=dst):
+        for j in range(m, SPAN - m):
             sweep(src, dst, j)
-            return carry
-
-        lax.fori_loop(m, SPAN - m, body, 0)
         src = dst
 
     for r in range(0, ROWS, 2):
@@ -197,16 +192,13 @@
     return pl.pallas_call(
         pack_kernel,
         name="pack",
-        out_shape=(
-            jax.ShapeDtypeStruct((DEVS, BLOCK, LANES), F32),
-            jax.ShapeDtypeStruct((BLOCK, LANES), F32),
-        ),
+        out_shape=jax.ShapeDtypeStruct((DEVS, BLOCK, LANES), F32),
         in_specs=[pl.BlockSpec(memory_space=pltpu.SMEM)] + vmem(5),
-        out_specs=tuple(vmem(2)),
+        out_specs=vmem(1)[0],
     )(t, iterate, initial, diffusion, courant_x, courant_y)
 
 
-def solve(up, own, down, coef_up, coef, coef_down):
+def solve(up, own, down):
     fwd, inv, shifts = tables()
     big = pltpu.VMEM((SPAN, STEPS, WIDE), F32)
     half = pltpu.VMEM((SPAN, HALF, WIDE), F32)
@@ -214,12 +206,12 @@
         solve_kernel,
         name="solve",
         out_shape=jax.ShapeDtypeStruct((STEPS * ROWS, LANES), F32),
-        in_specs=vmem(9),
+        in_specs=vmem(6),
         out_specs=vmem(1)[0],
         scratch_shapes=[
             pltpu.VMEM((SPAN, STEPS + 8, WIDE), F32),
-            pltpu.VMEM((STEPS, LANES), F32),
-            pltpu.VMEM((LOCAL, ROWS, LANES), F32),
+            pltpu.VMEM((STEPS + 8, LANES), F32),
+            pltpu.VMEM((4, ROWS, WIDE), F32),
             pltpu.VMEM((5, SPAN, WIDE), F32),
             half,
             pltpu.VMEM((SPAN, 8, WIDE), F32),
@@ -229,7 +221,7 @@
             big,
         ],
         compiler_params=pltpu.CompilerParams(vmem_limit_bytes=32 * 1024 * 1024),
-    )(jnp.asarray(fwd), jnp.asarray(inv), jnp.asarray(shifts), up, own, down, coef_up, coef, coef_down)
+    )(jnp.asarray(fwd), jnp.asarray(inv), jnp.asarray(shifts), up, own, down)
 
 
 def place(received):
@@ -244,17 +236,15 @@
 
 def local(iterate, initial, diffusion, courant_x, courant_y):
     t = lax.axis_index("tm").astype(jnp.int32).reshape(1)
-    send, coef = pack(t, iterate, initial, diffusion, courant_x, courant_y)
+    send = pack(t, iterate, initial, diffusion, courant_x, courant_y)
     count = lax.axis_size("space")
     down = [(i, i + 1) for i in range(count - 1)]
     up = [(i + 1, i) for i in range(count - 1)]
-    coef_up = lax.ppermute(coef, "space", down)
-    coef_down = lax.ppermute(coef, "space", up)
     own = lax.all_to_all(send, "tm", split_axis=0, concat_axis=0, tiled=True)
     own = own.reshape(DEVS * BLOCK, LANES)
     above = lax.ppermute(own, "space", down)
     below = lax.ppermute(own, "space", up)
-    new = solve(above, own, below, coef_up, coef, coef_down)
+    new = solve(above, own, below)
     back = lax.all_to_all(new.reshape(DEVS, LOCAL * ROWS, LANES), "tm", split_axis=0, concat_axis=0, tiled=True)
     return place(back)
 

time: 79.7 us -> 64.8 us (0.81)
  Pallas kernels: 21.7 us -> 9.68 us
  starting transfers between devices: 14 us -> 5.39 us
  waiting for transfers between devices: 5.92 us -> 12.8 us
  blocking collectives: 37.5 us -> 36.5 us
    pallas_call x1, Pallas kernels: 18.1 us -> 6.11 us  [solve(): pl.pallas_call(solve_kernel, name='solve', out_shape=jax.ShapeDtypeStruct...]
    ppermute x2 -> x0, starting transfers between devices: 8.6 us -> none  [the longest x1 6.68 us: local(): coef_down = lax.ppermute(coef, 'space', up)]
    ppermute x1, waiting for transfers between devices: 0.01 us -> 6.86 us  [local(): above = lax.ppermute(own, 'space', down)]
    ppermute x1, waiting for transfers between devices: 0.01 us -> 5.98 us  [local(): below = lax.ppermute(own, 'space', up)]
    ppermute x2 -> x0, waiting for transfers between devices: 5.91 us -> none  [the longest x1 5.91 us: local(): coef_up = lax.ppermute(coef, 'space', down)]
    all_to_all x1, blocking collectives: 16.5 us -> 15.5 us  [local(): lax.all_to_all(new.reshape(DEVS, LOCAL * ROWS, LANES), 'tm', split_axis=0...]
  transfers between devices with their start and end apart: 4 -> 2, of which waited for: 1 -> 2; matrix products, arithmetic and copies ran while one was open for 0% -> 0% of each run, Pallas kernels for 0% -> 0%
where the time goes in v2:
time: 64.8 us; the launch traced here: 64.5 us
  blocking collectives  36.5 us (56%)
  waiting for transfers between devices  12.8 us (20%)
  Pallas kernels  9.68 us (15%)
  starting transfers between devices  5.39 us (8%)
    all_to_all x1, blocking collectives, local(): own = lax.all_to_all(send, 'tm', split_axis=0, concat_axis=0, tiled=True)  21 us
    all_to_all x1, blocking collectives, local(): lax.all_to_all(new.reshape(DEVS, LOCAL * ROWS, LANES), 'tm', split_axis=0...  15.5 us
    ppermute x1, waiting for transfers between devices, local(): above = lax.ppermute(own, 'space', down)  6.86 us
    pallas_call x1, Pallas kernels, solve(): pl.pallas_call(solve_kernel, name='solve', out_shape=jax.ShapeDtypeStruct...  6.11 us
    ppermute x1, waiting for transfers between devices, local(): below = lax.ppermute(own, 'space', up)  5.98 us
    ppermute x1, starting transfers between devices, local(): below = lax.ppermute(own, 'space', up)  3.47 us
    ppermute x1, starting transfers between devices, local(): above = lax.ppermute(own, 'space', down)  1.92 us
    pallas_call x1, Pallas kernels, pack(): pl.pallas_call(pack_kernel, name='pack', out_shape=jax.ShapeDtypeStruct((...  1.91 us
  transfers between devices with their start and end apart: 2, of which 2 were waited for; matrix products, arithmetic and copies ran while one was open for 0% of the time, Pallas kernels for 0%

profile of v2, /device:TPU:257, one launch (start us, length us, event | category | flops | bytes accessed | tf_op | source)
XLA Modules:
  0.0 64.5 jit_solution(7456498362445429292)
XLA Ops:
  0.0 1.9 %pack.1 = f32[16,40,128]{2,1,0:T(8,128)} custom-call(s32[1]{0:T(128)} %bitcast.t_ref, f32[4,8,2048]{2,1,0:T(8,128)} %it_ref.1, f32[8,2048]{1,0:T(8,128)} %ini_ref.1, f32[8,2048]{1,0:T(8,128)} %dif_ref.1, f32[8,2048]{1,0:T(8,128)} %cx_ref.1, f32[8,2048]{1,0:T(8,128)} %cy_ref.1), custom_call_target="tpu_custom_call" | custom-call | tf_op jit(solution)/shard_map/pack/pallas_call | solution.py:192
  1.9 0.0 copy-start
  1.9 0.0 copy-start.1
  1.9 0.0 copy-start.2
  1.9 21.0 %all_to_all.10 = f32[16,40,128]{2,1,0:T(8,128)S(1)} all-to-all(f32[16,40,128]{2,1,0:T(8,128)} %pack.1), channel_id=1, replica_groups=mesh['tm'=16,'space'=32] {'tm'}, dimensions={0} | all-to-all | bytes 655360 | tf_op jit(solution)/shard_map/all_to_all | solution.py:243
  22.9 3.5 %collective-permute-start.1 = (f32[640,128]{1,0:T(8,128)S(1)}, f32[640,128]{1,0:T(8,128)S(1)}, u32[]{:S(2)}, u32[]{:S(2)}) collective-permute-start(f32[640,128]{1,0:T(8,128)S(1)} %bitcast.3), channel_id=1, source_target_pairs={{1,0},{2,1},{3,2},{4,3},{5,4},{6,5},{7,6},{8,7},{9,8},{10,9},{11,1... | collective-permute-start | bytes 983048 | tf_op jit(solution)/shard_map/ppermute | solution.py:246
  26.4 1.9 %collective-permute-start = (f32[640,128]{1,0:T(8,128)S(1)}, f32[640,128]{1,0:T(8,128)S(1)}, u32[]{:S(2)}, u32[]{:S(2)}) collective-permute-start(f32[640,128]{1,0:T(8,128)S(1)} %bitcast.4), channel_id=1, source_target_pairs={{0,1},{1,2},{2,3},{3,4},{4,5},{5,6},{6,7},{7,8},{8,9},{9,10},{10,1... | collective-permute-start | bytes 983048 | tf_op jit(solution)/shard_map/ppermute | solution.py:245
  28.3 6.0 %collective-permute-done.1.dn_ref = f32[640,128]{1,0:T(8,128)S(1)} collective-permute-done((f32[640,128]{1,0:T(8,128)S(1)}, f32[640,128]{1,0:T(8,128)S(1)}, u32[]{:S(2)}, u32[]{:S(2)}) %collective-permute-start.1) | collective-permute-done | bytes 327712 | tf_op jit(solution)/shard_map/ppermute | solution.py:246
  34.3 6.9 %collective-permute-done.up_ref = f32[640,128]{1,0:T(8,128)S(1)} collective-permute-done((f32[640,128]{1,0:T(8,128)S(1)}, f32[640,128]{1,0:T(8,128)S(1)}, u32[]{:S(2)}, u32[]{:S(2)}) %collective-permute-start) | collective-permute-done | bytes 327712 | tf_op jit(solution)/shard_map/ppermute | solution.py:245
  41.2 0.0 copy-done
  41.2 0.0 copy-done.1
  41.2 0.0 copy-done.2
  41.2 6.1 %solve.1 = f32[512,128]{1,0:T(8,128)S(1)} custom-call(f32[64,64]{1,0:T(8,128)S(1)} %copy-done.2, f32[64,64]{1,0:T(8,128)S(1)} %copy-done.1, f32[32,384]{1,0:T(8,128)S(1)} %copy-done, f32[640,128]{1,0:T(8,128)S(1)} %collective-permute-done.up_ref, f32[640,128]{1,0:T(8,128)S(1)} %bitcast.5, f32[640,128]{1,0:T(8,128)S(1)} %collective-permute-done.1.dn_ref), custom_call_target="tpu_custom_call" | custom-call | tf_op jit(solution)/shard_map/solve/pallas_call | solution.py:205
  47.3 15.5 %all_to_all.11.in_ref = f32[16,32,128]{2,1,0:T(8,128)} all-to-all(f32[16,32,128]{2,1,0:T(8,128)S(1)} %bitcast.6), channel_id=1, replica_groups=mesh['tm'=16,'space'=32] {'tm'}, dimensions={0} | all-to-all | bytes 524288 | tf_op jit(solution)/shard_map/all_to_all | solution.py:248
  62.8 1.7 %place.1 = f32[4,8,2048]{2,1,0:T(8,128)} custom-call(f32[16,32,128]{2,1,0:T(8,128)} %all_to_all.11.in_ref), custom_call_target="tpu_custom_call" | custom-call | tf_op jit(solution)/shard_map/place/pallas_call | solution.py:228
Async XLA Ops:
  1.9 39.2 %copy-start = (f32[32,384]{1,0:T(8,128)S(1)}, f32[32,384]{1,0:T(8,128)}, u32[]{:S(2)}) copy-start(f32[32,384]{1,0:T(8,128)} %constant.14.clone.shift_ref) | copy-start | bytes 147460
  1.9 39.2 %copy-start.1 = (f32[64,64]{1,0:T(8,128)S(1)}, f32[64,64]{1,0:T(8,128)}, u32[]{:S(2)}) copy-start(f32[64,64]{1,0:T(8,128)} %constant.13.clone.inv_ref) | copy-start | bytes 49156
  1.9 39.2 %copy-start.2 = (f32[64,64]{1,0:T(8,128)S(1)}, f32[64,64]{1,0:T(8,128)}, u32[]{:S(2)}) copy-start(f32[64,64]{1,0:T(8,128)} %constant.12.clone.fwd_ref) | copy-start | bytes 49156
  22.9 11.4 %collective-permute-start.1 = (f32[640,128]{1,0:T(8,128)S(1)}, f32[640,128]{1,0:T(8,128)S(1)}, u32[]{:S(2)}, u32[]{:S(2)}) collective-permute-start(f32[640,128]{1,0:T(8,128)S(1)} %bitcast.3), channel_id=1, source_target_pairs={{1,0},{2,1},{3,2},{4,3},{5,4},{6,5},{7,6},{8,7},{9,8},{10,9},{11,1... | collective-permute-start | bytes 983048 | tf_op jit(solution)/shard_map/ppermute | solution.py:246
  26.4 14.8 %collective-permute-start = (f32[640,128]{1,0:T(8,128)S(1)}, f32[640,128]{1,0:T(8,128)S(1)}, u32[]{:S(2)}, u32[]{:S(2)}) collective-permute-start(f32[640,128]{1,0:T(8,128)S(1)} %bitcast.4), channel_id=1, source_target_pairs={{0,1},{1,2},{2,3},{3,4},{4,5},{5,6},{6,7},{7,8},{8,9},{9,10},{10,1... | collective-permute-start | bytes 983048 | tf_op jit(solution)/shard_map/ppermute | solution.py:245

commit v3 on v2

v3 whole, which is shorter than its diff:
```python
import math

import jax
import jax.numpy as jnp
import numpy as np
from jax import lax
from jax.experimental import pallas as pl
from jax.experimental.pallas import tpu as pltpu
from jax.sharding import PartitionSpec as P

SWEEPS = 8
ALPHA = 0.01
STEPS = 64
HALF = STEPS // 2
DEVS = 16
LOCAL = STEPS // DEVS
ROWS = 8
LANES = 128
BLOCK = ROWS * LOCAL + ROWS
SPAN = 3 * ROWS
WIDE = 2 * LANES
F32 = jnp.float32


def tables():
    n = np.arange(STEPS)
    g = ALPHA ** (n / STEPS)
    k = np.arange(HALF)
    ang = 2.0 * np.pi * (np.outer(k, n) % STEPS) / STEPS
    fwd = np.concatenate([np.cos(ang) * g, -np.sin(ang) * g], 0)
    fwd[HALF] = (-1.0) ** n * g
    inv = np.concatenate([2.0 * np.cos(ang), -2.0 * np.sin(ang)], 0).T
    inv[:, 0] = 1.0
    inv[:, HALF] = (-1.0) ** n
    inv = inv / (STEPS * g[:, None])
    beta = ALPHA ** (1.0 / STEPS)
    shift_re = 1.0 - beta * np.cos(2.0 * np.pi * k / STEPS)
    shift_im = beta * np.sin(2.0 * np.pi * k / STEPS)
    shift_alt = shift_re.copy()
    shift_alt[0] = 1.0 + beta
    shifts = np.zeros((HALF, 3 * LANES), np.float32)
    shifts[:, :LANES] = shift_re[:, None]
    shifts[:, LANES : 2 * LANES] = shift_im[:, None]
    shifts[:, 2 * LANES :] = shift_alt[:, None]
    return fwd.astype(np.float32), inv.astype(np.float32), shifts


def lane_ids(rows):
    return lax.broadcasted_iota(jnp.int32, (rows, LANES), 1)


def rim(left, right):
    lane = lane_ids(ROWS)
    both = jnp.where(lane < 8, right, jnp.where(lane >= LANES - 8, left, 0.0))
    moved = pltpu.roll(both, 8, 1, stride=16, stride_axis=0)
    return jnp.sum(moved, axis=0, keepdims=True)


def pack_kernel(t_ref, it_ref, ini_ref, dif_ref, cx_ref, cy_ref, send_ref):
    t = t_ref[0]
    which, share = t % 4, t // 4
    coef = jnp.where(which < 2, jnp.where(which == 0, ini_ref[...], dif_ref[...]), jnp.where(which == 2, cx_ref[...], cy_ref[...]))
    turned = pltpu.roll(coef, (ROWS - 2 * share) % ROWS, 0)
    zero = jnp.zeros((ROWS, LANES), F32)

    def sides(cols, d):
        return rim(cols(d - 1) if d else zero, cols(d + 1) if d + 1 < DEVS else zero)

    for d in range(DEVS):
        rims = []
        for n in range(LOCAL):
            cols = lambda e: it_ref[n, :, e * LANES : (e + 1) * LANES]
            send_ref[d, n * ROWS : (n + 1) * ROWS, :] = cols(d)
            rims.append(sides(cols, d))
        rims.append(turned[:2, d * LANES : (d + 1) * LANES])
        rims.append(sides(lambda e: coef[:, e * LANES : (e + 1) * LANES], d))
        rims.append(jnp.zeros((1, LANES), F32))
        send_ref[d, LOCAL * ROWS :, :] = jnp.concatenate(rims, 0)


def mul(matrix, value):
    return jnp.dot(matrix, value, precision=lax.Precision.HIGHEST, preferred_element_type=F32)


def row(refs, j):
    return refs[j // ROWS].at[j % ROWS]


def build(ref, x_ref, wt_ref, rim_ref, coef_ref):
    lane = lane_ids(1)
    inside = (lane < 8) | (lane >= LANES - 8)
    for d in range(DEVS):
        base = d * BLOCK + LOCAL * ROWS
        rim_ref[d * LOCAL : (d + 1) * LOCAL, :] = ref[base : base + LOCAL, :]
        share = 2 * (d // 4)
        coef_ref[d % 4, share : share + 2, :LANES] = ref[base + LOCAL : base + LOCAL + 2, :]
        if d < 4:
            rim_ref[STEPS + d : STEPS + d + 1, :] = ref[base + LOCAL + 2 : base + LOCAL + 3, :]
    rims = rim_ref[...]
    for r in range(ROWS):
        for d in range(DEVS):
            x_ref[r, 8 + d * LOCAL : 8 + (d + 1) * LOCAL, :LANES] = ref[pl.ds(d * BLOCK + r, LOCAL, stride=ROWS), :]
        turned = jnp.where(inside, pltpu.roll(rims, (2 * LANES - 16 * r - 8) % LANES, 1), 0.0)
        x_ref[r, 8:, LANES:] = turned[:STEPS]
        for a in range(4):
            coef_ref[a, r : r + 1, LANES:] = turned[STEPS + a : STEPS + a + 1]
        x_ref[r, 7:8, :] = coef_ref[0, r : r + 1, :]
    dif, cx, cy = coef_ref[1], coef_ref[2], coef_ref[3]
    west = dif + jnp.maximum(cx, 0.0)
    east = dif + jnp.maximum(-cx, 0.0)
    north = dif + jnp.maximum(cy, 0.0)
    south = dif + jnp.maximum(-cy, 0.0)
    for a, value in enumerate((west, east, north, south, west + east + north + south)):
        wt_ref[a] = value


def diagonal(shift_ref, wt_ref, a_ref, alt_ref, b_ref, r):
    centre = wt_ref[4, r : r + 1, :]
    for g in range(HALF // 8):
        part = slice(8 * g, 8 * g + 8)
        rep = lambda c: jnp.concatenate([shift_ref[part, c * LANES : (c + 1) * LANES]] * 2, 1)
        s_im = rep(1)
        d_re = rep(0) + centre
        norm = 1.0 / (d_re * d_re + s_im * s_im)
        a_ref[r, part, :] = d_re * norm
        b_ref[r, part, :] = s_im * norm
        if g == 0:
            d_im = rep(2) + centre
            alt_ref[r] = d_im * (1.0 / (d_im * d_im + s_im * s_im))


def near(wts, here, above, below):
    width = here.shape[1]
    summed = wts[0] * pltpu.roll(here, 1, 1) + wts[1] * pltpu.roll(here, width - 1, 1)
    return summed + wts[2] * above + wts[3] * below


class Grid:
    def __init__(self, x, wt, a, alt, b):
        self.x, self.wt, self.a, self.alt, self.b = x, wt, a, alt, b

    def weights(self, j):
        ref, r = self.wt[j // ROWS], j % ROWS
        return [ref[a, r : r + 1, :] for a in range(5)]

    def divide(self, j, g, q_re, q_im):
        part = slice(8 * g, 8 * g + 8)
        cols = slice(0, q_re.shape[1])
        a_re, b = row(self.a, j)[part, cols], row(self.b, j)[part, cols]
        a_im = row(self.alt, j)[:, cols] if g == 0 else a_re
        return q_re * a_re + q_im * b, q_im * a_im - q_re * b

    def first(self, fwd_ref, j, dst):
        wts = self.weights(j)
        here = row(self.x, j)[8:, :]
        r = row(self.x, j)[7 : 7 + STEPS, :] - here
        r = r + near(wts, here, row(self.x, j - 1)[8:, :], row(self.x, j + 1)[8:, :]) - wts[4] * here
        hat = mul(fwd_ref[...], r)
        for g in range(HALF // 8):
            p_re, p_im = parts(g)
            dst[p_re, :], dst[p_im, :] = self.divide(j, g, hat[p_re], hat[p_im])

    def sweep(self, j, level, last):
        m, width = last, LANES if last == SWEEPS else WIDE
        wts = self.weights(j)
        here, above, below = level(m - 1, j), level(m - 1, j - 1), level(m - 1, j + 1)
        base, dst = level(1, j), level(m, j)
        for g in range(HALF // 8):
            sums = [near(wts, here[p, :], above[p, :], below[p, :])[:, :width] for p in parts(g)]
            for p, value in zip(parts(g), self.divide(j, g, *sums)):
                dst[p, :width] = base[p, :width] + value


def parts(g):
    return slice(8 * g, 8 * g + 8), slice(HALF + 8 * g, HALF + 8 * g + 8)


def own_kernel(fwd_ref, shift_ref, own_ref, x_ref, wt_ref, a_ref, alt_ref, b_ref, f_ref, rim_ref, coef_ref):
    build(own_ref, x_ref, wt_ref, rim_ref, coef_ref)
    grid = Grid(*[(None, ref, None) for ref in (x_ref, wt_ref, a_ref, alt_ref, b_ref)])
    for r in range(ROWS):
        diagonal(shift_ref, wt_ref, a_ref, alt_ref, b_ref, r)
    for r in range(1, ROWS - 1):
        grid.first(fwd_ref, ROWS + r, f_ref.at[r])


def below_kernel(
    fwd_ref, shift_ref, dn_ref, x1, wt1, a1, alt1, b1, f1,
    f15_ref, edge_ref, x_ref, wt_ref, a_ref, alt_ref, b_ref, f_ref, w_ref, rim_ref, coef_ref,
):
    build(dn_ref, x_ref, wt_ref, rim_ref, coef_ref)
    grid = Grid((None, x1, x_ref), (None, wt1, wt_ref), (None, a1, a_ref), (None, alt1, alt_ref), (None, b1, b_ref))
    for r in range(ROWS - 1):
        diagonal(shift_ref, wt_ref, a_ref, alt_ref, b_ref, r)

    def level(m, j):
        if m == 1:
            return f1.at[j - 8] if j < 15 else f15_ref if j == 15 else f_ref.at[j - 16]
        return edge_ref.at[m - 2, j - 8 - m] if j <= 9 + m else w_ref.at[m % 2, j - 8]

    for j in range(15, SPAN - 1):
        grid.first(fwd_ref, j, level(1, j))
    for m in range(2, SWEEPS):
        for j in range(8 + m, SPAN - m):
            grid.sweep(j, level, m)


def last_kernel(
    fwd_ref, inv_ref, shift_ref, up_ref, x1, wt1, a1, alt1, b1, f1, f15_ref, edge_ref,
    out_ref, x_ref, wt_ref, a_ref, alt_ref, b_ref, f_ref, w_ref, rim_ref, coef_ref,
):
    build(up_ref, x_ref, wt_ref, rim_ref, coef_ref)
    grid = Grid((x_ref, x1), (wt_ref, wt1), (a_ref, a1), (alt_ref, alt1), (b_ref, b1))
    for r in range(1, ROWS):
        diagonal(shift_ref, wt_ref, a_ref, alt_ref, b_ref, r)

    def level(m, j):
        if m == 1:
            return f_ref.at[j] if j <= 8 else f1.at[j - 8] if j < 15 else f15_ref
        return w_ref.at[m % 2, j] if j <= 7 + m else edge_ref.at[m - 2, j - 8 - m]

    for j in range(1, ROWS + 1):
        grid.first(fwd_ref, j, level(1, j))
    for m in range(2, SWEEPS + 1):
        for j in range(m, 8 + m):
            grid.sweep(j, level, m)

    for r in range(0, ROWS, 2):
        j = ROWS + r
        pair = jnp.concatenate([level(SWEEPS, j)[:, :LANES], level(SWEEPS, j + 1)[:, :LANES]], 1)
        corr = mul(inv_ref[...], pair)
        out_ref[pl.ds(r, STEPS, stride=ROWS), :] = x1[r, 8:, :LANES] + corr[:, :LANES]
        out_ref[pl.ds(r + 1, STEPS, stride=ROWS), :] = x1[r + 1, 8:, :LANES] + corr[:, LANES:]


def place_kernel(in_ref, out_ref):
    for d in range(DEVS):
        for n in range(LOCAL):
            out_ref[n, :, d * LANES : (d + 1) * LANES] = in_ref[d, n * ROWS : (n + 1) * ROWS, :]


def vmem(count):
    return [pl.BlockSpec(memory_space=pltpu.VMEM)] * count


def pack(t, iterate, initial, diffusion, courant_x, courant_y):
    return pl.pallas_call(
        pack_kernel,
        name="pack",
        out_shape=jax.ShapeDtypeStruct((DEVS, BLOCK, LANES), F32),
        in_specs=[pl.BlockSpec(memory_space=pltpu.SMEM)] + vmem(5),
        out_specs=vmem(1)[0],
    )(t, iterate, initial, diffusion, courant_x, courant_y)


BLOCKS = {
    "x": (ROWS, STEPS + 8, WIDE),
    "wt": (5, ROWS, WIDE),
    "a": (ROWS, HALF, WIDE),
    "alt": (ROWS, 8, WIDE),
    "b": (ROWS, HALF, WIDE),
}
FIELDS = (ROWS, STEPS, WIDE)
PAIRS = (SWEEPS - 2, 2, STEPS, WIDE)
EXTRA = [pltpu.VMEM((STEPS + 8, LANES), F32), pltpu.VMEM((4, ROWS, WIDE), F32)]


def call(kernel, name, flops, operands, shapes, scratch):
    return pl.pallas_call(
        kernel,
        name=name,
        out_shape=tuple(jax.ShapeDtypeStruct(shape, F32) for shape in shapes),
        in_specs=vmem(len(operands)),
        out_specs=tuple(vmem(len(shapes))),
        scratch_shapes=[pltpu.VMEM(shape, F32) for shape in scratch] + EXTRA,
        compiler_params=pltpu.CompilerParams(vmem_limit_bytes=24 * 1024 * 1024),
        cost_estimate=pl.CostEstimate(flops=flops, bytes_accessed=2**20, transcendentals=0),
    )(*operands)


def solve(up, own, down):
    fwd, inv, shifts = [jnp.asarray(table) for table in tables()]
    block = list(BLOCKS.values())
    mine = call(own_kernel, "own", 10**7, (fwd, shifts, own), block + [FIELDS], [])
    low = call(below_kernel, "below", 2 * 10**7, (fwd, shifts, down) + tuple(mine), [(STEPS, WIDE), PAIRS], block + [FIELDS, (2, 2 * ROWS, STEPS, WIDE)])
    args = (fwd, inv, shifts, up) + tuple(mine) + tuple(low)
    return call(last_kernel, "last", 3 * 10**7, args, [(STEPS * ROWS, LANES)], block + [(ROWS + 1, STEPS, WIDE), (2, 2 * ROWS, STEPS, WIDE)])[0]


def place(received):
    return pl.pallas_call(
        place_kernel,
        name="place",
        out_shape=jax.ShapeDtypeStruct((LOCAL, ROWS, DEVS * LANES), F32),
        in_specs=vmem(1),
        out_specs=vmem(1)[0],
    )(received)


def local(iterate, initial, diffusion, courant_x, courant_y):
    t = lax.axis_index("tm").astype(jnp.int32).reshape(1)
    send = pack(t, iterate, initial, diffusion, courant_x, courant_y)
    count = lax.axis_size("space")
    down = [(i, i + 1) for i in range(count - 1)]
    up = [(i + 1, i) for i in range(count - 1)]
    own = lax.all_to_all(send, "tm", split_axis=0, concat_axis=0, tiled=True)
    own = own.reshape(DEVS * BLOCK, LANES)
    above = lax.ppermute(own, "space", down)
    below = lax.ppermute(own, "space", up)
    new = solve(above, own, below)
    back = lax.all_to_all(new.reshape(DEVS, LOCAL * ROWS, LANES), "tm", split_axis=0, concat_axis=0, tiled=True)
    return place(back)


def solution(mesh):
    return jax.shard_map(
        local,
        mesh=mesh,
        in_specs=(
            P("tm", "space", None),
            P("space", None),
            P("space", None),
            P("space", None),
            P("space", None),
        ),
        out_specs=P("tm", "space", None),
        check_vma=False,
    )
```

time: 64.8 us -> 62 us (0.957)
  waiting for transfers between devices: 12.8 us -> 9.44 us
    ppermute x1, waiting for transfers between devices: 6.86 us -> 4.36 us  [local(): above = lax.ppermute(own, 'space', down)]
    ppermute x1, waiting for transfers between devices: 5.98 us -> 5.07 us  [local(): below = lax.ppermute(own, 'space', up)]
    pallas_call x1 -> x3, Pallas kernels: 6.11 us -> 6.61 us  [call(): pl.pallas_call(kernel, name=name, out_shape=tuple((jax.ShapeDtypeStruct(s...]
  transfers between devices with their start and end apart: 2 -> 2, of which waited for: 2 -> 2; matrix products, arithmetic and copies ran while one was open for 0% -> 0% of each run, Pallas kernels for 0% -> 5%
where the time goes in v3:
time: 62 us; the launch traced here: 61.6 us
  blocking collectives  36.5 us (59%)
  Pallas kernels  10.2 us (16%)
  waiting for transfers between devices  9.44 us (15%)
  starting transfers between devices  5.39 us (9%)
    all_to_all x1, blocking collectives, local(): own = lax.all_to_all(send, 'tm', split_axis=0, concat_axis=0, tiled=True)  21 us
    all_to_all x1, blocking collectives, local(): lax.all_to_all(new.reshape(DEVS, LOCAL * ROWS, LANES), 'tm', split_axis=0...  15.5 us
    pallas_call x3, Pallas kernels, call(): pl.pallas_call(kernel, name=name, out_shape=tuple((jax.ShapeDtypeStruct(s...  6.61 us
    ppermute x1, waiting for transfers between devices, local(): below = lax.ppermute(own, 'space', up)  5.07 us
    ppermute x1, waiting for transfers between devices, local(): above = lax.ppermute(own, 'space', down)  4.36 us
    ppermute x1, starting transfers between devices, local(): below = lax.ppermute(own, 'space', up)  3.47 us
    pallas_call x1, Pallas kernels, pack(): pl.pallas_call(pack_kernel, name='pack', out_shape=jax.ShapeDtypeStruct((...  1.93 us
    ppermute x1, starting transfers between devices, local(): above = lax.ppermute(own, 'space', down)  1.92 us
  transfers between devices with their start and end apart: 2, of which 2 were waited for; matrix products, arithmetic and copies ran while one was open for 0% of the time, Pallas kernels for 5%

profile of v3, /device:TPU:257, one launch (start us, length us, event | category | flops | bytes accessed | tf_op | source)
XLA Modules:
  0.0 61.6 jit_solution(1348073653440223485)
XLA Ops:
  0.0 1.9 %pack.1 = f32[16,40,128]{2,1,0:T(8,128)} custom-call(s32[1]{0:T(128)} %bitcast.t_ref, f32[4,8,2048]{2,1,0:T(8,128)} %it_ref.1, f32[8,2048]{1,0:T(8,128)} %ini_ref.1, f32[8,2048]{1,0:T(8,128)} %dif_ref.1, f32[8,2048]{1,0:T(8,128)} %cx_ref.1, f32[8,2048]{1,0:T(8,128)} %cy_ref.1), custom_call_target="tpu_custom_call" | custom-call | tf_op jit(solution)/shard_map/pack/pallas_call | solution.py:247
  1.9 0.0 copy-start
  1.9 0.0 copy-start.1
  1.9 21.0 %all_to_all.10 = f32[16,40,128]{2,1,0:T(8,128)S(1)} all-to-all(f32[16,40,128]{2,1,0:T(8,128)} %pack.1), channel_id=1, replica_groups=mesh['tm'=16,'space'=32] {'tm'}, dimensions={0} | all-to-all | bytes 655360 | tf_op jit(solution)/shard_map/all_to_all | solution.py:306
  22.9 3.5 %collective-permute-start.1 = (f32[640,128]{1,0:T(8,128)S(1)}, f32[640,128]{1,0:T(8,128)S(1)}, u32[]{:S(2)}, u32[]{:S(2)}) collective-permute-start(f32[640,128]{1,0:T(8,128)S(1)} %bitcast.3), channel_id=1, source_target_pairs={{1,0},{2,1},{3,2},{4,3},{5,4},{6,5},{7,6},{8,7},{9,8},{10,9},{11,1... | collective-permute-start | bytes 983048 | tf_op jit(solution)/shard_map/ppermute | solution.py:309
  26.4 1.9 %collective-permute-start = (f32[640,128]{1,0:T(8,128)S(1)}, f32[640,128]{1,0:T(8,128)S(1)}, u32[]{:S(2)}, u32[]{:S(2)}) collective-permute-start(f32[640,128]{1,0:T(8,128)S(1)} %bitcast.4), channel_id=1, source_target_pairs={{0,1},{1,2},{2,3},{3,4},{4,5},{5,6},{6,7},{7,8},{8,9},{9,10},{10,1... | collective-permute-start | bytes 983048 | tf_op jit(solution)/shard_map/ppermute | solution.py:308
  28.3 0.0 copy-done
  28.3 0.0 copy-done.1
  28.3 0.9 %own.1 = (f32[8,72,256]{2,1,0:T(8,128)S(1)}, f32[5,8,256]{2,1,0:T(8,128)S(1)}, f32[8,32,256]{2,1,0:T(8,128)S(1)}, f32[8,8,256]{2,1,0:T(8,128)S(1)}, f32[8,32,256...) custom-call(f32[64,64]{1,0:T(8,128)S(1)} %copy-done.1, f32[32,384]{1,0:T(8,128)S(1)} %copy-done, f32[640,128]{1,0:T(8,128)S(1)} %bitcast.5), custom_call_target="tpu_custom_call" | custom-call | flops 10000000 | bytes 1048576 | tf_op jit(solution)/shard_map/own/pallas_call | solution.py:269
  29.2 5.1 %collective-permute-done.1.dn_ref = f32[640,128]{1,0:T(8,128)S(1)} collective-permute-done((f32[640,128]{1,0:T(8,128)S(1)}, f32[640,128]{1,0:T(8,128)S(1)}, u32[]{:S(2)}, u32[]{:S(2)}) %collective-permute-start.1) | collective-permute-done | bytes 327712 | tf_op jit(solution)/shard_map/ppermute | solution.py:309
  34.3 0.0 copy-start.2
  34.3 2.5 %below.1 = (f32[64,256]{1,0:T(8,128)S(1)}, f32[6,2,64,256]{3,2,1,0:T(8,128)S(1)}) custom-call(f32[64,64]{1,0:T(8,128)S(1)} %copy-done.1, f32[32,384]{1,0:T(8,128)S(1)} %copy-done, f32[640,128]{1,0:T(8,128)S(1)} %collective-permute-done.1.dn_ref, f32[8,72,256]{2,1,0:T(8,128)S(1)} %get-tuple-element.13.x1, f32[5,8,256]{2,1,0:T(8,128)S(1)} %get-tuple-element.14.wt1, ...), custom_call_target="tpu_custom_call" | custom-call | flops 20000000 | bytes 1048576 | tf_op jit(solution)/shard_map/below/pallas_call | solution.py:269
  36.8 4.4 %collective-permute-done.up_ref = f32[640,128]{1,0:T(8,128)S(1)} collective-permute-done((f32[640,128]{1,0:T(8,128)S(1)}, f32[640,128]{1,0:T(8,128)S(1)}, u32[]{:S(2)}, u32[]{:S(2)}) %collective-permute-start) | collective-permute-done | bytes 327712 | tf_op jit(solution)/shard_map/ppermute | solution.py:308
  41.2 0.0 copy-done.2
  41.2 3.2 %last.1 = f32[512,128]{1,0:T(8,128)S(1)} custom-call(f32[64,64]{1,0:T(8,128)S(1)} %copy-done.1, f32[64,64]{1,0:T(8,128)S(1)} %copy-done.2, f32[32,384]{1,0:T(8,128)S(1)} %copy-done, f32[640,128]{1,0:T(8,128)S(1)} %collective-permute-done.up_ref, f32[8,72,256]{2,1,0:T(8,128)S(1)} %get-tuple-element.13.x1, f32[5,8,256]{2,1,0:T(8,128)S(1)} %get-tuple-element.14.wt1, ...), custom_call_target="tpu_custom_call" | custom-call | flops 30000000 | bytes 1048576 | tf_op jit(solution)/shard_map/last/pallas_call | solution.py:269
  44.4 15.5 %all_to_all.11.in_ref = f32[16,32,128]{2,1,0:T(8,128)} all-to-all(f32[16,32,128]{2,1,0:T(8,128)S(1)} %bitcast.6), channel_id=1, replica_groups=mesh['tm'=16,'space'=32] {'tm'}, dimensions={0} | all-to-all | bytes 524288 | tf_op jit(solution)/shard_map/all_to_all | solution.py:311
  59.9 1.7 %place.1 = f32[4,8,2048]{2,1,0:T(8,128)} custom-call(f32[16,32,128]{2,1,0:T(8,128)} %all_to_all.11.in_ref), custom_call_target="tpu_custom_call" | custom-call | tf_op jit(solution)/shard_map/place/pallas_call | solution.py:291
Async XLA Ops:
  1.9 26.4 %copy-start = (f32[32,384]{1,0:T(8,128)S(1)}, f32[32,384]{1,0:T(8,128)}, u32[]{:S(2)}) copy-start(f32[32,384]{1,0:T(8,128)} %constant.14.clone.shift_ref) | copy-start | bytes 147460
  1.9 26.4 %copy-start.1 = (f32[64,64]{1,0:T(8,128)S(1)}, f32[64,64]{1,0:T(8,128)}, u32[]{:S(2)}) copy-start(f32[64,64]{1,0:T(8,128)} %constant.12.clone.fwd_ref) | copy-start | bytes 49156
  22.9 11.4 %collective-permute-start.1 = (f32[640,128]{1,0:T(8,128)S(1)}, f32[640,128]{1,0:T(8,128)S(1)}, u32[]{:S(2)}, u32[]{:S(2)}) collective-permute-start(f32[640,128]{1,0:T(8,128)S(1)} %bitcast.3), channel_id=1, source_target_pairs={{1,0},{2,1},{3,2},{4,3},{5,4},{6,5},{7,6},{8,7},{9,8},{10,9},{11,1... | collective-permute-start | bytes 983048 | tf_op jit(solution)/shard_map/ppermute | solution.py:309
  26.4 14.8 %collective-permute-start = (f32[640,128]{1,0:T(8,128)S(1)}, f32[640,128]{1,0:T(8,128)S(1)}, u32[]{:S(2)}, u32[]{:S(2)}) collective-permute-start(f32[640,128]{1,0:T(8,128)S(1)} %bitcast.4), channel_id=1, source_target_pairs={{0,1},{1,2},{2,3},{3,4},{4,5},{5,6},{6,7},{7,8},{8,9},{9,10},{10,1... | collective-permute-start | bytes 983048 | tf_op jit(solution)/shard_map/ppermute | solution.py:308
  34.3 6.9 %copy-start.2 = (f32[64,64]{1,0:T(8,128)S(1)}, f32[64,64]{1,0:T(8,128)}, u32[]{:S(2)}) copy-start(f32[64,64]{1,0:T(8,128)} %constant.13.clone.inv_ref) | copy-start | bytes 49156

commit v4 on v3

--- a/solution.py
+++ b/solution.py
@@ -86,9 +86,11 @@
     return refs[j // ROWS].at[j % ROWS]
 
 
-def build(ref, x_ref, wt_ref, rim_ref, coef_ref):
-    lane = lane_ids(1)
-    inside = (lane < 8) | (lane >= LANES - 8)
+def build(ref, x_ref, wt_ref, rim_ref, coef_ref, main_ref=None):
+    def tiles(main, turned):
+        lane = lane_ids(main.shape[0])
+        return jnp.where(lane >= LANES - 8, turned, main), jnp.where(lane < 8, turned, main)
+
     for d in range(DEVS):
         base = d * BLOCK + LOCAL * ROWS
         rim_ref[d * LOCAL : (d + 1) * LOCAL, :] = ref[base : base + LOCAL, :]
@@ -100,10 +102,14 @@
     for r in range(ROWS):
         for d in range(DEVS):
             x_ref[r, 8 + d * LOCAL : 8 + (d + 1) * LOCAL, :LANES] = ref[pl.ds(d * BLOCK + r, LOCAL, stride=ROWS), :]
-        turned = jnp.where(inside, pltpu.roll(rims, (2 * LANES - 16 * r - 8) % LANES, 1), 0.0)
-        x_ref[r, 8:, LANES:] = turned[:STEPS]
+        turned = pltpu.roll(rims, (2 * LANES - 16 * r - 8) % LANES, 1)
+        main = x_ref[r, 8:, :LANES]
+        if main_ref is not None:
+            main_ref[r] = main
+        x_ref[r, 8:, :LANES], x_ref[r, 8:, LANES:] = tiles(main, turned[:STEPS])
         for a in range(4):
-            coef_ref[a, r : r + 1, LANES:] = turned[STEPS + a : STEPS + a + 1]
+            one = slice(r, r + 1)
+            coef_ref[a, one, :LANES], coef_ref[a, one, LANES:] = tiles(coef_ref[a, one, :LANES], turned[STEPS + a : STEPS + a + 1])
         x_ref[r, 7:8, :] = coef_ref[0, r : r + 1, :]
     dif, cx, cy = coef_ref[1], coef_ref[2], coef_ref[3]
     west = dif + jnp.maximum(cx, 0.0)
@@ -130,8 +136,10 @@
 
 
 def near(wts, here, above, below):
-    width = here.shape[1]
-    summed = wts[0] * pltpu.roll(here, 1, 1) + wts[1] * pltpu.roll(here, width - 1, 1)
+    west, east = [
+        jnp.concatenate([pltpu.roll(here[:, :LANES], by, 1), pltpu.roll(here[:, LANES:], by, 1)], 1) for by in (1, LANES - 1)
+    ]
+    summed = wts[0] * west + wts[1] * east
     return summed + wts[2] * above + wts[3] * below
 
 
@@ -145,9 +153,8 @@
 
     def divide(self, j, g, q_re, q_im):
         part = slice(8 * g, 8 * g + 8)
-        cols = slice(0, q_re.shape[1])
-        a_re, b = row(self.a, j)[part, cols], row(self.b, j)[part, cols]
-        a_im = row(self.alt, j)[:, cols] if g == 0 else a_re
+        a_re, b = row(self.a, j)[part, :], row(self.b, j)[part, :]
+        a_im = row(self.alt, j)[...] if g == 0 else a_re
         return q_re * a_re + q_im * b, q_im * a_im - q_re * b
 
     def first(self, fwd_ref, j, dst):
@@ -160,23 +167,29 @@
             p_re, p_im = parts(g)
             dst[p_re, :], dst[p_im, :] = self.divide(j, g, hat[p_re], hat[p_im])
 
-    def sweep(self, j, level, last):
-        m, width = last, LANES if last == SWEEPS else WIDE
+    def sweep(self, j, level, m):
+        values = {}
         wts = self.weights(j)
         here, above, below = level(m - 1, j), level(m - 1, j - 1), level(m - 1, j + 1)
-        base, dst = level(1, j), level(m, j)
+        base = level(1, j)
         for g in range(HALF // 8):
-            sums = [near(wts, here[p, :], above[p, :], below[p, :])[:, :width] for p in parts(g)]
+            sums = [near(wts, here[p, :], above[p, :], below[p, :]) for p in parts(g)]
             for p, value in zip(parts(g), self.divide(j, g, *sums)):
-                dst[p, :width] = base[p, :width] + value
+                values[p.start] = base[p, :] + value
+        return values
+
+    def store(self, j, level, m):
+        dst = level(m, j)
+        for start, value in self.sweep(j, level, m).items():
+            dst[start : start + 8, :] = value
 
 
 def parts(g):
     return slice(8 * g, 8 * g + 8), slice(HALF + 8 * g, HALF + 8 * g + 8)
 
 
-def own_kernel(fwd_ref, shift_ref, own_ref, x_ref, wt_ref, a_ref, alt_ref, b_ref, f_ref, rim_ref, coef_ref):
-    build(own_ref, x_ref, wt_ref, rim_ref, coef_ref)
+def own_kernel(fwd_ref, shift_ref, own_ref, main_ref, x_ref, wt_ref, a_ref, alt_ref, b_ref, f_ref, rim_ref, coef_ref):
+    build(own_ref, x_ref, wt_ref, rim_ref, coef_ref, main_ref)
     grid = Grid(*[(None, ref, None) for ref in (x_ref, wt_ref, a_ref, alt_ref, b_ref)])
     for r in range(ROWS):
         diagonal(shift_ref, wt_ref, a_ref, alt_ref, b_ref, r)
@@ -202,11 +215,11 @@
         grid.first(fwd_ref, j, level(1, j))
     for m in range(2, SWEEPS):
         for j in range(8 + m, SPAN - m):
-            grid.sweep(j, level, m)
+            grid.store(j, level, m)
 
 
 def last_kernel(
-    fwd_ref, inv_ref, shift_ref, up_ref, x1, wt1, a1, alt1, b1, f1, f15_ref, edge_ref,
+    fwd_ref, inv_ref, shift_ref, up_ref, main_ref, x1, wt1, a1, alt1, b1, f1, f15_ref, edge_ref,
     out_ref, x_ref, wt_ref, a_ref, alt_ref, b_ref, f_ref, w_ref, rim_ref, coef_ref,
 ):
     build(up_ref, x_ref, wt_ref, rim_ref, coef_ref)
@@ -221,22 +234,19 @@
 
     for j in range(1, ROWS + 1):
         grid.first(fwd_ref, j, level(1, j))
-    for m in range(2, SWEEPS + 1):
+    for m in range(2, SWEEPS):
         for j in range(m, 8 + m):
-            grid.sweep(j, level, m)
+            grid.store(j, level, m)
+    left = lane_ids(8) < LANES // 2
+
+    def final(j):
+        values = grid.sweep(j, level, SWEEPS)
+        return jnp.concatenate([jnp.where(left, values[p][:, :LANES], values[p][:, LANES:]) for p in range(0, STEPS, 8)], 0)
 
     for r in range(0, ROWS, 2):
-        j = ROWS + r
-        pair = jnp.concatenate([level(SWEEPS, j)[:, :LANES], level(SWEEPS, j + 1)[:, :LANES]], 1)
-        corr = mul(inv_ref[...], pair)
-        out_ref[pl.ds(r, STEPS, stride=ROWS), :] = x1[r, 8:, :LANES] + corr[:, :LANES]
-        out_ref[pl.ds(r + 1, STEPS, stride=ROWS), :] = x1[r + 1, 8:, :LANES] + corr[:, LANES:]
-
-
-def place_kernel(in_ref, out_ref):
-    for d in range(DEVS):
-        for n in range(LOCAL):
-            out_ref[n, :, d * LANES : (d + 1) * LANES] = in_ref[d, n * ROWS : (n + 1) * ROWS, :]
+        corr = mul(inv_ref[...], jnp.concatenate([final(ROWS + r), final(ROWS + r + 1)], 1))
+        for i in range(2):
+            out_ref[pl.ds(r + i, STEPS, stride=ROWS), :] = main_ref[r + i] + corr[:, i * LANES : (i + 1) * LANES]
 
 
 def vmem(count):
@@ -281,20 +291,14 @@
 def solve(up, own, down):
     fwd, inv, shifts = [jnp.asarray(table) for table in tables()]
     block = list(BLOCKS.values())
-    mine = call(own_kernel, "own", 10**7, (fwd, shifts, own), block + [FIELDS], [])
+    main, *mine = call(own_kernel, "own", 10**7, (fwd, shifts, own), [(ROWS, STEPS, LANES)] + block + [FIELDS], [])
     low = call(below_kernel, "below", 2 * 10**7, (fwd, shifts, down) + tuple(mine), [(STEPS, WIDE), PAIRS], block + [FIELDS, (2, 2 * ROWS, STEPS, WIDE)])
-    args = (fwd, inv, shifts, up) + tuple(mine) + tuple(low)
+    args = (fwd, inv, shifts, up, main) + tuple(mine) + tuple(low)
     return call(last_kernel, "last", 3 * 10**7, args, [(STEPS * ROWS, LANES)], block + [(ROWS + 1, STEPS, WIDE), (2, 2 * ROWS, STEPS, WIDE)])[0]
 
 
 def place(received):
-    return pl.pallas_call(
-        place_kernel,
-        name="place",
-        out_shape=jax.ShapeDtypeStruct((LOCAL, ROWS, DEVS * LANES), F32),
-        in_specs=vmem(1),
-        out_specs=vmem(1)[0],
-    )(received)
+    return received.reshape(DEVS, LOCAL, ROWS, LANES).transpose(1, 2, 0, 3).reshape(LOCAL, ROWS, DEVS * LANES)
 
 
 def local(iterate, initial, diffusion, courant_x, courant_y):

time: 62 us -> 60.3 us (0.973)
  Pallas kernels: 10.2 us -> 8.53 us
  local copies, waits for them, and re-layouts: 0.01 us -> 0.73 us
  blocking collectives: 36.5 us -> 35.8 us
    pallas_call x1 -> x0, Pallas kernels: 1.67 us -> none  [place(): pl.pallas_call(place_kernel, name='place', out_shape=jax.ShapeDtypeStruct...]
    reshape x0 -> x1, local copies, waits for them, and re-layouts: none -> 0.72 us  [place(): received.reshape(DEVS, LOCAL, ROWS, LANES).transpose(1, 2, 0, 3)]
    all_to_all x1, blocking collectives: 15.5 us -> 14.8 us  [local(): lax.all_to_all(new.reshape(DEVS, LOCAL * ROWS, LANES), 'tm', split_axis=0...]
  transfers between devices with their start and end apart: 2 -> 2, of which waited for: 2 -> 2; matrix products, arithmetic and copies ran while one was open for 0% -> 0% of each run, Pallas kernels for 5% -> 6%
where the time goes in v4:
time: 60.3 us; the launch traced here: 60 us
  blocking collectives  35.8 us (59%)
  waiting for transfers between devices  9.49 us (16%)
  Pallas kernels  8.53 us (14%)
  starting transfers between devices  5.39 us (9%)
  local copies, waits for them, and re-layouts  0.73 us (1%)
    all_to_all x1, blocking collectives, local(): own = lax.all_to_all(send, 'tm', split_axis=0, concat_axis=0, tiled=True)  21 us
    all_to_all x1, blocking collectives, local(): lax.all_to_all(new.reshape(DEVS, LOCAL * ROWS, LANES), 'tm', split_axis=0...  14.8 us
    pallas_call x3, Pallas kernels, call(): pl.pallas_call(kernel, name=name, out_shape=tuple((jax.ShapeDtypeStruct(s...  6.6 us
    ppermute x1, waiting for transfers between devices, local(): below = lax.ppermute(own, 'space', up)  5.04 us
    ppermute x1, waiting for transfers between devices, local(): above = lax.ppermute(own, 'space', down)  4.46 us
    ppermute x1, starting transfers between devices, local(): below = lax.ppermute(own, 'space', up)  3.47 us
    pallas_call x1, Pallas kernels, pack(): pl.pallas_call(pack_kernel, name='pack', out_shape=jax.ShapeDtypeStruct((...  1.93 us
    ppermute x1, starting transfers between devices, local(): above = lax.ppermute(own, 'space', down)  1.92 us
  transfers between devices with their start and end apart: 2, of which 2 were waited for; matrix products, arithmetic and copies ran while one was open for 0% of the time, Pallas kernels for 6%

profile of v4, /device:TPU:257, one launch (start us, length us, event | category | flops | bytes accessed | tf_op | source)
XLA Modules:
  0.0 60.0 jit_solution(3238371621952792742)
XLA Ops:
  0.0 1.9 %pack.1 = f32[16,40,128]{2,1,0:T(8,128)} custom-call(s32[1]{0:T(128)} %bitcast.t_ref, f32[4,8,2048]{2,1,0:T(8,128)} %it_ref.1, f32[8,2048]{1,0:T(8,128)} %ini_ref.1, f32[8,2048]{1,0:T(8,128)} %dif_ref.1, f32[8,2048]{1,0:T(8,128)} %cx_ref.1, f32[8,2048]{1,0:T(8,128)} %cy_ref.1), custom_call_target="tpu_custom_call" | custom-call | tf_op jit(solution)/shard_map/pack/pallas_call | solution.py:257
  1.9 0.0 copy-start
  1.9 0.0 copy-start.1
  1.9 21.0 %all_to_all.10 = f32[16,40,128]{2,1,0:T(8,128)S(1)} all-to-all(f32[16,40,128]{2,1,0:T(8,128)} %pack.1), channel_id=1, replica_groups=mesh['tm'=16,'space'=32] {'tm'}, dimensions={0} | all-to-all | bytes 655360 | tf_op jit(solution)/shard_map/all_to_all | solution.py:310
  22.9 3.5 %collective-permute-start.1 = (f32[640,128]{1,0:T(8,128)S(1)}, f32[640,128]{1,0:T(8,128)S(1)}, u32[]{:S(2)}, u32[]{:S(2)}) collective-permute-start(f32[640,128]{1,0:T(8,128)S(1)} %bitcast.10), channel_id=1, source_target_pairs={{1,0},{2,1},{3,2},{4,3},{5,4},{6,5},{7,6},{8,7},{9,8},{10,9},{11,1... | collective-permute-start | bytes 983048 | tf_op jit(solution)/shard_map/ppermute | solution.py:313
  26.4 1.9 %collective-permute-start = (f32[640,128]{1,0:T(8,128)S(1)}, f32[640,128]{1,0:T(8,128)S(1)}, u32[]{:S(2)}, u32[]{:S(2)}) collective-permute-start(f32[640,128]{1,0:T(8,128)S(1)} %bitcast.11), channel_id=1, source_target_pairs={{0,1},{1,2},{2,3},{3,4},{4,5},{5,6},{6,7},{7,8},{8,9},{9,10},{10,1... | collective-permute-start | bytes 983048 | tf_op jit(solution)/shard_map/ppermute | solution.py:312
  28.3 0.0 copy-done
  28.3 0.0 copy-done.1
  28.3 0.9 %own.1 = (f32[8,64,128]{2,1,0:T(8,128)S(1)}, f32[8,72,256]{2,1,0:T(8,128)S(1)}, f32[5,8,256]{2,1,0:T(8,128)S(1)}, f32[8,32,256]{2,1,0:T(8,128)S(1)}, f32[8,8,256...) custom-call(f32[64,64]{1,0:T(8,128)S(1)} %copy-done.1, f32[32,384]{1,0:T(8,128)S(1)} %copy-done, ...), custom_call_target="tpu_custom_call" | custom-call | flops 10000000 | bytes 1048576 | tf_op jit(solution)/shard_map/own/pallas_call | solution.py:279
  29.3 5.0 %collective-permute-done.1.dn_ref = f32[640,128]{1,0:T(8,128)S(1)} collective-permute-done((f32[640,128]{1,0:T(8,128)S(1)}, f32[640,128]{1,0:T(8,128)S(1)}, u32[]{:S(2)}, u32[]{:S(2)}) %collective-permute-start.1) | collective-permute-done | bytes 327712 | tf_op jit(solution)/shard_map/ppermute | solution.py:313
  34.3 0.0 copy-start.2
  34.3 2.4 %below.1 = (f32[64,256]{1,0:T(8,128)S(1)}, f32[6,2,64,256]{3,2,1,0:T(8,128)S(1)}) custom-call(f32[64,64]{1,0:T(8,128)S(1)} %copy-done.1, f32[32,384]{1,0:T(8,128)S(1)} %copy-done, f32[640,128]{1,0:T(8,128)S(1)} %collective-permute-done.1.dn_ref, f32[8,72,256]{2,1,0:T(8,128)S(1)} %get-tuple-element.15.x1, f32[5,8,256]{2,1,0:T(8,128)S(1)} %get-tuple-element.16.wt1, ...), custom_call_target="tpu_custom_call" | custom-call | flops 20000000 | bytes 1048576 | tf_op jit(solution)/shard_map/below/pallas_call | solution.py:279
  36.7 4.5 %collective-permute-done.up_ref = f32[640,128]{1,0:T(8,128)S(1)} collective-permute-done((f32[640,128]{1,0:T(8,128)S(1)}, f32[640,128]{1,0:T(8,128)S(1)}, u32[]{:S(2)}, u32[]{:S(2)}) %collective-permute-start) | collective-permute-done | bytes 327712 | tf_op jit(solution)/shard_map/ppermute | solution.py:312
  41.2 0.0 copy-done.2
  41.2 3.3 %last.1 = f32[512,128]{1,0:T(8,128)S(1)} custom-call(f32[64,64]{1,0:T(8,128)S(1)} %copy-done.1, f32[64,64]{1,0:T(8,128)S(1)} %copy-done.2, f32[32,384]{1,0:T(8,128)S(1)} %copy-done, f32[640,128]{1,0:T(8,128)S(1)} %collective-permute-done.up_ref, f32[8,64,128]{2,1,0:T(8,128)S(1)} %get-tuple-element.14.main_ref, f32[8,72,256]{2,1,0:T(8,128)S(1)} %get-tuple-element.15.x1, ...), custom_call_target="tpu_custom_call" | custom-call | flops 30000000 | bytes 1048576 | tf_op jit(solution)/shard_map/last/pallas_call | solution.py:279
  44.5 14.8 %all_to_all.11 = f32[16,32,128]{2,1,0:T(8,128)S(1)} all-to-all(f32[16,32,128]{2,1,0:T(8,128)S(1)} %bitcast.13), channel_id=1, replica_groups=mesh['tm'=16,'space'=32] {'tm'}, dimensions={0} | all-to-all | bytes 524288 | tf_op jit(solution)/shard_map/all_to_all | solution.py:315
  59.3 0.7 %copy_bitcast_fusion = f32[4,8,2048]{2,1,0:T(8,128)} fusion(f32[16,32,128]{2,1,0:T(8,128)S(1)} %all_to_all.11), kind=kLoop, calls=%fused_computation | loop fusion | bytes 524288 | tf_op jit(solution)/shard_map/reshape | solution.py:301
Async XLA Ops:
  1.9 26.4 %copy-start = (f32[32,384]{1,0:T(8,128)S(1)}, f32[32,384]{1,0:T(8,128)}, u32[]{:S(2)}) copy-start(f32[32,384]{1,0:T(8,128)} %constant.14.clone.shift_ref) | copy-start | bytes 147460
  1.9 26.4 %copy-start.1 = (f32[64,64]{1,0:T(8,128)S(1)}, f32[64,64]{1,0:T(8,128)}, u32[]{:S(2)}) copy-start(f32[64,64]{1,0:T(8,128)} %constant.12.clone.fwd_ref) | copy-start | bytes 49156
  22.9 11.4 %collective-permute-start.1 = (f32[640,128]{1,0:T(8,128)S(1)}, f32[640,128]{1,0:T(8,128)S(1)}, u32[]{:S(2)}, u32[]{:S(2)}) collective-permute-start(f32[640,128]{1,0:T(8,128)S(1)} %bitcast.10), channel_id=1, source_target_pairs={{1,0},{2,1},{3,2},{4,3},{5,4},{6,5},{7,6},{8,7},{9,8},{10,9},{11,1... | collective-permute-start | bytes 983048 | tf_op jit(solution)/shard_map/ppermute | solution.py:313
  26.4 14.8 %collective-permute-start = (f32[640,128]{1,0:T(8,128)S(1)}, f32[640,128]{1,0:T(8,128)S(1)}, u32[]{:S(2)}, u32[]{:S(2)}) collective-permute-start(f32[640,128]{1,0:T(8,128)S(1)} %bitcast.11), channel_id=1, source_target_pairs={{0,1},{1,2},{2,3},{3,4},{4,5},{5,6},{6,7},{7,8},{8,9},{9,10},{10,1... | collective-permute-start | bytes 983048 | tf_op jit(solution)/shard_map/ppermute | solution.py:312
  34.3 6.9 %copy-start.2 = (f32[64,64]{1,0:T(8,128)S(1)}, f32[64,64]{1,0:T(8,128)}, u32[]{:S(2)}) copy-start(f32[64,64]{1,0:T(8,128)} %constant.13.clone.inv_ref) | copy-start | bytes 49156

commit v5 on v4

--- a/solution.py
+++ b/solution.py
@@ -257,7 +257,7 @@
     return pl.pallas_call(
         pack_kernel,
         name="pack",
-        out_shape=jax.ShapeDtypeStruct((DEVS, BLOCK, LANES), F32),
+        out_shape=pltpu.VMEM((DEVS, BLOCK, LANES), F32),
         in_specs=[pl.BlockSpec(memory_space=pltpu.SMEM)] + vmem(5),
         out_specs=vmem(1)[0],
     )(t, iterate, initial, diffusion, courant_x, courant_y)

time: 60.3 us -> 59.6 us (0.988)
    pallas_call x1, Pallas kernels: 1.93 us -> 1.2 us  [pack(): pl.pallas_call(pack_kernel, name='pack', out_shape=pltpu.VMEM((DEVS, BLOC...]
where the time goes in v5:
time: 59.6 us; the launch traced here: 59.3 us
  blocking collectives  35.6 us (60%)
  waiting for transfers between devices  9.33 us (16%)
  Pallas kernels  8.19 us (14%)
  starting transfers between devices  5.39 us (9%)
  local copies, waits for them, and re-layouts  0.74 us (1%)
    all_to_all x1, blocking collectives, local(): own = lax.all_to_all(send, 'tm', split_axis=0, concat_axis=0, tiled=True)  20.8 us
    all_to_all x1, blocking collectives, local(): lax.all_to_all(new.reshape(DEVS, LOCAL * ROWS, LANES), 'tm', split_axis=0...  14.8 us
    pallas_call x3, Pallas kernels, call(): pl.pallas_call(kernel, name=name, out_shape=tuple((jax.ShapeDtypeStruct(s...  6.98 us
    ppermute x1, waiting for transfers between devices, local(): below = lax.ppermute(own, 'space', up)  5 us
    ppermute x1, waiting for transfers between devices, local(): above = lax.ppermute(own, 'space', down)  4.33 us
    ppermute x1, starting transfers between devices, local(): below = lax.ppermute(own, 'space', up)  3.47 us
    ppermute x1, starting transfers between devices, local(): above = lax.ppermute(own, 'space', down)  1.92 us
    pallas_call x1, Pallas kernels, pack(): pl.pallas_call(pack_kernel, name='pack', out_shape=pltpu.VMEM((DEVS, BLOC...  1.2 us
  transfers between devices with their start and end apart: 2, of which 2 were waited for; matrix products, arithmetic and copies ran while one was open for 0% of the time, Pallas kernels for 6%

profile of v5, /device:TPU:257, one launch (start us, length us, event | category | flops | bytes accessed | tf_op | source)
XLA Modules:
  0.0 59.3 jit_solution(5195527983633503018)
XLA Ops:
  0.0 1.2 %pack.1 = f32[16,40,128]{2,1,0:T(8,128)S(1)} custom-call(s32[1]{0:T(128)} %bitcast.t_ref, f32[4,8,2048]{2,1,0:T(8,128)} %it_ref.1, f32[8,2048]{1,0:T(8,128)} %ini_ref.1, f32[8,2048]{1,0:T(8,128)} %dif_ref.1, f32[8,2048]{1,0:T(8,128)} %cx_ref.1, f32[8,2048]{1,0:T(8,128)} %cy_ref.1), custom_call_target="tpu_custom_call" | custom-call | tf_op jit(solution)/shard_map/pack/pallas_call | solution.py:257
  1.2 0.0 copy-start
  1.2 0.0 copy-start.1
  1.2 20.8 %all_to_all.10 = f32[16,40,128]{2,1,0:T(8,128)S(1)} all-to-all(f32[16,40,128]{2,1,0:T(8,128)S(1)} %pack.1), channel_id=1, replica_groups=mesh['tm'=16,'space'=32] {'tm'}, dimensions={0} | all-to-all | bytes 655360 | tf_op jit(solution)/shard_map/all_to_all | solution.py:310
  22.0 3.5 %collective-permute-start.1 = (f32[640,128]{1,0:T(8,128)S(1)}, f32[640,128]{1,0:T(8,128)S(1)}, u32[]{:S(2)}, u32[]{:S(2)}) collective-permute-start(f32[640,128]{1,0:T(8,128)S(1)} %bitcast.10), channel_id=1, source_target_pairs={{1,0},{2,1},{3,2},{4,3},{5,4},{6,5},{7,6},{8,7},{9,8},{10,9},{11,1... | collective-permute-start | bytes 983048 | tf_op jit(solution)/shard_map/ppermute | solution.py:313
  25.5 1.9 %collective-permute-start = (f32[640,128]{1,0:T(8,128)S(1)}, f32[640,128]{1,0:T(8,128)S(1)}, u32[]{:S(2)}, u32[]{:S(2)}) collective-permute-start(f32[640,128]{1,0:T(8,128)S(1)} %bitcast.11), channel_id=1, source_target_pairs={{0,1},{1,2},{2,3},{3,4},{4,5},{5,6},{6,7},{7,8},{8,9},{9,10},{10,1... | collective-permute-start | bytes 983048 | tf_op jit(solution)/shard_map/ppermute | solution.py:312
  27.4 0.0 copy-done
  27.4 0.0 copy-done.1
  27.4 1.0 %own.1 = (f32[8,64,128]{2,1,0:T(8,128)S(1)}, f32[8,72,256]{2,1,0:T(8,128)S(1)}, f32[5,8,256]{2,1,0:T(8,128)S(1)}, f32[8,32,256]{2,1,0:T(8,128)S(1)}, f32[8,8,256...) custom-call(f32[64,64]{1,0:T(8,128)S(1)} %copy-done.1, f32[32,384]{1,0:T(8,128)S(1)} %copy-done, ...), custom_call_target="tpu_custom_call" | custom-call | flops 10000000 | bytes 1048576 | tf_op jit(solution)/shard_map/own/pallas_call | solution.py:279
  28.4 5.0 %collective-permute-done.1.dn_ref = f32[640,128]{1,0:T(8,128)S(1)} collective-permute-done((f32[640,128]{1,0:T(8,128)S(1)}, f32[640,128]{1,0:T(8,128)S(1)}, u32[]{:S(2)}, u32[]{:S(2)}) %collective-permute-start.1) | collective-permute-done | bytes 327712 | tf_op jit(solution)/shard_map/ppermute | solution.py:313
  33.4 0.0 copy-start.2
  33.4 2.5 %below.1 = (f32[64,256]{1,0:T(8,128)S(1)}, f32[6,2,64,256]{3,2,1,0:T(8,128)S(1)}) custom-call(f32[64,64]{1,0:T(8,128)S(1)} %copy-done.1, f32[32,384]{1,0:T(8,128)S(1)} %copy-done, f32[640,128]{1,0:T(8,128)S(1)} %collective-permute-done.1.dn_ref, f32[8,72,256]{2,1,0:T(8,128)S(1)} %get-tuple-element.15.x1, f32[5,8,256]{2,1,0:T(8,128)S(1)} %get-tuple-element.16.wt1, ...), custom_call_target="tpu_custom_call" | custom-call | flops 20000000 | bytes 1048576 | tf_op jit(solution)/shard_map/below/pallas_call | solution.py:279
  35.9 4.3 %collective-permute-done.up_ref = f32[640,128]{1,0:T(8,128)S(1)} collective-permute-done((f32[640,128]{1,0:T(8,128)S(1)}, f32[640,128]{1,0:T(8,128)S(1)}, u32[]{:S(2)}, u32[]{:S(2)}) %collective-permute-start) | collective-permute-done | bytes 327712 | tf_op jit(solution)/shard_map/ppermute | solution.py:312
  40.3 0.0 copy-done.2
  40.3 3.5 %last.1 = f32[512,128]{1,0:T(8,128)S(1)} custom-call(f32[64,64]{1,0:T(8,128)S(1)} %copy-done.1, f32[64,64]{1,0:T(8,128)S(1)} %copy-done.2, f32[32,384]{1,0:T(8,128)S(1)} %copy-done, f32[640,128]{1,0:T(8,128)S(1)} %collective-permute-done.up_ref, f32[8,64,128]{2,1,0:T(8,128)S(1)} %get-tuple-element.14.main_ref, f32[8,72,256]{2,1,0:T(8,128)S(1)} %get-tuple-element.15.x1, ...), custom_call_target="tpu_custom_call" | custom-call | flops 30000000 | bytes 1048576 | tf_op jit(solution)/shard_map/last/pallas_call | solution.py:279
  43.8 14.8 %all_to_all.11 = f32[16,32,128]{2,1,0:T(8,128)S(1)} all-to-all(f32[16,32,128]{2,1,0:T(8,128)S(1)} %bitcast.13), channel_id=1, replica_groups=mesh['tm'=16,'space'=32] {'tm'}, dimensions={0} | all-to-all | bytes 524288 | tf_op jit(solution)/shard_map/all_to_all | solution.py:315
  58.6 0.7 %copy_bitcast_fusion = f32[4,8,2048]{2,1,0:T(8,128)} fusion(f32[16,32,128]{2,1,0:T(8,128)S(1)} %all_to_all.11), kind=kLoop, calls=%fused_computation | loop fusion | bytes 524288 | tf_op jit(solution)/shard_map/reshape | solution.py:301
Async XLA Ops:
  1.2 26.2 %copy-start = (f32[32,384]{1,0:T(8,128)S(1)}, f32[32,384]{1,0:T(8,128)}, u32[]{:S(2)}) copy-start(f32[32,384]{1,0:T(8,128)} %constant.14.clone.shift_ref) | copy-start | bytes 147460
  1.2 26.2 %copy-start.1 = (f32[64,64]{1,0:T(8,128)S(1)}, f32[64,64]{1,0:T(8,128)}, u32[]{:S(2)}) copy-start(f32[64,64]{1,0:T(8,128)} %constant.12.clone.fwd_ref) | copy-start | bytes 49156
  22.0 11.4 %collective-permute-start.1 = (f32[640,128]{1,0:T(8,128)S(1)}, f32[640,128]{1,0:T(8,128)S(1)}, u32[]{:S(2)}, u32[]{:S(2)}) collective-permute-start(f32[640,128]{1,0:T(8,128)S(1)} %bitcast.10), channel_id=1, source_target_pairs={{1,0},{2,1},{3,2},{4,3},{5,4},{6,5},{7,6},{8,7},{9,8},{10,9},{11,1... | collective-permute-start | bytes 983048 | tf_op jit(solution)/shard_map/ppermute | solution.py:313
  25.5 14.8 %collective-permute-start = (f32[640,128]{1,0:T(8,128)S(1)}, f32[640,128]{1,0:T(8,128)S(1)}, u32[]{:S(2)}, u32[]{:S(2)}) collective-permute-start(f32[640,128]{1,0:T(8,128)S(1)} %bitcast.11), channel_id=1, source_target_pairs={{0,1},{1,2},{2,3},{3,4},{4,5},{5,6},{6,7},{7,8},{8,9},{9,10},{10,1... | collective-permute-start | bytes 983048 | tf_op jit(solution)/shard_map/ppermute | solution.py:312
  33.4 6.9 %copy-start.2 = (f32[64,64]{1,0:T(8,128)S(1)}, f32[64,64]{1,0:T(8,128)}, u32[]{:S(2)}) copy-start(f32[64,64]{1,0:T(8,128)} %constant.13.clone.inv_ref) | copy-start | bytes 49156

commit v6 on v5

--- a/solution.py
+++ b/solution.py
@@ -38,6 +38,8 @@
     shift_im = beta * np.sin(2.0 * np.pi * k / STEPS)
     shift_alt = shift_re.copy()
     shift_alt[0] = 1.0 + beta
+    order = n.reshape(DEVS, LOCAL).T.reshape(-1)
+    fwd, inv = fwd[:, order], inv[order]
     shifts = np.zeros((HALF, 3 * LANES), np.float32)
     shifts[:, :LANES] = shift_re[:, None]
     shifts[:, LANES : 2 * LANES] = shift_im[:, None]
@@ -56,26 +58,33 @@
     return jnp.sum(moved, axis=0, keepdims=True)
 
 
+def flip(tile):
+    row = lax.broadcasted_iota(jnp.int32, (ROWS, LANES), 0)
+    return jnp.take_along_axis(tile, ROWS - 1 - row, axis=0)
+
+
 def pack_kernel(t_ref, it_ref, ini_ref, dif_ref, cx_ref, cy_ref, send_ref):
     t = t_ref[0]
     which, share = t % 4, t // 4
     coef = jnp.where(which < 2, jnp.where(which == 0, ini_ref[...], dif_ref[...]), jnp.where(which == 2, cx_ref[...], cy_ref[...]))
-    turned = pltpu.roll(coef, (ROWS - 2 * share) % ROWS, 0)
+    sign = jnp.where(which == 3, -1.0, 1.0)
     zero = jnp.zeros((ROWS, LANES), F32)
 
-    def sides(cols, d):
-        return rim(cols(d - 1) if d else zero, cols(d + 1) if d + 1 < DEVS else zero)
-
+    def sides(tiles, d):
+        return rim(tiles[d - 1] if d else zero, tiles[d + 1] if d + 1 < DEVS else zero)
+
+    plain = [[it_ref[n, :, e * LANES : (e + 1) * LANES] for e in range(DEVS)] for n in range(LOCAL)]
+    plain.append([coef[:, e * LANES : (e + 1) * LANES] for e in range(DEVS)])
+    turned = [[flip(tile) for tile in tiles] for tiles in plain]
+    turned[LOCAL] = [sign * tile for tile in turned[LOCAL]]
     for d in range(DEVS):
-        rims = []
+        tiles = turned if d % 2 else plain
         for n in range(LOCAL):
-            cols = lambda e: it_ref[n, :, e * LANES : (e + 1) * LANES]
-            send_ref[d, n * ROWS : (n + 1) * ROWS, :] = cols(d)
-            rims.append(sides(cols, d))
-        rims.append(turned[:2, d * LANES : (d + 1) * LANES])
-        rims.append(sides(lambda e: coef[:, e * LANES : (e + 1) * LANES], d))
-        rims.append(jnp.zeros((1, LANES), F32))
-        send_ref[d, LOCAL * ROWS :, :] = jnp.concatenate(rims, 0)
+            send_ref[d, n * ROWS : (n + 1) * ROWS, :] = tiles[n][d]
+        tail = [sides(tiles[n], d) for n in range(LOCAL)]
+        tail.append(pltpu.roll(tiles[LOCAL][d], (ROWS - 2 * share) % ROWS, 0)[:2])
+        tail.append(sides(tiles[LOCAL], d))
+        send_ref[d, LOCAL * ROWS :, :] = jnp.concatenate(tail + [zero[:1]], 0)
 
 
 def mul(matrix, value):
@@ -86,31 +95,30 @@
     return refs[j // ROWS].at[j % ROWS]
 
 
-def build(ref, x_ref, wt_ref, rim_ref, coef_ref, main_ref=None):
+def build(ref, x_ref, wt_ref, coef_ref, main_ref=None):
     def tiles(main, turned):
         lane = lane_ids(main.shape[0])
         return jnp.where(lane >= LANES - 8, turned, main), jnp.where(lane < 8, turned, main)
 
+    def steps(offset, stride):
+        starts = [half * 8 * BLOCK + n * stride + offset for n in range(LOCAL) for half in range(2)]
+        return jnp.concatenate([ref[pl.ds(start, 8, stride=BLOCK), :] for start in starts], 0)
+
     for d in range(DEVS):
-        base = d * BLOCK + LOCAL * ROWS
-        rim_ref[d * LOCAL : (d + 1) * LOCAL, :] = ref[base : base + LOCAL, :]
-        share = 2 * (d // 4)
-        coef_ref[d % 4, share : share + 2, :LANES] = ref[base + LOCAL : base + LOCAL + 2, :]
-        if d < 4:
-            rim_ref[STEPS + d : STEPS + d + 1, :] = ref[base + LOCAL + 2 : base + LOCAL + 3, :]
-    rims = rim_ref[...]
+        base, share = d * BLOCK + (ROWS + 1) * LOCAL, 2 * (d // 4)
+        coef_ref[d % 4, share : share + 2, :LANES] = ref[base : base + 2, :]
+    rims = jnp.concatenate([steps(ROWS * LOCAL, 1), ref[pl.ds((ROWS + 1) * LOCAL + 2, 4, stride=BLOCK), :]], 0)
     for r in range(ROWS):
-        for d in range(DEVS):
-            x_ref[r, 8 + d * LOCAL : 8 + (d + 1) * LOCAL, :LANES] = ref[pl.ds(d * BLOCK + r, LOCAL, stride=ROWS), :]
-        turned = pltpu.roll(rims, (2 * LANES - 16 * r - 8) % LANES, 1)
-        main = x_ref[r, 8:, :LANES]
+        main = steps(r, ROWS)
         if main_ref is not None:
             main_ref[r] = main
-        x_ref[r, 8:, :LANES], x_ref[r, 8:, LANES:] = tiles(main, turned[:STEPS])
+        turned = pltpu.roll(rims, (2 * LANES - 16 * r - 8) % LANES, 1)
+        x_ref[r, DEVS:, :LANES], x_ref[r, DEVS:, LANES:] = tiles(main, turned[:STEPS])
         for a in range(4):
             one = slice(r, r + 1)
             coef_ref[a, one, :LANES], coef_ref[a, one, LANES:] = tiles(coef_ref[a, one, :LANES], turned[STEPS + a : STEPS + a + 1])
-        x_ref[r, 7:8, :] = coef_ref[0, r : r + 1, :]
+        x_ref[r, :1, :] = coef_ref[0, r : r + 1, :]
+        x_ref[r, 1:DEVS, :] = x_ref[r, STEPS : STEPS + DEVS - 1, :]
     dif, cx, cy = coef_ref[1], coef_ref[2], coef_ref[3]
     west = dif + jnp.maximum(cx, 0.0)
     east = dif + jnp.maximum(-cx, 0.0)
@@ -159,9 +167,9 @@
 
     def first(self, fwd_ref, j, dst):
         wts = self.weights(j)
-        here = row(self.x, j)[8:, :]
-        r = row(self.x, j)[7 : 7 + STEPS, :] - here
-        r = r + near(wts, here, row(self.x, j - 1)[8:, :], row(self.x, j + 1)[8:, :]) - wts[4] * here
+        here = row(self.x, j)[DEVS:, :]
+        r = row(self.x, j)[:STEPS, :] - here
+        r = r + near(wts, here, row(self.x, j - 1)[DEVS:, :], row(self.x, j + 1)[DEVS:, :]) - wts[4] * here
         hat = mul(fwd_ref[...], r)
         for g in range(HALF // 8):
             p_re, p_im = parts(g)
@@ -188,8 +196,8 @@
     return slice(8 * g, 8 * g + 8), slice(HALF + 8 * g, HALF + 8 * g + 8)
 
 
-def own_kernel(fwd_ref, shift_ref, own_ref, main_ref, x_ref, wt_ref, a_ref, alt_ref, b_ref, f_ref, rim_ref, coef_ref):
-    build(own_ref, x_ref, wt_ref, rim_ref, coef_ref, main_ref)
+def own_kernel(fwd_ref, shift_ref, own_ref, main_ref, x_ref, wt_ref, a_ref, alt_ref, b_ref, f_ref, coef_ref):
+    build(own_ref, x_ref, wt_ref, coef_ref, main_ref)
     grid = Grid(*[(None, ref, None) for ref in (x_ref, wt_ref, a_ref, alt_ref, b_ref)])
     for r in range(ROWS):
         diagonal(shift_ref, wt_ref, a_ref, alt_ref, b_ref, r)
@@ -199,9 +207,9 @@
 
 def below_kernel(
     fwd_ref, shift_ref, dn_ref, x1, wt1, a1, alt1, b1, f1,
-    f15_ref, edge_ref, x_ref, wt_ref, a_ref, alt_ref, b_ref, f_ref, w_ref, rim_ref, coef_ref,
+    f15_ref, edge_ref, x_ref, wt_ref, a_ref, alt_ref, b_ref, f_ref, w_ref, coef_ref,
 ):
-    build(dn_ref, x_ref, wt_ref, rim_ref, coef_ref)
+    build(dn_ref, x_ref, wt_ref, coef_ref)
     grid = Grid((None, x1, x_ref), (None, wt1, wt_ref), (None, a1, a_ref), (None, alt1, alt_ref), (None, b1, b_ref))
     for r in range(ROWS - 1):
         diagonal(shift_ref, wt_ref, a_ref, alt_ref, b_ref, r)
@@ -219,10 +227,10 @@
 
 
 def last_kernel(
-    fwd_ref, inv_ref, shift_ref, up_ref, main_ref, x1, wt1, a1, alt1, b1, f1, f15_ref, edge_ref,
-    out_ref, x_ref, wt_ref, a_ref, alt_ref, b_ref, f_ref, w_ref, rim_ref, coef_ref,
+    t_ref, fwd_ref, inv_ref, shift_ref, up_ref, main_ref, x1, wt1, a1, alt1, b1, f1, f15_ref, edge_ref,
+    out_ref, x_ref, wt_ref, a_ref, alt_ref, b_ref, f_ref, w_ref, coef_ref,
 ):
-    build(up_ref, x_ref, wt_ref, rim_ref, coef_ref)
+    build(up_ref, x_ref, wt_ref, coef_ref)
     grid = Grid((x_ref, x1), (wt_ref, wt1), (a_ref, a1), (alt_ref, alt1), (b_ref, b1))
     for r in range(1, ROWS):
         diagonal(shift_ref, wt_ref, a_ref, alt_ref, b_ref, r)
@@ -246,7 +254,10 @@
     for r in range(0, ROWS, 2):
         corr = mul(inv_ref[...], jnp.concatenate([final(ROWS + r), final(ROWS + r + 1)], 1))
         for i in range(2):
-            out_ref[pl.ds(r + i, STEPS, stride=ROWS), :] = main_ref[r + i] + corr[:, i * LANES : (i + 1) * LANES]
+            new = main_ref[r + i] + corr[:, i * LANES : (i + 1) * LANES]
+            place = jnp.where(t_ref[0] % 2 == 0, r + i, ROWS - 1 - r - i)
+            for n in range(LOCAL):
+                out_ref[pl.ds(n * ROWS + place, DEVS, stride=ROWS * LOCAL), :] = new[n * DEVS : (n + 1) * DEVS]
 
 
 def vmem(count):
@@ -264,7 +275,7 @@
 
 
 BLOCKS = {
-    "x": (ROWS, STEPS + 8, WIDE),
+    "x": (ROWS, STEPS + DEVS, WIDE),
     "wt": (5, ROWS, WIDE),
     "a": (ROWS, HALF, WIDE),
     "alt": (ROWS, 8, WIDE),
@@ -272,15 +283,15 @@
 }
 FIELDS = (ROWS, STEPS, WIDE)
 PAIRS = (SWEEPS - 2, 2, STEPS, WIDE)
-EXTRA = [pltpu.VMEM((STEPS + 8, LANES), F32), pltpu.VMEM((4, ROWS, WIDE), F32)]
-
-
-def call(kernel, name, flops, operands, shapes, scratch):
+EXTRA = [pltpu.VMEM((4, ROWS, WIDE), F32)]
+
+
+def call(kernel, name, flops, operands, shapes, scratch, scalars=0):
     return pl.pallas_call(
         kernel,
         name=name,
         out_shape=tuple(jax.ShapeDtypeStruct(shape, F32) for shape in shapes),
-        in_specs=vmem(len(operands)),
+        in_specs=[pl.BlockSpec(memory_space=pltpu.SMEM)] * scalars + vmem(len(operands) - scalars),
         out_specs=tuple(vmem(len(shapes))),
         scratch_shapes=[pltpu.VMEM(shape, F32) for shape in scratch] + EXTRA,
         compiler_params=pltpu.CompilerParams(vmem_limit_bytes=24 * 1024 * 1024),
@@ -288,13 +299,13 @@
     )(*operands)
 
 
-def solve(up, own, down):
+def solve(t, above, own, below):
     fwd, inv, shifts = [jnp.asarray(table) for table in tables()]
     block = list(BLOCKS.values())
     main, *mine = call(own_kernel, "own", 10**7, (fwd, shifts, own), [(ROWS, STEPS, LANES)] + block + [FIELDS], [])
-    low = call(below_kernel, "below", 2 * 10**7, (fwd, shifts, down) + tuple(mine), [(STEPS, WIDE), PAIRS], block + [FIELDS, (2, 2 * ROWS, STEPS, WIDE)])
-    args = (fwd, inv, shifts, up, main) + tuple(mine) + tuple(low)
-    return call(last_kernel, "last", 3 * 10**7, args, [(STEPS * ROWS, LANES)], block + [(ROWS + 1, STEPS, WIDE), (2, 2 * ROWS, STEPS, WIDE)])[0]
+    low = call(below_kernel, "below", 2 * 10**7, (fwd, shifts, below) + tuple(mine), [(STEPS, WIDE), PAIRS], block + [FIELDS, (2, 2 * ROWS, STEPS, WIDE)])
+    args = (t, fwd, inv, shifts, above, main) + tuple(mine) + tuple(low)
+    return call(last_kernel, "last", 3 * 10**7, args, [(STEPS * ROWS, LANES)], block + [(ROWS + 1, STEPS, WIDE), (2, 2 * ROWS, STEPS, WIDE)], 1)[0]
 
 
 def place(received):
@@ -304,14 +315,18 @@
 def local(iterate, initial, diffusion, courant_x, courant_y):
     t = lax.axis_index("tm").astype(jnp.int32).reshape(1)
     send = pack(t, iterate, initial, diffusion, courant_x, courant_y)
-    count = lax.axis_size("space")
-    down = [(i, i + 1) for i in range(count - 1)]
-    up = [(i + 1, i) for i in range(count - 1)]
     own = lax.all_to_all(send, "tm", split_axis=0, concat_axis=0, tiled=True)
     own = own.reshape(DEVS * BLOCK, LANES)
-    above = lax.ppermute(own, "space", down)
-    below = lax.ppermute(own, "space", up)
-    new = solve(above, own, below)
+    count, halo = lax.axis_size("space"), []
+    for way in (1, 0):
+        pairs = []
+        for d in range(DEVS):
+            for i in range(count - 1):
+                lower, upper = d * count + i + 1, d * count + i
+                pairs.append((upper, lower) if d % 2 == way else (lower, upper))
+        halo.append(lax.ppermute(own, ("tm", "space"), pairs))
+    below, above = halo
+    new = solve(t, above, own, below)
     back = lax.all_to_all(new.reshape(DEVS, LOCAL * ROWS, LANES), "tm", split_axis=0, concat_axis=0, tiled=True)
     return place(back)
 

time: 59.6 us -> 57.1 us (0.958)
  waiting for transfers between devices: 9.33 us -> 1.61 us
  starting transfers between devices: 5.39 us -> 8.59 us
  blocking collectives: 35.6 us -> 37.6 us
    ppermute x2, waiting for transfers between devices: 9.33 us -> 1.61 us  [local(): halo.append(lax.ppermute(own, ('tm', 'space'), pairs))]
    ppermute x2, starting transfers between devices: 5.39 us -> 8.59 us  [local(): halo.append(lax.ppermute(own, ('tm', 'space'), pairs))]
    all_to_all x1, blocking collectives: 14.8 us -> 16.8 us  [local(): lax.all_to_all(new.reshape(DEVS, LOCAL * ROWS, LANES), 'tm', split_axis=0...]
  transfers between devices with their start and end apart: 2 -> 2, of which waited for: 2 -> 1; matrix products, arithmetic and copies ran while one was open for 0% -> 0% of each run, Pallas kernels for 6% -> 6%
where the time goes in v6:
time: 57.1 us; the launch traced here: 56.7 us
  blocking collectives  37.6 us (66%)
  starting transfers between devices  8.59 us (15%)
  Pallas kernels  8.07 us (14%)
  waiting for transfers between devices  1.61 us (3%)
  local copies, waits for them, and re-layouts  0.74 us (1%)
    all_to_all x1, blocking collectives, local(): own = lax.all_to_all(send, 'tm', split_axis=0, concat_axis=0, tiled=True)  20.8 us
    all_to_all x1, blocking collectives, local(): lax.all_to_all(new.reshape(DEVS, LOCAL * ROWS, LANES), 'tm', split_axis=0...  16.8 us
    ppermute x2, starting transfers between devices, local(): halo.append(lax.ppermute(own, ('tm', 'space'), pairs))  8.59 us
    pallas_call x3, Pallas kernels, call(): pl.pallas_call(kernel, name=name, out_shape=tuple((jax.ShapeDtypeStruct(s...  6.87 us
    ppermute x2, waiting for transfers between devices, local(): halo.append(lax.ppermute(own, ('tm', 'space'), pairs))  1.61 us
    pallas_call x1, Pallas kernels, pack(): pl.pallas_call(pack_kernel, name='pack', out_shape=pltpu.VMEM((DEVS, BLOC...  1.2 us
  transfers between devices with their start and end apart: 2, of which 1 were waited for; matrix products, arithmetic and copies ran while one was open for 0% of the time, Pallas kernels for 6%

profile of v6, /device:TPU:257, one launch (start us, length us, event | category | flops | bytes accessed | tf_op | source)
XLA Modules:
  0.0 56.7 jit_solution(9611081014799831328)
XLA Ops:
  0.0 1.2 %pack.1 = f32[16,40,128]{2,1,0:T(8,128)S(1)} custom-call(s32[1]{0:T(128)} %bitcast.t_ref, f32[4,8,2048]{2,1,0:T(8,128)} %it_ref.1, f32[8,2048]{1,0:T(8,128)} %ini_ref.1, f32[8,2048]{1,0:T(8,128)} %dif_ref.1, f32[8,2048]{1,0:T(8,128)} %cx_ref.1, f32[8,2048]{1,0:T(8,128)} %cy_ref.1), custom_call_target="tpu_custom_call" | custom-call | tf_op jit(solution)/shard_map/pack/pallas_call | solution.py:268
  1.2 0.0 copy-start
  1.2 0.0 copy-start.1
  1.2 20.8 %all_to_all.10 = f32[16,40,128]{2,1,0:T(8,128)S(1)} all-to-all(f32[16,40,128]{2,1,0:T(8,128)S(1)} %pack.1), channel_id=1, replica_groups=mesh['tm'=16,'space'=32] {'tm'}, dimensions={0} | all-to-all | bytes 655360 | tf_op jit(solution)/shard_map/all_to_all | solution.py:318
  22.0 3.1 %collective-permute-start.1 = (f32[640,128]{1,0:T(8,128)S(1)}, f32[640,128]{1,0:T(8,128)S(1)}, u32[]{:S(2)}, u32[]{:S(2)}) collective-permute-start(f32[640,128]{1,0:T(8,128)S(1)} %bitcast.10), channel_id=1, source_target_pairs={{1,0},{2,1},{3,2},{4,3},{5,4},{6,5},{7,6},{8,7},{9,8},{10,9},{11,1... | collective-permute-start | bytes 983048 | tf_op jit(solution)/shard_map/ppermute | solution.py:327
  25.1 5.5 %collective-permute-start = (f32[640,128]{1,0:T(8,128)S(1)}, f32[640,128]{1,0:T(8,128)S(1)}, u32[]{:S(2)}, u32[]{:S(2)}) collective-permute-start(f32[640,128]{1,0:T(8,128)S(1)} %bitcast.11), channel_id=1, source_target_pairs={{0,1},{1,2},{2,3},{3,4},{4,5},{5,6},{6,7},{7,8},{8,9},{9,10},{10,1... | collective-permute-start | bytes 983048 | tf_op jit(solution)/shard_map/ppermute | solution.py:327
  30.6 0.0 copy-done
  30.6 0.0 copy-done.1
  30.6 0.9 %own.1 = (f32[8,64,128]{2,1,0:T(8,128)S(1)}, f32[8,80,256]{2,1,0:T(8,128)S(1)}, f32[5,8,256]{2,1,0:T(8,128)S(1)}, f32[8,32,256]{2,1,0:T(8,128)S(1)}, f32[8,8,256...) custom-call(f32[64,64]{1,0:T(8,128)S(1)} %copy-done.1, f32[32,384]{1,0:T(8,128)S(1)} %copy-done, ...), custom_call_target="tpu_custom_call" | custom-call | flops 10000000 | bytes 1048576 | tf_op jit(solution)/shard_map/own/pallas_call | solution.py:290
  31.5 1.6 %collective-permute-done.1.dn_ref = f32[640,128]{1,0:T(8,128)S(1)} collective-permute-done((f32[640,128]{1,0:T(8,128)S(1)}, f32[640,128]{1,0:T(8,128)S(1)}, u32[]{:S(2)}, u32[]{:S(2)}) %collective-permute-start.1) | collective-permute-done | bytes 327712 | tf_op jit(solution)/shard_map/ppermute | solution.py:327
  33.1 0.0 copy-start.2
  33.1 2.5 %below.1 = (f32[64,256]{1,0:T(8,128)S(1)}, f32[6,2,64,256]{3,2,1,0:T(8,128)S(1)}) custom-call(f32[64,64]{1,0:T(8,128)S(1)} %copy-done.1, f32[32,384]{1,0:T(8,128)S(1)} %copy-done, f32[640,128]{1,0:T(8,128)S(1)} %collective-permute-done.1.dn_ref, f32[8,80,256]{2,1,0:T(8,128)S(1)} %get-tuple-element.15.x1, f32[5,8,256]{2,1,0:T(8,128)S(1)} %get-tuple-element.16.wt1, ...), custom_call_target="tpu_custom_call" | custom-call | flops 20000000 | bytes 1048576 | tf_op jit(solution)/shard_map/below/pallas_call | solution.py:290
  35.6 0.0 collective-permute-done.up_ref
  35.6 0.0 copy-done.2
  35.6 3.5 %last.1 = f32[512,128]{1,0:T(8,128)S(1)} custom-call(s32[1]{0:T(128)} %bitcast.t_ref, f32[64,64]{1,0:T(8,128)S(1)} %copy-done.1, f32[64,64]{1,0:T(8,128)S(1)} %copy-done.2, f32[32,384]{1,0:T(8,128)S(1)} %copy-done, f32[640,128]{1,0:T(8,128)S(1)} %collective-permute-done.up_ref, f32[8,64,128]{2,1,0:T(8,128)S(1)} %get-tuple-element.14.main_ref, ...), custom_call_target="tpu_custom_call" | custom-call | flops 30000000 | bytes 1048576 | tf_op jit(solution)/shard_map/last/pallas_call | solution.py:290
  39.2 16.8 %all_to_all.11 = f32[16,32,128]{2,1,0:T(8,128)S(1)} all-to-all(f32[16,32,128]{2,1,0:T(8,128)S(1)} %bitcast.13), channel_id=1, replica_groups=mesh['tm'=16,'space'=32] {'tm'}, dimensions={0} | all-to-all | bytes 524288 | tf_op jit(solution)/shard_map/all_to_all | solution.py:330
  56.0 0.7 %copy_bitcast_fusion = f32[4,8,2048]{2,1,0:T(8,128)} fusion(f32[16,32,128]{2,1,0:T(8,128)S(1)} %all_to_all.11), kind=kLoop, calls=%fused_computation | loop fusion | bytes 524288 | tf_op jit(solution)/shard_map/reshape | solution.py:312
Async XLA Ops:
  1.2 29.4 %copy-start = (f32[32,384]{1,0:T(8,128)S(1)}, f32[32,384]{1,0:T(8,128)}, u32[]{:S(2)}) copy-start(f32[32,384]{1,0:T(8,128)} %constant.14.clone.shift_ref) | copy-start | bytes 147460
  1.2 29.4 %copy-start.1 = (f32[64,64]{1,0:T(8,128)S(1)}, f32[64,64]{1,0:T(8,128)}, u32[]{:S(2)}) copy-start(f32[64,64]{1,0:T(8,128)} %constant.12.clone.fwd_ref) | copy-start | bytes 49156
  22.0 11.1 %collective-permute-start.1 = (f32[640,128]{1,0:T(8,128)S(1)}, f32[640,128]{1,0:T(8,128)S(1)}, u32[]{:S(2)}, u32[]{:S(2)}) collective-permute-start(f32[640,128]{1,0:T(8,128)S(1)} %bitcast.10), channel_id=1, source_target_pairs={{1,0},{2,1},{3,2},{4,3},{5,4},{6,5},{7,6},{8,7},{9,8},{10,9},{11,1... | collective-permute-start | bytes 983048 | tf_op jit(solution)/shard_map/ppermute | solution.py:327
  25.1 10.5 %collective-permute-start = (f32[640,128]{1,0:T(8,128)S(1)}, f32[640,128]{1,0:T(8,128)S(1)}, u32[]{:S(2)}, u32[]{:S(2)}) collective-permute-start(f32[640,128]{1,0:T(8,128)S(1)} %bitcast.11), channel_id=1, source_target_pairs={{0,1},{1,2},{2,3},{3,4},{4,5},{5,6},{6,7},{7,8},{8,9},{9,10},{10,1... | collective-permute-start | bytes 983048 | tf_op jit(solution)/shard_map/ppermute | solution.py:327
  33.1 2.5 %copy-start.2 = (f32[64,64]{1,0:T(8,128)S(1)}, f32[64,64]{1,0:T(8,128)}, u32[]{:S(2)}) copy-start(f32[64,64]{1,0:T(8,128)} %constant.13.clone.inv_ref) | copy-start | bytes 49156

commit v7 on v6

--- a/solution.py
+++ b/solution.py
@@ -20,6 +20,7 @@
 SPAN = 3 * ROWS
 WIDE = 2 * LANES
 F32 = jnp.float32
+BF16 = jnp.bfloat16
 
 
 def tables():
@@ -87,8 +88,22 @@
         send_ref[d, LOCAL * ROWS :, :] = jnp.concatenate(tail + [zero[:1]], 0)
 
 
+def pieces(value):
+    first = value.astype(BF16)
+    rest = value - first.astype(F32)
+    second = rest.astype(BF16)
+    return first, second, (rest - second.astype(F32)).astype(BF16)
+
+
+def stacked(table):
+    one, two, three = [np.asarray(part) for part in pieces(table)]
+    return np.concatenate([one, two, one, two, one, three], 1)
+
+
 def mul(matrix, value):
-    return jnp.dot(matrix, value, precision=lax.Precision.HIGHEST, preferred_element_type=F32)
+    one, two, three = pieces(value)
+    parts_of = jnp.concatenate([one, one, two, two, three, one], 0)
+    return jnp.dot(matrix, parts_of, preferred_element_type=F32)
 
 
 def row(refs, j):
@@ -196,7 +211,13 @@
     return slice(8 * g, 8 * g + 8), slice(HALF + 8 * g, HALF + 8 * g + 8)
 
 
-def own_kernel(fwd_ref, shift_ref, own_ref, main_ref, x_ref, wt_ref, a_ref, alt_ref, b_ref, f_ref, coef_ref):
+def early(m, j):
+    return (m - 2) * 4 + j - 8 - m if m in (2, 3) and 8 + m <= j < 16 - m else None
+
+
+def own_kernel(
+    fwd_ref, shift_ref, own_ref, main_ref, x_ref, wt_ref, a_ref, alt_ref, b_ref, f_ref, early_ref, coef_ref
+):
     build(own_ref, x_ref, wt_ref, coef_ref, main_ref)
     grid = Grid(*[(None, ref, None) for ref in (x_ref, wt_ref, a_ref, alt_ref, b_ref)])
     for r in range(ROWS):
@@ -204,9 +225,16 @@
     for r in range(1, ROWS - 1):
         grid.first(fwd_ref, ROWS + r, f_ref.at[r])
 
+    def level(m, j):
+        return f_ref.at[j - 8] if m == 1 else early_ref.at[early(m, j)]
+
+    for m in (2, 3):
+        for j in range(8 + m, 16 - m):
+            grid.store(j, level, m)
+
 
 def below_kernel(
-    fwd_ref, shift_ref, dn_ref, x1, wt1, a1, alt1, b1, f1,
+    fwd_ref, shift_ref, dn_ref, x1, wt1, a1, alt1, b1, f1, early_ref,
     f15_ref, edge_ref, x_ref, wt_ref, a_ref, alt_ref, b_ref, f_ref, w_ref, coef_ref,
 ):
     build(dn_ref, x_ref, wt_ref, coef_ref)
@@ -217,17 +245,20 @@
     def level(m, j):
         if m == 1:
             return f1.at[j - 8] if j < 15 else f15_ref if j == 15 else f_ref.at[j - 16]
-        return edge_ref.at[m - 2, j - 8 - m] if j <= 9 + m else w_ref.at[m % 2, j - 8]
+        if early(m, j) is not None:
+            return early_ref.at[early(m, j)]
+        return edge_ref.at[m - 4, j - 8 - m] if j <= 9 + m else w_ref.at[m % 2, j - 8]
 
     for j in range(15, SPAN - 1):
         grid.first(fwd_ref, j, level(1, j))
     for m in range(2, SWEEPS):
         for j in range(8 + m, SPAN - m):
-            grid.store(j, level, m)
+            if early(m, j) is None:
+                grid.store(j, level, m)
 
 
 def last_kernel(
-    t_ref, fwd_ref, inv_ref, shift_ref, up_ref, main_ref, x1, wt1, a1, alt1, b1, f1, f15_ref, edge_ref,
+    t_ref, fwd_ref, inv_ref, shift_ref, up_ref, main_ref, x1, wt1, a1, alt1, b1, f1, early_ref, f15_ref, edge_ref,
     out_ref, x_ref, wt_ref, a_ref, alt_ref, b_ref, f_ref, w_ref, coef_ref,
 ):
     build(up_ref, x_ref, wt_ref, coef_ref)
@@ -238,7 +269,9 @@
     def level(m, j):
         if m == 1:
             return f_ref.at[j] if j <= 8 else f1.at[j - 8] if j < 15 else f15_ref
-        return w_ref.at[m % 2, j] if j <= 7 + m else edge_ref.at[m - 2, j - 8 - m]
+        if early(m, j) is not None:
+            return early_ref.at[early(m, j)]
+        return w_ref.at[m % 2, j] if j <= 7 + m else edge_ref.at[m - 4, j - 8 - m]
 
     for j in range(1, ROWS + 1):
         grid.first(fwd_ref, j, level(1, j))
@@ -282,7 +315,7 @@
     "b": (ROWS, HALF, WIDE),
 }
 FIELDS = (ROWS, STEPS, WIDE)
-PAIRS = (SWEEPS - 2, 2, STEPS, WIDE)
+PAIRS = (SWEEPS - 4, 2, STEPS, WIDE)
 EXTRA = [pltpu.VMEM((4, ROWS, WIDE), F32)]
 
 
@@ -300,9 +333,10 @@
 
 
 def solve(t, above, own, below):
-    fwd, inv, shifts = [jnp.asarray(table) for table in tables()]
+    fwd, inv, shifts = tables()
+    fwd, inv, shifts = jnp.asarray(stacked(fwd)), jnp.asarray(stacked(inv)), jnp.asarray(shifts)
     block = list(BLOCKS.values())
-    main, *mine = call(own_kernel, "own", 10**7, (fwd, shifts, own), [(ROWS, STEPS, LANES)] + block + [FIELDS], [])
+    main, *mine = call(own_kernel, "own", 10**7, (fwd, shifts, own), [(ROWS, STEPS, LANES)] + block + [FIELDS, (6, STEPS, WIDE)], [])
     low = call(below_kernel, "below", 2 * 10**7, (fwd, shifts, below) + tuple(mine), [(STEPS, WIDE), PAIRS], block + [FIELDS, (2, 2 * ROWS, STEPS, WIDE)])
     args = (t, fwd, inv, shifts, above, main) + tuple(mine) + tuple(low)
     return call(last_kernel, "last", 3 * 10**7, args, [(STEPS * ROWS, LANES)], block + [(ROWS + 1, STEPS, WIDE), (2, 2 * ROWS, STEPS, WIDE)], 1)[0]

time: 57.1 us -> 56.7 us (level)
  Pallas kernels: 8.07 us -> 7.36 us
    pallas_call x3, Pallas kernels: 6.87 us -> 6.17 us  [call(): pl.pallas_call(kernel, name=name, out_shape=tuple((jax.ShapeDtypeStruct(s...]
  transfers between devices with their start and end apart: 2 -> 2, of which waited for: 1 -> 1; matrix products, arithmetic and copies ran while one was open for 0% -> 0% of each run, Pallas kernels for 6% -> 5%
where the time goes in v7:
time: 56.7 us; the launch traced here: 56.4 us
  blocking collectives  38 us (67%)
  starting transfers between devices  8.59 us (15%)
  Pallas kernels  7.36 us (13%)
  waiting for transfers between devices  1.65 us (3%)
  local copies, waits for them, and re-layouts  0.74 us (1%)
    all_to_all x1, blocking collectives, local(): own = lax.all_to_all(send, 'tm', split_axis=0, concat_axis=0, tiled=True)  20.8 us
    all_to_all x1, blocking collectives, local(): lax.all_to_all(new.reshape(DEVS, LOCAL * ROWS, LANES), 'tm', split_axis=0...  17.2 us
    ppermute x2, starting transfers between devices, local(): halo.append(lax.ppermute(own, ('tm', 'space'), pairs))  8.59 us
    pallas_call x3, Pallas kernels, call(): pl.pallas_call(kernel, name=name, out_shape=tuple((jax.ShapeDtypeStruct(s...  6.17 us
    ppermute x2, waiting for transfers between devices, local(): halo.append(lax.ppermute(own, ('tm', 'space'), pairs))  1.65 us
    pallas_call x1, Pallas kernels, pack(): pl.pallas_call(pack_kernel, name='pack', out_shape=pltpu.VMEM((DEVS, BLOC...  1.2 us
  transfers between devices with their start and end apart: 2, of which 1 were waited for; matrix products, arithmetic and copies ran while one was open for 0% of the time, Pallas kernels for 5%

profile of v7, /device:TPU:257, one launch (start us, length us, event | category | flops | bytes accessed | tf_op | source)
XLA Modules:
  0.0 56.4 jit_solution(3780127080028180884)
XLA Ops:
  0.0 1.2 %pack.1 = f32[16,40,128]{2,1,0:T(8,128)S(1)} custom-call(s32[1]{0:T(128)} %bitcast.t_ref, f32[4,8,2048]{2,1,0:T(8,128)} %it_ref.1, f32[8,2048]{1,0:T(8,128)} %ini_ref.1, f32[8,2048]{1,0:T(8,128)} %dif_ref.1, f32[8,2048]{1,0:T(8,128)} %cx_ref.1, f32[8,2048]{1,0:T(8,128)} %cy_ref.1), custom_call_target="tpu_custom_call" | custom-call | tf_op jit(solution)/shard_map/pack/pallas_call | solution.py:301
  1.2 0.0 copy-start
  1.2 0.0 copy-start.1
  1.2 20.8 %all_to_all.10 = f32[16,40,128]{2,1,0:T(8,128)S(1)} all-to-all(f32[16,40,128]{2,1,0:T(8,128)S(1)} %pack.1), channel_id=1, replica_groups=mesh['tm'=16,'space'=32] {'tm'}, dimensions={0} | all-to-all | bytes 655360 | tf_op jit(solution)/shard_map/all_to_all | solution.py:352
  22.0 3.1 %collective-permute-start.1 = (f32[640,128]{1,0:T(8,128)S(1)}, f32[640,128]{1,0:T(8,128)S(1)}, u32[]{:S(2)}, u32[]{:S(2)}) collective-permute-start(f32[640,128]{1,0:T(8,128)S(1)} %bitcast.10), channel_id=1, source_target_pairs={{1,0},{2,1},{3,2},{4,3},{5,4},{6,5},{7,6},{8,7},{9,8},{10,9},{11,1... | collective-permute-start | bytes 983048 | tf_op jit(solution)/shard_map/ppermute | solution.py:361
  25.1 5.5 %collective-permute-start = (f32[640,128]{1,0:T(8,128)S(1)}, f32[640,128]{1,0:T(8,128)S(1)}, u32[]{:S(2)}, u32[]{:S(2)}) collective-permute-start(f32[640,128]{1,0:T(8,128)S(1)} %bitcast.11), channel_id=1, source_target_pairs={{0,1},{1,2},{2,3},{3,4},{4,5},{5,6},{6,7},{7,8},{8,9},{9,10},{10,1... | collective-permute-start | bytes 983048 | tf_op jit(solution)/shard_map/ppermute | solution.py:361
  30.6 0.0 copy-done
  30.6 0.0 copy-done.1
  30.6 0.9 %own.1 = (f32[8,64,128]{2,1,0:T(8,128)S(1)}, f32[8,80,256]{2,1,0:T(8,128)S(1)}, f32[5,8,256]{2,1,0:T(8,128)S(1)}, f32[8,32,256]{2,1,0:T(8,128)S(1)}, f32[8,8,256...) custom-call(bf16[64,384]{1,0:T(8,128)(2,1)S(1)} %copy-done.1, ...), custom_call_target="tpu_custom_call" | custom-call | flops 10000000 | bytes 1048576 | tf_op jit(solution)/shard_map/own/pallas_call | solution.py:323
  31.5 1.6 %collective-permute-done.1.dn_ref = f32[640,128]{1,0:T(8,128)S(1)} collective-permute-done((f32[640,128]{1,0:T(8,128)S(1)}, f32[640,128]{1,0:T(8,128)S(1)}, u32[]{:S(2)}, u32[]{:S(2)}) %collective-permute-start.1) | collective-permute-done | bytes 327712 | tf_op jit(solution)/shard_map/ppermute | solution.py:361
  33.1 0.0 copy-start.2
  33.1 2.1 %below.1 = (f32[64,256]{1,0:T(8,128)S(1)}, f32[4,2,64,256]{3,2,1,0:T(8,128)S(1)}) custom-call(bf16[64,384]{1,0:T(8,128)(2,1)S(1)} %copy-done.1, f32[32,384]{1,0:T(8,128)S(1)} %copy-done, f32[640,128]{1,0:T(8,128)S(1)} %collective-permute-done.1.dn_ref, f32[8,80,256]{2,1,0:T(8,128)S(1)} %get-tuple-element.16.x1, f32[5,8,256]{2,1,0:T(8,128)S(1)} %get-tuple-element.17.wt1, ...), custom_call_target="tpu_custom_call" | custom-call | flops 20000000 | bytes 1048576 | tf_op jit(solution)/shard_map/below/pallas_call | solution.py:323
  35.2 0.0 collective-permute-done.up_ref
  35.3 0.0 copy-done.2
  35.3 3.2 %last.1 = f32[512,128]{1,0:T(8,128)S(1)} custom-call(s32[1]{0:T(128)} %bitcast.t_ref, bf16[64,384]{1,0:T(8,128)(2,1)S(1)} %copy-done.1, bf16[64,384]{1,0:T(8,128)(2,1)S(1)} %copy-done.2, f32[32,384]{1,0:T(8,128)S(1)} %copy-done, f32[640,128]{1,0:T(8,128)S(1)} %collective-permute-done.up_ref, f32[8,64,128]{2,1,0:T(8,128)S(1)} %get-tuple-element.15.main_ref, ...), custom_call_target="tpu_custom_call" | custom-call | flops 30000000 | bytes 1048576 | tf_op jit(solution)/shard_map/last/pallas_call | solution.py:323
  38.5 17.2 %all_to_all.11 = f32[16,32,128]{2,1,0:T(8,128)S(1)} all-to-all(f32[16,32,128]{2,1,0:T(8,128)S(1)} %bitcast.13), channel_id=1, replica_groups=mesh['tm'=16,'space'=32] {'tm'}, dimensions={0} | all-to-all | bytes 524288 | tf_op jit(solution)/shard_map/all_to_all | solution.py:364
  55.7 0.7 %copy_bitcast_fusion = f32[4,8,2048]{2,1,0:T(8,128)} fusion(f32[16,32,128]{2,1,0:T(8,128)S(1)} %all_to_all.11), kind=kLoop, calls=%fused_computation | loop fusion | bytes 524288 | tf_op jit(solution)/shard_map/reshape | solution.py:346
Async XLA Ops:
  1.2 29.4 %copy-start = (f32[32,384]{1,0:T(8,128)S(1)}, f32[32,384]{1,0:T(8,128)}, u32[]{:S(2)}) copy-start(f32[32,384]{1,0:T(8,128)} %constant.14.clone.shift_ref) | copy-start | bytes 147460
  1.2 29.4 %copy-start.1 = (bf16[64,384]{1,0:T(8,128)(2,1)S(1)}, bf16[64,384]{1,0:T(8,128)(2,1)}, u32[]{:S(2)}) copy-start(bf16[64,384]{1,0:T(8,128)(2,1)} %constant.12.clone.fwd_ref) | copy-start | bytes 147460
  22.0 11.1 %collective-permute-start.1 = (f32[640,128]{1,0:T(8,128)S(1)}, f32[640,128]{1,0:T(8,128)S(1)}, u32[]{:S(2)}, u32[]{:S(2)}) collective-permute-start(f32[640,128]{1,0:T(8,128)S(1)} %bitcast.10), channel_id=1, source_target_pairs={{1,0},{2,1},{3,2},{4,3},{5,4},{6,5},{7,6},{8,7},{9,8},{10,9},{11,1... | collective-permute-start | bytes 983048 | tf_op jit(solution)/shard_map/ppermute | solution.py:361
  25.1 10.1 %collective-permute-start = (f32[640,128]{1,0:T(8,128)S(1)}, f32[640,128]{1,0:T(8,128)S(1)}, u32[]{:S(2)}, u32[]{:S(2)}) collective-permute-start(f32[640,128]{1,0:T(8,128)S(1)} %bitcast.11), channel_id=1, source_target_pairs={{0,1},{1,2},{2,3},{3,4},{4,5},{5,6},{6,7},{7,8},{8,9},{9,10},{10,1... | collective-permute-start | bytes 983048 | tf_op jit(solution)/shard_map/ppermute | solution.py:361
  33.1 2.1 %copy-start.2 = (bf16[64,384]{1,0:T(8,128)(2,1)S(1)}, bf16[64,384]{1,0:T(8,128)(2,1)}, u32[]{:S(2)}) copy-start(bf16[64,384]{1,0:T(8,128)(2,1)} %constant.13.clone.inv_ref) | copy-start | bytes 147460

commit v8 on v7

--- a/solution.py
+++ b/solution.py
@@ -19,6 +19,7 @@
 BLOCK = ROWS * LOCAL + ROWS
 SPAN = 3 * ROWS
 WIDE = 2 * LANES
+TILES = (slice(0, LANES), slice(LANES, WIDE))
 F32 = jnp.float32
 BF16 = jnp.bfloat16
 
@@ -159,10 +160,7 @@
 
 
 def near(wts, here, above, below):
-    west, east = [
-        jnp.concatenate([pltpu.roll(here[:, :LANES], by, 1), pltpu.roll(here[:, LANES:], by, 1)], 1) for by in (1, LANES - 1)
-    ]
-    summed = wts[0] * west + wts[1] * east
+    summed = wts[0] * pltpu.roll(here, 1, 1) + wts[1] * pltpu.roll(here, LANES - 1, 1)
     return summed + wts[2] * above + wts[3] * below
 
 
@@ -170,41 +168,43 @@
     def __init__(self, x, wt, a, alt, b):
         self.x, self.wt, self.a, self.alt, self.b = x, wt, a, alt, b
 
-    def weights(self, j):
+    def weights(self, j, cols):
         ref, r = self.wt[j // ROWS], j % ROWS
-        return [ref[a, r : r + 1, :] for a in range(5)]
-
-    def divide(self, j, g, q_re, q_im):
+        return [ref[a, r : r + 1, cols] for a in range(5)]
+
+    def divide(self, j, g, cols, q_re, q_im):
         part = slice(8 * g, 8 * g + 8)
-        a_re, b = row(self.a, j)[part, :], row(self.b, j)[part, :]
-        a_im = row(self.alt, j)[...] if g == 0 else a_re
+        a_re, b = row(self.a, j)[part, cols], row(self.b, j)[part, cols]
+        a_im = row(self.alt, j)[:, cols] if g == 0 else a_re
         return q_re * a_re + q_im * b, q_im * a_im - q_re * b
 
     def first(self, fwd_ref, j, dst):
-        wts = self.weights(j)
-        here = row(self.x, j)[DEVS:, :]
-        r = row(self.x, j)[:STEPS, :] - here
-        r = r + near(wts, here, row(self.x, j - 1)[DEVS:, :], row(self.x, j + 1)[DEVS:, :]) - wts[4] * here
-        hat = mul(fwd_ref[...], r)
+        rs = []
+        for cols in TILES:
+            wts = self.weights(j, cols)
+            here, above, below = [row(self.x, i)[DEVS:, cols] for i in (j, j - 1, j + 1)]
+            rs.append(row(self.x, j)[:STEPS, cols] - here + near(wts, here, above, below) - wts[4] * here)
+        hat = mul(fwd_ref[...], jnp.concatenate(rs, 1))
         for g in range(HALF // 8):
             p_re, p_im = parts(g)
-            dst[p_re, :], dst[p_im, :] = self.divide(j, g, hat[p_re], hat[p_im])
-
-    def sweep(self, j, level, m):
+            for cols in TILES:
+                dst[p_re, cols], dst[p_im, cols] = self.divide(j, g, cols, hat[p_re, cols], hat[p_im, cols])
+
+    def sweep(self, j, level, m, cols):
         values = {}
-        wts = self.weights(j)
+        wts = self.weights(j, cols)
         here, above, below = level(m - 1, j), level(m - 1, j - 1), level(m - 1, j + 1)
         base = level(1, j)
         for g in range(HALF // 8):
-            sums = [near(wts, here[p, :], above[p, :], below[p, :]) for p in parts(g)]
-            for p, value in zip(parts(g), self.divide(j, g, *sums)):
-                values[p.start] = base[p, :] + value
+            sums = [near(wts, here[p, cols], above[p, cols], below[p, cols]) for p in parts(g)]
+            for p, value in zip(parts(g), self.divide(j, g, cols, *sums)):
+                values[p.start] = base[p, cols] + value
         return values
 
-    def store(self, j, level, m):
+    def store(self, j, level, m, cols):
         dst = level(m, j)
-        for start, value in self.sweep(j, level, m).items():
-            dst[start : start + 8, :] = value
+        for start, value in self.sweep(j, level, m, cols).items():
+            dst[start : start + 8, cols] = value
 
 
 def parts(g):
@@ -230,7 +230,8 @@
 
     for m in (2, 3):
         for j in range(8 + m, 16 - m):
-            grid.store(j, level, m)
+            for cols in TILES:
+                grid.store(j, level, m, cols)
 
 
 def below_kernel(
@@ -254,7 +255,8 @@
     for m in range(2, SWEEPS):
         for j in range(8 + m, SPAN - m):
             if early(m, j) is None:
-                grid.store(j, level, m)
+                for cols in TILES:
+                    grid.store(j, level, m, cols)
 
 
 def last_kernel(
@@ -277,12 +279,36 @@
         grid.first(fwd_ref, j, level(1, j))
     for m in range(2, SWEEPS):
         for j in range(m, 8 + m):
-            grid.store(j, level, m)
-    left = lane_ids(8) < LANES // 2
+            for cols in TILES:
+                grid.store(j, level, m, cols)
+    lane, picked = lane_ids(8), {}
+    left = lane < LANES // 2
+
+    def pick(ref, mask=left):
+        return jnp.where(mask, ref[:, TILES[0]], ref[:, TILES[1]])
+
+    def old(j, p):
+        if (j, p.start) not in picked:
+            picked[j, p.start] = pick(level(SWEEPS - 1, j).at[p])
+        return picked[j, p.start]
 
     def final(j):
-        values = grid.sweep(j, level, SWEEPS)
-        return jnp.concatenate([jnp.where(left, values[p][:, :LANES], values[p][:, LANES:]) for p in range(0, STEPS, 8)], 0)
+        values = {}
+        wts = [jnp.where(left[:1], *pair) for pair in zip(*[grid.weights(j, cols) for cols in TILES])]
+        for g in range(HALF // 8):
+            sums = []
+            for p in parts(g):
+                here = level(SWEEPS - 1, j).at[p]
+                west = pltpu.roll(pick(here, left | (lane == LANES - 1)), 1, 1)
+                east = pltpu.roll(pick(here, left & (lane > 0)), LANES - 1, 1)
+                sums.append(wts[0] * west + wts[1] * east + wts[2] * old(j - 1, p) + wts[3] * old(j + 1, p))
+            p_re, p_im = parts(g)
+            a_re, b = pick(row(grid.a, j).at[p_re]), pick(row(grid.b, j).at[p_re])
+            a_im = pick(row(grid.alt, j)) if g == 0 else a_re
+            base = level(1, j)
+            values[p_re.start] = pick(base.at[p_re]) + (sums[0] * a_re + sums[1] * b)
+            values[p_im.start] = pick(base.at[p_im]) + (sums[1] * a_im - sums[0] * b)
+        return jnp.concatenate([values[p] for p in range(0, STEPS, 8)], 0)
 
     for r in range(0, ROWS, 2):
         corr = mul(inv_ref[...], jnp.concatenate([final(ROWS + r), final(ROWS + r + 1)], 1))

time: 56.7 us -> 56.6 us (level)
  no operation moved by 1% of the time
where the time goes in v8:
time: 56.6 us; the launch traced here: 56.3 us
  blocking collectives  38.1 us (67%)
  starting transfers between devices  8.59 us (15%)
  Pallas kernels  7.18 us (13%)
  waiting for transfers between devices  1.65 us (3%)
  local copies, waits for them, and re-layouts  0.74 us (1%)
    all_to_all x1, blocking collectives, local(): own = lax.all_to_all(send, 'tm', split_axis=0, concat_axis=0, tiled=True)  20.8 us
    all_to_all x1, blocking collectives, local(): lax.all_to_all(new.reshape(DEVS, LOCAL * ROWS, LANES), 'tm', split_axis=0...  17.3 us
    ppermute x2, starting transfers between devices, local(): halo.append(lax.ppermute(own, ('tm', 'space'), pairs))  8.59 us
    pallas_call x3, Pallas kernels, call(): pl.pallas_call(kernel, name=name, out_shape=tuple((jax.ShapeDtypeStruct(s...  5.98 us
    ppermute x2, waiting for transfers between devices, local(): halo.append(lax.ppermute(own, ('tm', 'space'), pairs))  1.65 us
    pallas_call x1, Pallas kernels, pack(): pl.pallas_call(pack_kernel, name='pack', out_shape=pltpu.VMEM((DEVS, BLOC...  1.2 us
  transfers between devices with their start and end apart: 2, of which 1 were waited for; matrix products, arithmetic and copies ran while one was open for 0% of the time, Pallas kernels for 5%

profile of v8, /device:TPU:257, one launch (start us, length us, event | category | flops | bytes accessed | tf_op | source)
XLA Modules:
  0.0 56.3 jit_solution(3760997328222044620)
XLA Ops:
  0.0 1.2 %pack.1 = f32[16,40,128]{2,1,0:T(8,128)S(1)} custom-call(s32[1]{0:T(128)} %bitcast.t_ref, f32[4,8,2048]{2,1,0:T(8,128)} %it_ref.1, f32[8,2048]{1,0:T(8,128)} %ini_ref.1, f32[8,2048]{1,0:T(8,128)} %dif_ref.1, f32[8,2048]{1,0:T(8,128)} %cx_ref.1, f32[8,2048]{1,0:T(8,128)} %cy_ref.1), custom_call_target="tpu_custom_call" | custom-call | tf_op jit(solution)/shard_map/pack/pallas_call | solution.py:327
  1.2 0.0 copy-start
  1.2 0.0 copy-start.1
  1.2 20.8 %all_to_all.10 = f32[16,40,128]{2,1,0:T(8,128)S(1)} all-to-all(f32[16,40,128]{2,1,0:T(8,128)S(1)} %pack.1), channel_id=1, replica_groups=mesh['tm'=16,'space'=32] {'tm'}, dimensions={0} | all-to-all | bytes 655360 | tf_op jit(solution)/shard_map/all_to_all | solution.py:378
  22.0 3.1 %collective-permute-start.1 = (f32[640,128]{1,0:T(8,128)S(1)}, f32[640,128]{1,0:T(8,128)S(1)}, u32[]{:S(2)}, u32[]{:S(2)}) collective-permute-start(f32[640,128]{1,0:T(8,128)S(1)} %bitcast.10), channel_id=1, source_target_pairs={{1,0},{2,1},{3,2},{4,3},{5,4},{6,5},{7,6},{8,7},{9,8},{10,9},{11,1... | collective-permute-start | bytes 983048 | tf_op jit(solution)/shard_map/ppermute | solution.py:387
  25.1 5.5 %collective-permute-start = (f32[640,128]{1,0:T(8,128)S(1)}, f32[640,128]{1,0:T(8,128)S(1)}, u32[]{:S(2)}, u32[]{:S(2)}) collective-permute-start(f32[640,128]{1,0:T(8,128)S(1)} %bitcast.11), channel_id=1, source_target_pairs={{0,1},{1,2},{2,3},{3,4},{4,5},{5,6},{6,7},{7,8},{8,9},{9,10},{10,1... | collective-permute-start | bytes 983048 | tf_op jit(solution)/shard_map/ppermute | solution.py:387
  30.6 0.0 copy-done
  30.6 0.0 copy-done.1
  30.6 0.9 %own.1 = (f32[8,64,128]{2,1,0:T(8,128)S(1)}, f32[8,80,256]{2,1,0:T(8,128)S(1)}, f32[5,8,256]{2,1,0:T(8,128)S(1)}, f32[8,32,256]{2,1,0:T(8,128)S(1)}, f32[8,8,256...) custom-call(bf16[64,384]{1,0:T(8,128)(2,1)S(1)} %copy-done.1, ...), custom_call_target="tpu_custom_call" | custom-call | flops 10000000 | bytes 1048576 | tf_op jit(solution)/shard_map/own/pallas_call | solution.py:349
  31.5 1.6 %collective-permute-done.1.dn_ref = f32[640,128]{1,0:T(8,128)S(1)} collective-permute-done((f32[640,128]{1,0:T(8,128)S(1)}, f32[640,128]{1,0:T(8,128)S(1)}, u32[]{:S(2)}, u32[]{:S(2)}) %collective-permute-start.1) | collective-permute-done | bytes 327712 | tf_op jit(solution)/shard_map/ppermute | solution.py:387
  33.1 0.0 copy-start.2
  33.1 2.0 %below.1 = (f32[64,256]{1,0:T(8,128)S(1)}, f32[4,2,64,256]{3,2,1,0:T(8,128)S(1)}) custom-call(bf16[64,384]{1,0:T(8,128)(2,1)S(1)} %copy-done.1, f32[32,384]{1,0:T(8,128)S(1)} %copy-done, f32[640,128]{1,0:T(8,128)S(1)} %collective-permute-done.1.dn_ref, f32[8,80,256]{2,1,0:T(8,128)S(1)} %get-tuple-element.16.x1, f32[5,8,256]{2,1,0:T(8,128)S(1)} %get-tuple-element.17.wt1, ...), custom_call_target="tpu_custom_call" | custom-call | flops 20000000 | bytes 1048576 | tf_op jit(solution)/shard_map/below/pallas_call | solution.py:349
  35.2 0.0 collective-permute-done.up_ref
  35.2 0.0 copy-done.2
  35.2 3.1 %last.1 = f32[512,128]{1,0:T(8,128)S(1)} custom-call(s32[1]{0:T(128)} %bitcast.t_ref, bf16[64,384]{1,0:T(8,128)(2,1)S(1)} %copy-done.1, bf16[64,384]{1,0:T(8,128)(2,1)S(1)} %copy-done.2, f32[32,384]{1,0:T(8,128)S(1)} %copy-done, f32[640,128]{1,0:T(8,128)S(1)} %collective-permute-done.up_ref, f32[8,64,128]{2,1,0:T(8,128)S(1)} %get-tuple-element.15.main_ref, ...), custom_call_target="tpu_custom_call" | custom-call | flops 30000000 | bytes 1048576 | tf_op jit(solution)/shard_map/last/pallas_call | solution.py:349
  38.3 17.3 %all_to_all.11 = f32[16,32,128]{2,1,0:T(8,128)S(1)} all-to-all(f32[16,32,128]{2,1,0:T(8,128)S(1)} %bitcast.13), channel_id=1, replica_groups=mesh['tm'=16,'space'=32] {'tm'}, dimensions={0} | all-to-all | bytes 524288 | tf_op jit(solution)/shard_map/all_to_all | solution.py:390
  55.6 0.7 %copy_bitcast_fusion = f32[4,8,2048]{2,1,0:T(8,128)} fusion(f32[16,32,128]{2,1,0:T(8,128)S(1)} %all_to_all.11), kind=kLoop, calls=%fused_computation | loop fusion | bytes 524288 | tf_op jit(solution)/shard_map/reshape | solution.py:372
Async XLA Ops:
  1.2 29.4 %copy-start = (f32[32,384]{1,0:T(8,128)S(1)}, f32[32,384]{1,0:T(8,128)}, u32[]{:S(2)}) copy-start(f32[32,384]{1,0:T(8,128)} %constant.14.clone.shift_ref) | copy-start | bytes 147460
  1.2 29.4 %copy-start.1 = (bf16[64,384]{1,0:T(8,128)(2,1)S(1)}, bf16[64,384]{1,0:T(8,128)(2,1)}, u32[]{:S(2)}) copy-start(bf16[64,384]{1,0:T(8,128)(2,1)} %constant.12.clone.fwd_ref) | copy-start | bytes 147460
  22.0 11.1 %collective-permute-start.1 = (f32[640,128]{1,0:T(8,128)S(1)}, f32[640,128]{1,0:T(8,128)S(1)}, u32[]{:S(2)}, u32[]{:S(2)}) collective-permute-start(f32[640,128]{1,0:T(8,128)S(1)} %bitcast.10), channel_id=1, source_target_pairs={{1,0},{2,1},{3,2},{4,3},{5,4},{6,5},{7,6},{8,7},{9,8},{10,9},{11,1... | collective-permute-start | bytes 983048 | tf_op jit(solution)/shard_map/ppermute | solution.py:387
  25.1 10.1 %collective-permute-start = (f32[640,128]{1,0:T(8,128)S(1)}, f32[640,128]{1,0:T(8,128)S(1)}, u32[]{:S(2)}, u32[]{:S(2)}) collective-permute-start(f32[640,128]{1,0:T(8,128)S(1)} %bitcast.11), channel_id=1, source_target_pairs={{0,1},{1,2},{2,3},{3,4},{4,5},{5,6},{6,7},{7,8},{8,9},{9,10},{10,1... | collective-permute-start | bytes 983048 | tf_op jit(solution)/shard_map/ppermute | solution.py:387
  33.1 2.1 %copy-start.2 = (bf16[64,384]{1,0:T(8,128)(2,1)S(1)}, bf16[64,384]{1,0:T(8,128)(2,1)}, u32[]{:S(2)}) copy-start(bf16[64,384]{1,0:T(8,128)(2,1)} %constant.13.clone.inv_ref) | copy-start | bytes 147460

commit v9 on v8

--- a/solution.py
+++ b/solution.py
@@ -79,8 +79,11 @@
     plain.append([coef[:, e * LANES : (e + 1) * LANES] for e in range(DEVS)])
     turned = [[flip(tile) for tile in tiles] for tiles in plain]
     turned[LOCAL] = [sign * tile for tile in turned[LOCAL]]
+    odd = t_ref[1] % 2 == 1
+    pick = lambda one, two: [[jnp.where(odd, b, a) for a, b in zip(*rows)] for rows in zip(one, two)]
+    sets = pick(plain, turned), pick(turned, plain)
     for d in range(DEVS):
-        tiles = turned if d % 2 else plain
+        tiles = sets[d % 2]
         for n in range(LOCAL):
             send_ref[d, n * ROWS : (n + 1) * ROWS, :] = tiles[n][d]
         tail = [sides(tiles[n], d) for n in range(LOCAL)]
@@ -111,7 +114,7 @@
     return refs[j // ROWS].at[j % ROWS]
 
 
-def build(ref, x_ref, wt_ref, coef_ref, main_ref=None):
+def build(ref, x_ref, wt_ref, coef_ref, main_ref=None, mirrored=False):
     def tiles(main, turned):
         lane = lane_ids(main.shape[0])
         return jnp.where(lane >= LANES - 8, turned, main), jnp.where(lane < 8, turned, main)
@@ -124,11 +127,15 @@
         base, share = d * BLOCK + (ROWS + 1) * LOCAL, 2 * (d // 4)
         coef_ref[d % 4, share : share + 2, :LANES] = ref[base : base + 2, :]
     rims = jnp.concatenate([steps(ROWS * LOCAL, 1), ref[pl.ds((ROWS + 1) * LOCAL + 2, 4, stride=BLOCK), :]], 0)
+    if mirrored:
+        for a in range(4):
+            coef_ref[a, :, :LANES] = flip(coef_ref[a, :, :LANES])
     for r in range(ROWS):
-        main = steps(r, ROWS)
+        source = ROWS - 1 - r if mirrored else r
+        main = steps(source, ROWS)
         if main_ref is not None:
             main_ref[r] = main
-        turned = pltpu.roll(rims, (2 * LANES - 16 * r - 8) % LANES, 1)
+        turned = pltpu.roll(rims, (2 * LANES - 16 * source - 8) % LANES, 1)
         x_ref[r, DEVS:, :LANES], x_ref[r, DEVS:, LANES:] = tiles(main, turned[:STEPS])
         for a in range(4):
             one = slice(r, r + 1)
@@ -136,6 +143,7 @@
         x_ref[r, :1, :] = coef_ref[0, r : r + 1, :]
         x_ref[r, 1:DEVS, :] = x_ref[r, STEPS : STEPS + DEVS - 1, :]
     dif, cx, cy = coef_ref[1], coef_ref[2], coef_ref[3]
+    cy = -cy if mirrored else cy
     west = dif + jnp.maximum(cx, 0.0)
     east = dif + jnp.maximum(-cx, 0.0)
     north = dif + jnp.maximum(cy, 0.0)
@@ -238,7 +246,7 @@
     fwd_ref, shift_ref, dn_ref, x1, wt1, a1, alt1, b1, f1, early_ref,
     f15_ref, edge_ref, x_ref, wt_ref, a_ref, alt_ref, b_ref, f_ref, w_ref, coef_ref,
 ):
-    build(dn_ref, x_ref, wt_ref, coef_ref)
+    build(dn_ref, x_ref, wt_ref, coef_ref, mirrored=True)
     grid = Grid((None, x1, x_ref), (None, wt1, wt_ref), (None, a1, a_ref), (None, alt1, alt_ref), (None, b1, b_ref))
     for r in range(ROWS - 1):
         diagonal(shift_ref, wt_ref, a_ref, alt_ref, b_ref, r)
@@ -263,7 +271,7 @@
     t_ref, fwd_ref, inv_ref, shift_ref, up_ref, main_ref, x1, wt1, a1, alt1, b1, f1, early_ref, f15_ref, edge_ref,
     out_ref, x_ref, wt_ref, a_ref, alt_ref, b_ref, f_ref, w_ref, coef_ref,
 ):
-    build(up_ref, x_ref, wt_ref, coef_ref)
+    build(up_ref, x_ref, wt_ref, coef_ref, mirrored=True)
     grid = Grid((x_ref, x1), (wt_ref, wt1), (a_ref, a1), (alt_ref, alt1), (b_ref, b1))
     for r in range(1, ROWS):
         diagonal(shift_ref, wt_ref, a_ref, alt_ref, b_ref, r)
@@ -283,6 +291,7 @@
                 grid.store(j, level, m, cols)
     lane, picked = lane_ids(8), {}
     left = lane < LANES // 2
+    odd = t_ref[2]
 
     def pick(ref, mask=left):
         return jnp.where(mask, ref[:, TILES[0]], ref[:, TILES[1]])
@@ -314,7 +323,7 @@
         corr = mul(inv_ref[...], jnp.concatenate([final(ROWS + r), final(ROWS + r + 1)], 1))
         for i in range(2):
             new = main_ref[r + i] + corr[:, i * LANES : (i + 1) * LANES]
-            place = jnp.where(t_ref[0] % 2 == 0, r + i, ROWS - 1 - r - i)
+            place = r + i + odd * (ROWS - 1 - 2 * (r + i))
             for n in range(LOCAL):
                 out_ref[pl.ds(n * ROWS + place, DEVS, stride=ROWS * LOCAL), :] = new[n * DEVS : (n + 1) * DEVS]
 
@@ -373,17 +382,19 @@
 
 
 def local(iterate, initial, diffusion, courant_x, courant_y):
-    t = lax.axis_index("tm").astype(jnp.int32).reshape(1)
+    t, s = lax.axis_index("tm"), lax.axis_index("space")
+    t = jnp.stack([t, s, (t + s) % 2]).astype(jnp.int32)
     send = pack(t, iterate, initial, diffusion, courant_x, courant_y)
     own = lax.all_to_all(send, "tm", split_axis=0, concat_axis=0, tiled=True)
     own = own.reshape(DEVS * BLOCK, LANES)
     count, halo = lax.axis_size("space"), []
-    for way in (1, 0):
+    for way in (0, 1):
         pairs = []
         for d in range(DEVS):
             for i in range(count - 1):
-                lower, upper = d * count + i + 1, d * count + i
-                pairs.append((upper, lower) if d % 2 == way else (lower, upper))
+                if (i + d) % 2 == way:
+                    one, two = d * count + i, d * count + i + 1
+                    pairs += [(one, two), (two, one)]
         halo.append(lax.ppermute(own, ("tm", "space"), pairs))
     below, above = halo
     new = solve(t, above, own, below)

time: 56.6 us -> 58.4 us (1.032)
  the two profiles are of different devices: /device:TPU:257 before, /device:TPU:1 now
where the time goes in v9:
time: 58.4 us; the launch traced here: 58.2 us
  blocking collectives  40 us (68%)
  Pallas kernels  7.81 us (13%)
  starting transfers between devices  5.37 us (9%)
  waiting for transfers between devices  2.86 us (5%)
  local copies, waits for them, and re-layouts  1.39 us (2%)
  other arithmetic  0.64 us (1%)
    all_to_all x1, blocking collectives, local(): own = lax.all_to_all(send, 'tm', split_axis=0, concat_axis=0, tiled=True)  22.5 us
    all_to_all x1, blocking collectives, local(): lax.all_to_all(new.reshape(DEVS, LOCAL * ROWS, LANES), 'tm', split_axis=0...  17.5 us
    pallas_call x3, Pallas kernels, call(): pl.pallas_call(kernel, name=name, out_shape=tuple((jax.ShapeDtypeStruct(s...  6.61 us
    ppermute x2, starting transfers between devices, local(): halo.append(lax.ppermute(own, ('tm', 'space'), pairs))  5.37 us
    ppermute x2, waiting for transfers between devices, local(): halo.append(lax.ppermute(own, ('tm', 'space'), pairs))  2.86 us
    pallas_call x1, Pallas kernels, pack(): pl.pallas_call(pack_kernel, name='pack', out_shape=pltpu.VMEM((DEVS, BLOC...  1.21 us
  transfers between devices with their start and end apart: 2, of which 1 were waited for; matrix products, arithmetic and copies ran while one was open for 0% of the time, Pallas kernels for 5%

profile of v9, /device:TPU:1, one launch (start us, length us, event | category | flops | bytes accessed | tf_op | source)
XLA Modules:
  0.0 58.2 jit_solution(1821446428035057172)
XLA Ops:
  0.0 0.6 %pad_add_fusion.t_ref = s32[3]{0:T(128)} fusion(s32[1]{0:T(128)} %bitcast.2, s32[1]{0:T(128)} %bitcast.1, s32[1]{0:T(128)} %bitcast), kind=kLoop, calls=%fused_computation.1 | loop fusion | flops 6 | bytes 24 | tf_op jit(solution)/shard_map/stack | solution.py:386
  0.6 1.2 %pack.1 = f32[16,40,128]{2,1,0:T(8,128)S(1)} custom-call(s32[3]{0:T(128)} %pad_add_fusion.t_ref, f32[4,8,2048]{2,1,0:T(8,128)} %it_ref.1, f32[8,2048]{1,0:T(8,128)} %ini_ref.1, f32[8,2048]{1,0:T(8,128)} %dif_ref.1, f32[8,2048]{1,0:T(8,128)} %cx_ref.1, f32[8,2048]{1,0:T(8,128)} %cy_ref.1), custom_call_target="tpu_custom_call" | custom-call | tf_op jit(solution)/shard_map/pack/pallas_call | solution.py:336
  1.9 0.0 copy-start
  1.9 0.0 copy-start.1
  1.9 22.5 %all_to_all.10 = f32[16,40,128]{2,1,0:T(8,128)S(1)} all-to-all(f32[16,40,128]{2,1,0:T(8,128)S(1)} %pack.1), channel_id=1, replica_groups=mesh['tm'=16,'space'=32] {'tm'}, dimensions={0} | all-to-all | bytes 655360 | tf_op jit(solution)/shard_map/all_to_all | solution.py:388
  24.3 0.7 %collective-permute-start.1 = (f32[640,128]{1,0:T(8,128)S(1)}, f32[640,128]{1,0:T(8,128)S(1)}, u32[]{:S(2)}, u32[]{:S(2)}) collective-permute-start(f32[640,128]{1,0:T(8,128)S(1)} %bitcast.12), channel_id=1, source_target_pairs={{0,1},{1,0},{2,3},{3,2},{4,5},{5,4},{6,7},{7,6},{8,9},{9,8},{10,11... | collective-permute-start | bytes 983048 | tf_op jit(solution)/shard_map/ppermute | solution.py:398
  25.0 4.7 %collective-permute-start = (f32[640,128]{1,0:T(8,128)S(1)}, f32[640,128]{1,0:T(8,128)S(1)}, u32[]{:S(2)}, u32[]{:S(2)}) collective-permute-start(f32[640,128]{1,0:T(8,128)S(1)} %bitcast.13), channel_id=1, source_target_pairs={{1,2},{2,1},{3,4},{4,3},{5,6},{6,5},{7,8},{8,7},{9,10},{10,9},{11,... | collective-permute-start | bytes 983048 | tf_op jit(solution)/shard_map/ppermute | solution.py:398
  29.7 0.0 copy-done
  29.7 0.0 copy-done.1
  29.8 0.9 %own.1 = (f32[8,64,128]{2,1,0:T(8,128)S(1)}, f32[8,80,256]{2,1,0:T(8,128)S(1)}, f32[5,8,256]{2,1,0:T(8,128)S(1)}, f32[8,32,256]{2,1,0:T(8,128)S(1)}, f32[8,8,256...) custom-call(bf16[64,384]{1,0:T(8,128)(2,1)S(1)} %copy-done.1, ...), custom_call_target="tpu_custom_call" | custom-call | flops 10000000 | bytes 1048576 | tf_op jit(solution)/shard_map/own/pallas_call | solution.py:358
  30.6 0.0 collective-permute-done.1.dn_ref
  30.6 0.0 copy-start.2
  30.6 2.1 %below.1 = (f32[64,256]{1,0:T(8,128)S(1)}, f32[4,2,64,256]{3,2,1,0:T(8,128)S(1)}) custom-call(bf16[64,384]{1,0:T(8,128)(2,1)S(1)} %copy-done.1, f32[32,384]{1,0:T(8,128)S(1)} %copy-done, f32[640,128]{1,0:T(8,128)S(1)} %collective-permute-done.1.dn_ref, f32[8,80,256]{2,1,0:T(8,128)S(1)} %get-tuple-element.16.x1, f32[5,8,256]{2,1,0:T(8,128)S(1)} %get-tuple-element.17.wt1, ...), custom_call_target="tpu_custom_call" | custom-call | flops 20000000 | bytes 1048576 | tf_op jit(solution)/shard_map/below/pallas_call | solution.py:358
  32.7 2.9 %collective-permute-done.up_ref = f32[640,128]{1,0:T(8,128)S(1)} collective-permute-done((f32[640,128]{1,0:T(8,128)S(1)}, f32[640,128]{1,0:T(8,128)S(1)}, u32[]{:S(2)}, u32[]{:S(2)}) %collective-permute-start) | collective-permute-done | bytes 327712 | tf_op jit(solution)/shard_map/ppermute | solution.py:398
  35.6 0.0 copy-start.3
  35.6 0.0 copy-done.2
  35.6 0.6 %copy-done.3 = s32[3]{0:T(128)S(1)} copy-done((s32[3]{0:T(128)S(1)}, s32[3]{0:T(128)}, u32[]{:S(2)}) %copy-start.3) | copy-done | bytes 36
  36.2 3.7 %last.1 = f32[512,128]{1,0:T(8,128)S(1)} custom-call(s32[3]{0:T(128)S(1)} %copy-done.3, bf16[64,384]{1,0:T(8,128)(2,1)S(1)} %copy-done.1, bf16[64,384]{1,0:T(8,128)(2,1)S(1)} %copy-done.2, f32[32,384]{1,0:T(8,128)S(1)} %copy-done, f32[640,128]{1,0:T(8,128)S(1)} %collective-permute-done.up_ref, f32[8,64,128]{2,1,0:T(8,128)S(1)} %get-tuple-element.15.main_ref, ...), custom_call_target="tpu_custom_call" | custom-call | flops 30000000 | bytes 1048576 | tf_op jit(solution)/shard_map/last/pallas_call | solution.py:358
  39.9 17.5 %all_to_all.11 = f32[16,32,128]{2,1,0:T(8,128)S(1)} all-to-all(f32[16,32,128]{2,1,0:T(8,128)S(1)} %bitcast.15), channel_id=1, replica_groups=mesh['tm'=16,'space'=32] {'tm'}, dimensions={0} | all-to-all | bytes 524288 | tf_op jit(solution)/shard_map/all_to_all | solution.py:401
  57.4 0.7 %copy_bitcast_fusion = f32[4,8,2048]{2,1,0:T(8,128)} fusion(f32[16,32,128]{2,1,0:T(8,128)S(1)} %all_to_all.11), kind=kLoop, calls=%fused_computation | loop fusion | bytes 524288 | tf_op jit(solution)/shard_map/reshape | solution.py:381
Async XLA Ops:
  1.9 27.9 %copy-start = (f32[32,384]{1,0:T(8,128)S(1)}, f32[32,384]{1,0:T(8,128)}, u32[]{:S(2)}) copy-start(f32[32,384]{1,0:T(8,128)} %constant.30.clone.shift_ref) | copy-start | bytes 147460
  1.9 27.9 %copy-start.1 = (bf16[64,384]{1,0:T(8,128)(2,1)S(1)}, bf16[64,384]{1,0:T(8,128)(2,1)}, u32[]{:S(2)}) copy-start(bf16[64,384]{1,0:T(8,128)(2,1)} %constant.28.clone.fwd_ref) | copy-start | bytes 147460
  24.3 6.3 %collective-permute-start.1 = (f32[640,128]{1,0:T(8,128)S(1)}, f32[640,128]{1,0:T(8,128)S(1)}, u32[]{:S(2)}, u32[]{:S(2)}) collective-permute-start(f32[640,128]{1,0:T(8,128)S(1)} %bitcast.12), channel_id=1, source_target_pairs={{0,1},{1,0},{2,3},{3,2},{4,5},{5,4},{6,7},{7,6},{8,9},{9,8},{10,11... | collective-permute-start | bytes 983048 | tf_op jit(solution)/shard_map/ppermute | solution.py:398
  25.0 10.5 %collective-permute-start = (f32[640,128]{1,0:T(8,128)S(1)}, f32[640,128]{1,0:T(8,128)S(1)}, u32[]{:S(2)}, u32[]{:S(2)}) collective-permute-start(f32[640,128]{1,0:T(8,128)S(1)} %bitcast.13), channel_id=1, source_target_pairs={{1,2},{2,1},{3,4},{4,3},{5,6},{6,5},{7,8},{8,7},{9,10},{10,9},{11,... | collective-permute-start | bytes 983048 | tf_op jit(solution)/shard_map/ppermute | solution.py:398
  30.6 5.0 %copy-start.2 = (bf16[64,384]{1,0:T(8,128)(2,1)S(1)}, bf16[64,384]{1,0:T(8,128)(2,1)}, u32[]{:S(2)}) copy-start(bf16[64,384]{1,0:T(8,128)(2,1)} %constant.29.clone.inv_ref) | copy-start | bytes 147460
  35.6 0.7 %copy-start.3 = (s32[3]{0:T(128)S(1)}, s32[3]{0:T(128)}, u32[]{:S(2)}) copy-start(s32[3]{0:T(128)} %pad_add_fusion.t_ref) | copy-start | bytes 40
